TPU v7x, 32 devices: a whole 2x2x4 slice. The times are simulated.
32 devices in a mesh: dp: 8 (over y, x, core), expert: 4 (over z).
Axes of the slice: x: 2, y: 2, z: 4, core: 2. Of those that a mesh axis runs over, the one named last changes fastest.
Arguments:
- hidden_in: bfloat16 [8192, 1536], P(('dp', 'expert')), may hold values from -6 to 6
- cotangent: bfloat16 [8192, 1536], P(('dp', 'expert')), may hold values from -6 to 6
- routes: int32 [8192, 6], P(('dp', 'expert')), may hold values from 0 to 23, all different within a row; in each aligned block of 256 rows (0 to 255, 256 to 511, ...) at most 80 rows name the same one
- route_weights: float32 [8192, 6], P(('dp', 'expert')), may hold values from 0.15 to 0.5
- dense_weights: float32 [1536, 7168], P(('dp', 'expert')), may hold values from -4 to 4
- dense_momentum: float32 [1536, 7168], P(('dp', 'expert')), may hold values from -160 to 160
- expert_weights: float32 [24, 3, 1536, 512], P('expert', None, 'dp'), may hold values from -0.25 to 0.25
- expert_momentum: float32 [24, 3, 1536, 512], P('expert', None, 'dp'), may hold values from -80 to 80
- norm_gains: float32 [2, 1536], P(None, ('dp', 'expert')), may hold values from 0.5 to 1.5
- gain_first: float32 [2, 1536], P(None, ('dp', 'expert')), may hold values from -448 to 448
- gain_second: float32 [2, 1536], P(None, ('dp', 'expert')), may hold values from 24576 to 98304
Outputs:
- block_out: bfloat16 [8192, 1536], P(('dp', 'expert'))
- input_grad: float32 [8192, 1536], P(('dp', 'expert'))
- dense_grad: float32 [1536, 7168], P(('dp', 'expert'))
- dense_moment: float32 [1536, 7168], P(('dp', 'expert'))
- dense_new: float32 [1536, 7168], P(('dp', 'expert'))
- expert_grad: float32 [24, 3, 1536, 512], P('expert', None, 'dp')
- expert_moment: float32 [24, 3, 1536, 512], P('expert', None, 'dp')
- expert_new: float32 [24, 3, 1536, 512], P('expert', None, 'dp')
- gain_grad: float32 [2, 1536], P(None, ('dp', 'expert'))
- gain_first_new: float32 [2, 1536], P(None, ('dp', 'expert'))
- gain_second_new: float32 [2, 1536], P(None, ('dp', 'expert'))
- gain_new: float32 [2, 1536], P(None, ('dp', 'expert'))
Inputs may be any that keep to these rules, and one draw needn't show every extreme that they name: `routes`: each row names 6 different experts; in each aligned block of 256 rows, the rows of one device, no expert is named by more than 80 rows, and that bound is reached.
All inputs are finite; a program needn't handle non-finite values.
Results may differ from a plain program's by a relative error of at most 0.025.
Values may be sent and summed in bfloat16 or wider, within the bound.
A program may use at most 384 MiB of HBM per device.

v0:
```python
import jax
import jax.numpy as jnp
from jax import lax
from jax.sharding import PartitionSpec as P

HEADS = 12
HD = 128
KVH = 4
FFE = 512
FFS = 1024
NS_STEPS = 5
STEP = 10


POLY_FIRST = 3.4445
POLY_SECOND = -4.775
POLY_THIRD = 2.0315
MOMENTUM_DECAY = 0.95
LEARN_RATE = 0.6
WEIGHT_DECAY = 0.1
GAIN_RATE = 0.8
FIRST_DECAY = 0.9
SECOND_DECAY = 0.95


def partner(value, axis, bit):
    mask = 2**bit
    pairs = [(source, source ^ mask) for source in range(lax.axis_size(axis))]
    return lax.ppermute(value, axis, pairs)


def shortened(value):

    def short(part):
        return part.astype(jnp.bfloat16) if part.dtype == jnp.float32 else part

    return jax.tree.map(short, value)


def norm_scale(values):
    return lax.rsqrt(jnp.mean(values * values, axis=-1, keepdims=True) + 1e-06)


def slot_table(route_rows, expert_count, capacity):
    flat_routes = route_rows.reshape(-1)
    choices_hot = (
        flat_routes[:, None] == jnp.arange(expert_count, dtype=jnp.int32)[None, :]
    ).astype(jnp.int32)
    earlier = jnp.cumsum(choices_hot, axis=0) - choices_hot
    return flat_routes * capacity + jnp.sum(earlier * choices_hot, axis=1)


def block_scores(query_block, key_block, first_row, block_rows, last_row):
    score_scale = HD ** (-0.5)
    scores = (
        jnp.einsum("qgrd,kgd->grqk", query_block, key_block, preferred_element_type=jnp.float32)
        * score_scale
    )
    allowed = jnp.arange(last_row)[None, :] <= (first_row + jnp.arange(block_rows))[:, None]
    return jnp.where(allowed, scores, -1e30)


def attend_forward(query, key_rows, value_rows, block_rows):
    length = query.shape[0]
    query_heads = query.reshape(length, KVH, HEADS // KVH, HD)
    key_heads = key_rows.reshape(length, KVH, HD)
    value_heads = value_rows.reshape(length, KVH, HD)
    scores = block_scores(query_heads, key_heads, 0, block_rows, block_rows)
    highest = jnp.max(scores, axis=-1, keepdims=True)
    raised = jnp.exp(scores - highest)
    totals = jnp.sum(raised, axis=-1, keepdims=True)
    weights = (raised / totals).astype(jnp.bfloat16)
    outputs = jnp.einsum("grqk,kgd->qgrd", weights, value_heads, preferred_element_type=jnp.float32)
    saved_stats = [(highest, totals)]
    attended = outputs.reshape(length, HEADS * HD)
    return (attended.astype(jnp.bfloat16), saved_stats)


def attend_backward(query, key_rows, value_rows, grad_attended, saved_stats, block_rows):
    length = query.shape[0]
    score_scale = HD ** (-0.5)
    query_heads = query.reshape(length, KVH, HEADS // KVH, HD)
    grad_heads = grad_attended.reshape(length, KVH, HEADS // KVH, HD)
    key_heads = key_rows.reshape(length, KVH, HD)
    value_heads = value_rows.reshape(length, KVH, HD)
    grad_key = jnp.zeros((length, KVH, HD), jnp.float32)
    grad_value = jnp.zeros((length, KVH, HD), jnp.float32)
    query_parts = []
    for block_index, first_row in enumerate(range(0, length, block_rows)):
        last_row = first_row + block_rows
        scores = block_scores(query_heads, key_heads, first_row, block_rows, last_row)
        highest, totals = saved_stats[block_index]
        weights = jnp.exp(scores - highest) / totals
        grad_weights = jnp.einsum(
            "qgrd,kgd->grqk", grad_heads, value_heads, preferred_element_type=jnp.float32
        )
        inner_sum = jnp.sum(weights * grad_weights, axis=-1, keepdims=True)
        grad_scores = (weights * (grad_weights - inner_sum)).astype(jnp.bfloat16)
        query_parts.append(
            jnp.einsum("grqk,kgd->qgrd", grad_scores, key_heads, preferred_element_type=jnp.float32)
            * score_scale
        )
        grad_key = grad_key.at[:last_row].add(
            jnp.einsum(
                "grqk,qgrd->kgd", grad_scores, query_heads, preferred_element_type=jnp.float32
            )
            * score_scale
        )
        grad_value = grad_value.at[:last_row].add(
            jnp.einsum(
                "grqk,qgrd->kgd",
                weights.astype(jnp.bfloat16),
                grad_heads,
                preferred_element_type=jnp.float32,
            )
        )
    grad_query = query_parts[0].reshape(length, HEADS * HD)
    return (
        grad_query.astype(jnp.bfloat16),
        grad_key.reshape(length, KVH * HD).astype(jnp.bfloat16),
        grad_value.reshape(length, KVH * HD).astype(jnp.bfloat16),
    )


def pair_total(values):
    return values + partner(values.astype(jnp.bfloat16), "dp", 0).astype(values.dtype)


def rows_over_expert(values):
    return lax.all_gather(shortened(values), "expert", axis=0, tiled=True).astype(values.dtype)


def newton_schulz(owned):
    squares = pair_total(jnp.sum(owned * owned, axis=(1, 2)))
    current = owned / (jnp.sqrt(squares)[:, None, None] + 1e-07)
    for iteration in range(NS_STEPS):
        rounded = current.astype(jnp.bfloat16)
        gram_matrix = pair_total(
            jnp.einsum("urf,urg->ufg", rounded, rounded, preferred_element_type=jnp.float32)
        )
        gram_low = gram_matrix.astype(jnp.bfloat16)
        polynomial = POLY_SECOND * gram_matrix + POLY_THIRD * jnp.einsum(
            "ufg,ugh->ufh", gram_low, gram_low, preferred_element_type=jnp.float32
        )
        current = POLY_FIRST * current + jnp.einsum(
            "urf,ufg->urg",
            rounded,
            polynomial.astype(jnp.bfloat16),
            preferred_element_type=jnp.float32,
        )
    return current


def on_device(
    hidden_in,
    cotangent,
    routes,
    route_weights,
    dense_weights,
    dense_momentum,
    expert_weights,
    expert_momentum,
    norm_gains,
    gain_first,
    gain_second,
):
    length, width = hidden_in.shape
    topk_count = routes.shape[1]
    local_experts = expert_weights.shape[0]
    expert_count = local_experts * lax.axis_size("expert")
    capacity = 5 * length * topk_count // (4 * expert_count)
    block_rows = min(512, length)
    query_width = HEADS * HD
    kv_width = KVH * HD
    qkv_end = query_width + 2 * kv_width
    shared_base = 2 * query_width + 2 * kv_width
    dense_all, gains_all = (
        lax.all_gather(dense_weights.astype(jnp.bfloat16), ("dp", "expert"), axis=0, tiled=True),
        lax.all_gather(norm_gains.astype(jnp.bfloat16), ("dp", "expert"), axis=1, tiled=True),
    )
    expert_all = lax.all_gather(expert_weights.astype(jnp.bfloat16), "dp", axis=2, tiled=True)
    inputs = hidden_in.astype(jnp.float32)
    gain_attend = gains_all[0].astype(jnp.float32)
    gain_mixer = gains_all[1].astype(jnp.float32)
    scale_attend = norm_scale(inputs)
    normed_attend = (inputs * scale_attend * gain_attend).astype(jnp.bfloat16)
    projected = jnp.dot(
        normed_attend, dense_all[:, :qkv_end], preferred_element_type=jnp.float32
    ).astype(jnp.bfloat16)
    query = projected[:, :query_width]
    key_rows = projected[:, query_width : query_width + kv_width]
    value_rows = projected[:, query_width + kv_width :]
    attended, saved_stats = attend_forward(query, key_rows, value_rows, block_rows)
    residual = inputs + jnp.einsum(
        "sq,dq->sd", attended, dense_all[:, qkv_end:shared_base], preferred_element_type=jnp.float32
    )
    scale_mixer = norm_scale(residual)
    normed_mixer = (residual * scale_mixer * gain_mixer).astype(jnp.bfloat16)
    shared_pre = jnp.dot(
        normed_mixer,
        dense_all[:, shared_base : shared_base + 2 * FFS],
        preferred_element_type=jnp.float32,
    )
    shared_gate = shared_pre[:, :FFS]
    shared_up = shared_pre[:, FFS:]
    shared_act = (jax.nn.silu(shared_gate) * shared_up).astype(jnp.bfloat16)
    shared_out = jnp.einsum(
        "sf,df->sd",
        shared_act,
        dense_all[:, shared_base + 2 * FFS :],
        preferred_element_type=jnp.float32,
    )
    slots = slot_table(routes, expert_count, capacity)
    slot_total = expert_count * capacity
    pair_rows = length * topk_count
    owner = (
        jnp.zeros((slot_total,), jnp.int32)
        .at[slots]
        .set(jnp.arange(pair_rows, dtype=jnp.int32) // topk_count)
    )
    filled = (
        jnp.zeros((slot_total,), jnp.bfloat16).at[slots].set(jnp.ones((pair_rows,), jnp.bfloat16))
    )
    outgoing = (normed_mixer[owner] * filled[:, None]).reshape(expert_count, capacity, width)
    received = lax.all_to_all(outgoing, "expert", split_axis=0, concat_axis=1, tiled=True)
    gate_pre = jnp.einsum(
        "jrd,jdf->jrf", received, expert_all[:, 0], preferred_element_type=jnp.float32
    )
    up_pre = jnp.einsum(
        "jrd,jdf->jrf", received, expert_all[:, 1], preferred_element_type=jnp.float32
    )
    expert_act = (jax.nn.silu(gate_pre) * up_pre).astype(jnp.bfloat16)
    expert_out = jnp.einsum(
        "jrf,jdf->jrd", expert_act, expert_all[:, 2], preferred_element_type=jnp.float32
    ).astype(jnp.bfloat16)
    returned = lax.all_to_all(expert_out, "expert", split_axis=1, concat_axis=0, tiled=True)
    picked = (
        returned.reshape(slot_total, width)[slots]
        .reshape(length, topk_count, width)
        .astype(jnp.float32)
    )
    routed = jnp.sum(picked * route_weights[:, :, None], axis=1)
    block_out = (residual + shared_out + routed).astype(jnp.bfloat16)
    grad_out = cotangent.astype(jnp.float32)
    dense_back = lax.all_gather(
        dense_weights.astype(jnp.bfloat16), ("dp", "expert"), axis=0, tiled=True
    )
    expert_back = lax.all_gather(expert_weights.astype(jnp.bfloat16), "dp", axis=2, tiled=True)
    grad_picked = (route_weights[:, :, None] * grad_out[:, None, :]).reshape(pair_rows, width)
    grad_returned = (
        jnp.zeros((slot_total, width), jnp.float32)
        .at[slots]
        .set(grad_picked)
        .astype(jnp.bfloat16)
        .reshape(expert_count, capacity, width)
    )
    grad_expert_out = lax.all_to_all(
        grad_returned, "expert", split_axis=0, concat_axis=1, tiled=True
    )
    grad_act = jnp.einsum(
        "jrd,jdf->jrf", grad_expert_out, expert_back[:, 2], preferred_element_type=jnp.float32
    )
    gate_sig = jax.nn.sigmoid(gate_pre)
    grad_gate = (grad_act * up_pre * gate_sig * (1.0 + gate_pre * (1.0 - gate_sig))).astype(
        jnp.bfloat16
    )
    grad_up = (grad_act * jax.nn.silu(gate_pre)).astype(jnp.bfloat16)
    grad_weight_down = jnp.einsum(
        "jrd,jrf->jdf", grad_expert_out, expert_act, preferred_element_type=jnp.float32
    )
    grad_weight_gate = jnp.einsum(
        "jrd,jrf->jdf", received, grad_gate, preferred_element_type=jnp.float32
    )
    grad_weight_up = jnp.einsum(
        "jrd,jrf->jdf", received, grad_up, preferred_element_type=jnp.float32
    )
    grad_received = (
        jnp.einsum("jrf,jdf->jrd", grad_gate, expert_back[:, 0], preferred_element_type=jnp.float32)
        + jnp.einsum("jrf,jdf->jrd", grad_up, expert_back[:, 1], preferred_element_type=jnp.float32)
    ).astype(jnp.bfloat16)
    grad_sent = lax.all_to_all(grad_received, "expert", split_axis=1, concat_axis=0, tiled=True)
    grad_normed = jnp.sum(
        grad_sent.reshape(slot_total, width)[slots]
        .reshape(length, topk_count, width)
        .astype(jnp.float32),
        axis=1,
    )
    grad_weight_sdown = jnp.einsum(
        "sd,sf->df", cotangent, shared_act, preferred_element_type=jnp.float32
    )
    grad_shared_act = jnp.dot(
        cotangent, dense_back[:, shared_base + 2 * FFS :], preferred_element_type=jnp.float32
    )
    shared_sig = jax.nn.sigmoid(shared_gate)
    grad_shared_pre = jnp.concatenate(
        [
            grad_shared_act * shared_up * shared_sig * (1.0 + shared_gate * (1.0 - shared_sig)),
            grad_shared_act * jax.nn.silu(shared_gate),
        ],
        1,
    ).astype(jnp.bfloat16)
    grad_weight_sgu = jnp.einsum(
        "sd,sf->df", normed_mixer, grad_shared_pre, preferred_element_type=jnp.float32
    )
    grad_normed = grad_normed + jnp.einsum(
        "sf,df->sd",
        grad_shared_pre,
        dense_back[:, shared_base : shared_base + 2 * FFS],
        preferred_element_type=jnp.float32,
    )
    grad_scaled = grad_normed * gain_mixer
    grad_residual = (
        grad_out
        + scale_mixer * grad_scaled
        - residual * scale_mixer**3 * jnp.mean(grad_scaled * residual, axis=-1, keepdims=True)
    )
    grad_gain_mixer = jnp.sum(grad_normed * residual * scale_mixer, axis=0)
    grad_attn_low = grad_residual.astype(jnp.bfloat16)
    grad_weight_out = jnp.einsum(
        "sd,sq->dq", grad_attn_low, attended, preferred_element_type=jnp.float32
    )
    grad_attended = jnp.dot(
        grad_attn_low, dense_back[:, qkv_end:shared_base], preferred_element_type=jnp.float32
    ).astype(jnp.bfloat16)
    grad_query, grad_key, grad_value = attend_backward(
        query, key_rows, value_rows, grad_attended, saved_stats, block_rows
    )
    grad_projected = jnp.concatenate([grad_query, grad_key, grad_value], 1)
    grad_weight_qkv = jnp.einsum(
        "sd,sc->dc", normed_attend, grad_projected, preferred_element_type=jnp.float32
    )
    grad_normed_attend = jnp.einsum(
        "sc,dc->sd", grad_projected, dense_back[:, :qkv_end], preferred_element_type=jnp.float32
    )
    grad_scaled_attend = grad_normed_attend * gain_attend
    grad_inputs = (
        grad_residual
        + scale_attend * grad_scaled_attend
        - inputs * scale_attend**3 * jnp.mean(grad_scaled_attend * inputs, axis=-1, keepdims=True)
    )
    grad_gain_attend = jnp.sum(grad_normed_attend * inputs * scale_attend, axis=0)
    grad_dense_local = jnp.concatenate(
        [grad_weight_qkv, grad_weight_out, grad_weight_sgu, grad_weight_sdown], 1
    )
    grad_gain_local = jnp.stack([grad_gain_attend, grad_gain_mixer], 0)
    dense_grad, gain_grad = (
        lax.psum_scatter(grad_dense_local, ("dp", "expert"), scatter_dimension=0, tiled=True),
        lax.psum_scatter(grad_gain_local, ("dp", "expert"), scatter_dimension=1, tiled=True),
    )
    expert_grad = lax.psum_scatter(
        jnp.stack([grad_weight_gate, grad_weight_up, grad_weight_down], 1).astype(jnp.bfloat16),
        "dp",
        scatter_dimension=2,
        tiled=True,
    ).astype(jnp.float32)
    dense_moment = MOMENTUM_DECAY * dense_momentum + dense_grad
    expert_moment = MOMENTUM_DECAY * expert_momentum + expert_grad
    dense_rows = rows_over_expert(dense_moment)
    row_count = dense_rows.shape[0]
    half_rows = row_count // 2
    expert_size = lax.axis_size("expert")
    dense_columns = dense_rows.shape[1]
    dense_total = dense_columns // FFE
    dense_share = (dense_total + expert_size - 1) // expert_size
    padded_rows = jnp.pad(
        dense_rows, ((0, 0), (0, dense_share * expert_size * FFE - dense_columns))
    )
    my_columns = lax.dynamic_slice_in_dim(
        padded_rows, lax.axis_index("expert") * (dense_share * FFE), dense_share * FFE, 1
    )
    dense_units = my_columns.reshape(row_count, dense_share, FFE).transpose(1, 0, 2)
    expert_units = expert_moment.reshape(-1, row_count, FFE)
    expert_unit_count = expert_units.shape[0]
    pair_count = lax.axis_size("dp") // 2
    base_count = expert_unit_count + dense_share
    unit_count = (base_count + pair_count - 1) // pair_count * pair_count
    all_units = jnp.concatenate(
        [
            expert_units,
            dense_units,
            jnp.zeros((unit_count - base_count, row_count, FFE), jnp.float32),
        ],
        0,
    )
    per_pair = unit_count // pair_count
    outgoing_units = (
        all_units.reshape(pair_count, per_pair, 2, half_rows, FFE)
        .transpose(0, 2, 1, 3, 4)
        .reshape(2 * pair_count, per_pair, half_rows, FFE)
    )
    owned = lax.all_to_all(
        outgoing_units.astype(jnp.bfloat16), "dp", split_axis=0, concat_axis=2, tiled=True
    ).astype(outgoing_units.dtype)[0]
    orthogonal = newton_schulz(owned)
    returned_units = lax.all_to_all(
        orthogonal[None].astype(jnp.bfloat16), "dp", split_axis=2, concat_axis=0, tiled=True
    ).astype(jnp.float32)
    orth_units = (
        returned_units.reshape(pair_count, 2, per_pair, half_rows, FFE)
        .transpose(0, 2, 1, 3, 4)
        .reshape(unit_count, row_count, FFE)
    )
    orth_expert = orth_units[:expert_unit_count].reshape(expert_weights.shape)
    orth_mine = orth_units[expert_unit_count:base_count].reshape(dense_share * row_count, FFE)
    orth_gathered = rows_over_expert(orth_mine).reshape(expert_size * dense_share, row_count, FFE)[
        :dense_total
    ]
    stripe = dense_weights.shape[0]
    orth_rows = lax.dynamic_slice_in_dim(
        orth_gathered, lax.axis_index("expert") * stripe, stripe, 1
    )
    orth_stripe = orth_rows.transpose(1, 0, 2).reshape(stripe, dense_columns)
    keep_factor = 1.0 - LEARN_RATE * WEIGHT_DECAY
    dense_new = keep_factor * dense_weights - LEARN_RATE * orth_stripe
    expert_new = keep_factor * expert_weights - LEARN_RATE * orth_expert
    first_new = FIRST_DECAY * gain_first + (1.0 - FIRST_DECAY) * gain_grad
    second_new = SECOND_DECAY * gain_second + (1.0 - SECOND_DECAY) * gain_grad * gain_grad
    step_ratio = (
        first_new
        / (1.0 - FIRST_DECAY**STEP)
        / (jnp.sqrt(second_new / (1.0 - SECOND_DECAY**STEP)) + 1e-08)
    )
    gain_new = norm_gains - GAIN_RATE * step_ratio
    return (
        block_out,
        grad_inputs,
        dense_grad,
        dense_moment,
        dense_new,
        expert_grad,
        expert_moment,
        expert_new,
        gain_grad,
        first_new,
        second_new,
        gain_new,
    )


def solution(mesh):
    in_specs = (
        P(("dp", "expert"), None),
        P(("dp", "expert"), None),
        P(("dp", "expert"), None),
        P(("dp", "expert"), None),
        P(("dp", "expert"), None),
        P(("dp", "expert"), None),
        P("expert", None, "dp", None),
        P("expert", None, "dp", None),
        P(None, ("dp", "expert")),
        P(None, ("dp", "expert")),
        P(None, ("dp", "expert")),
    )
    out_specs = (
        P(("dp", "expert"), None),
        P(("dp", "expert"), None),
        P(("dp", "expert"), None),
        P(("dp", "expert"), None),
        P(("dp", "expert"), None),
        P("expert", None, "dp", None),
        P("expert", None, "dp", None),
        P("expert", None, "dp", None),
        P(None, ("dp", "expert")),
        P(None, ("dp", "expert")),
        P(None, ("dp", "expert")),
        P(None, ("dp", "expert")),
    )
    return jax.shard_map(
        on_device, mesh=mesh, in_specs=in_specs, out_specs=out_specs, check_vma=False
    )
```

profile of v0, /device:TPU:0, one launch (start us, length us, event | category | flops | bytes accessed | tf_op | source)
XLA Modules:
  0.0 2116.1 jit_solution(17494271405193459743)
XLA Ops:
  41.6 14.1 scatter_custom_fusion.2
  69.9 253.9 %all-gather = bf16[32,48,2]{1,2,0:T(2,128)(2,1)S(1)} all-gather(bf16[1,48,2]{1,2,0:T(2,128)(2,1)S(1)} %convert_bitcast_fusion.4), channel_id=1, replica_groups=mesh['dp'=8,'expert'=4] {'dp','expert'}, dimensions={0}, use_global_device_ids=true | all-gather | bytes 6336 | tf_op jit(solution)/shard_map/all_gather | solution.py:179
  384.5 119.6 %all-to-all-done = bf16[24,80,1536]{2,1,0:T(8,128)(2,1)} async-done(((bf16[24,80,1536]{2,1,0:T(8,128)(2,1)}), bf16[24,80,1536]{2,1,0:T(8,128)(2,1)}, u32[]{:S(2)}, u32[]{:S(2)}) %all-to-all-start) | async-done | bytes 5898272 | tf_op jit(solution)/shard_map/all_to_all | solution.py:225
  551.2 13.4 add_convert_fusion
  597.6 153.0 %all-to-all-done.3 = bf16[6,320,1536]{2,0,1:T(8,128)(2,1)} async-done(((bf16[6,320,1536]{2,0,1:T(8,128)(2,1)}), bf16[6,320,1536]{2,0,1:T(8,128)(2,1)}, u32[]{:S(2)}, u32[]{:S(2)}) %all-to-all-start.3) | async-done | bytes 5898272 | tf_op jit(solution)/shard_map/all_to_all | solution.py:281
  758.4 13.8 gather_fusion.2
  819.9 29.9 %pad_maximum_fusion = f32[1536,7168]{1,0:T(8,128)} fusion(f32[1536,1024]{1,0:T(8,128)} %convolution_bitcast_fusion, f32[1536,2048]{1,0:T(8,128)} %fusion.114, f32[1536,1536]{1,0:T(8,128)} %fusion.116, f32[1536,2560]{1,0:T(8,128)} %fusion.115), kind=kLoop, calls=%fused_computation.7 | loop fusion | flops 33030144 | bytes 88080384 | tf_op jit(solution)/shard_map/concatenate | solution.py:342
  861.6 12.4 convert_bitcast_fusion.3
  882.0 23.9 %pad_maximum_fusion.1 = bf16[6,3,1536,512]{3,2,0,1:T(8,128)(2,1)} fusion(bf16[6,1,1536,512]{3,2,0,1:T(8,128)(2,1)} %convert_bitcast_fusion.1, bf16[6,1,1536,512]{3,2,0,1:T(8,128)(2,1)} %convert_bitcast_fusion.2, bf16[6,1,1536,512]{3,2,0,1:T(8,128)(2,1)} %convert_bitcast_fusion.3), kind=kLoop, calls=%fused_computation.8 | loop fusion | flops 28311552 | bytes 56623104 | tf_op jit(solution)/shard_map/stack | solution.py:351
  906.2 332.1 %reduce-scatter.6.cloned.1.call-done = f32[48,7168]{1,0:T(8,128)} async-done(((f32[1536,7168]{1,0:T(8,128)}), f32[48,7168]{1,0:T(8,128)}) %reduce-scatter.6.cloned.1.call-update) | async-done | bytes 1376272 | tf_op jit(solution)/shard_map/reduce_scatter | solution.py:347
  1241.2 173.5 %reduce-scatter.8.cloned.1.call-done = bf16[6,3,192,512]{3,2,0,1:T(8,128)(2,1)} async-done(((bf16[6,3,1536,512]{3,2,0,1:T(8,128)(2,1)}), bf16[6,3,192,512]{3,2,0,1:T(8,128)(2,1)}) %reduce-scatter.8.cloned.1.call-update) | async-done | bytes 3538960 | tf_op jit(solution)/shard_map/reduce_scatter | solution.py:350
  1423.6 50.2 %all-gather.10.cloned.1.call-done = bf16[192,7168]{1,0:T(8,128)(2,1)} async-done(((bf16[48,7168]{1,0:T(8,128)(2,1)}), bf16[192,7168]{1,0:T(8,128)(2,1)}) %all-gather.10.cloned.1.call-update) | async-done | bytes 2752528 | tf_op jit(solution)/shard_map/all_gather | solution.py:130
  1476.2 58.1 %all_to_all.84 = bf16[8,6,96,512]{3,2,1,0:T(8,128)(2,1)S(1)} all-to-all(bf16[8,6,96,512]{3,2,1,0:T(8,128)(2,1)S(1)} %bitcast.199), channel_id=1, replica_groups=mesh['dp'=8,'expert'=4] {'dp'}, dimensions={0} | all-to-all | bytes 9437184 | tf_op jit(solution)/shard_map/all_to_all | solution.py:391
  1542.5 12.9 fusion.165
  1561.3 16.4 fusion.86
  1577.7 16.7 fusion.166
  1610.9 18.5 multiply_add_fusion.2
  1648.5 19.7 fusion.82
  1668.2 15.5 fusion.168
  1702.6 17.5 multiply_add_fusion
  1739.1 21.8 %fusion.21 = bf16[1,6,768,512]{3,2,1,0:T(8,128)(2,1)} fusion(f32[6,768,512]{2,1,0:T(8,128)} %multiply_add_fusion, f32[6,512,512]{2,1,0:T(8,128)} %get-tuple-element.142, bf16[6,512,512]{2,1,0:T(8,128)(2,1)} %copy-done.54), kind=kOutput, calls=%fused_computation.58 | convolution fusion | flops 4050124800 | bytes 23592960 | tf_op jit(solution)/shard_map/urf,ufg->urg/dot_general | solution.py:145
  1788.0 57.5 %all-to-all-done.5 = bf16[1,6,768,512]{3,1,0,2:T(8,128)(2,1)} async-done(((bf16[1,6,768,512]{3,1,0,2:T(8,128)(2,1)}), bf16[1,6,768,512]{3,1,0,2:T(8,128)(2,1)}, u32[]{:S(2)}, u32[]{:S(2)}) %all-to-all-start.5) | async-done | bytes 4718624 | tf_op jit(solution)/shard_map/all_to_all | solution.py:395
  1864.7 158.7 %all-to-all-done.1 = bf16[6,320,1536]{2,0,1:T(8,128)(2,1)} async-done(((bf16[6,320,1536]{2,0,1:T(8,128)(2,1)}), bf16[6,320,1536]{2,0,1:T(8,128)(2,1)}, u32[]{:S(2)}, u32[]{:S(2)}) %all-to-all-start.1) | async-done | bytes 5898272 | tf_op jit(solution)/shard_map/all_to_all | solution.py:236
  2031.2 13.8 gather_fusion.1
  (292 shorter events, 483.7 us)
Async XLA Ops:
  7.2 335.3 %all-gather.6.cloned.1.call-start = ((), (), s32[]{:S(2)}) async-start(), calls=%async_computation.9 | async-start | bytes 22708224 | tf_op jit(solution)/shard_map/all_gather | solution.py:178
  9.5 500.4 %all-gather.8.cloned.1.call-start = ((), (), s32[]{:S(2)}) async-start(), calls=%async_computation.10 | async-start | bytes 31850496 | tf_op jit(solution)/shard_map/all_gather | solution.py:181
  63.4 278.2 %copy-start.5 = (bf16[256,1536]{1,0:T(8,128)(2,1)S(1)}, bf16[256,1536]{1,0:T(8,128)(2,1)}, u32[]{:S(2)}) copy-start(bf16[256,1536]{1,0:T(8,128)(2,1)} %param.19) | copy-start | bytes 2359300
  63.4 309.6 %all-to-all-start.2 = ((bf16[24,80,1536]{2,1,0:T(8,128)(2,1)}), bf16[24,80,1536]{2,1,0:T(8,128)(2,1)}, u32[]{:S(2)}, u32[]{:S(2)}) async-start(bf16[24,80,1536]{2,1,0:T(8,128)(2,1)} %bitcast.196), calls=%async_computation.2 | async-start | bytes 11796480 | tf_op jit(solution)/shard_map/all_to_all | solution.py:257
  359.4 436.5 %copy-start.2 = (f32[256,1536]{1,0:T(8,128)}, f32[256,1536]{1,0:T(8,128)S(1)}, u32[]{:S(2)}) copy-start(f32[256,1536]{1,0:T(8,128)S(1)} %get-tuple-element.128) | copy-start | bytes 4718596
  373.0 131.1 %all-to-all-start = ((bf16[24,80,1536]{2,1,0:T(8,128)(2,1)}), bf16[24,80,1536]{2,1,0:T(8,128)(2,1)}, u32[]{:S(2)}, u32[]{:S(2)}) async-start(bf16[24,80,1536]{2,1,0:T(8,128)(2,1)} %broadcast_multiply_fusion), calls=%async_computation | async-start | bytes 11796480 | tf_op jit(solution)/shard_map/all_to_all | solution.py:225
  573.8 176.9 %all-to-all-start.3 = ((bf16[6,320,1536]{2,0,1:T(8,128)(2,1)}), bf16[6,320,1536]{2,0,1:T(8,128)(2,1)}, u32[]{:S(2)}, u32[]{:S(2)}) async-start(bf16[6,320,1536]{2,0,1:T(8,128)(2,1)} %copy.149), calls=%async_computation.3 | async-start | bytes 15728640 | tf_op jit(solution)/shard_map/all_to_all | solution.py:281
  579.3 659.0 %reduce-scatter.6.cloned.1.call-start = ((), (), s32[]{:S(2)}) async-start(), calls=%async_computation.11 | async-start | bytes 45416448 | tf_op jit(solution)/shard_map/reduce_scatter | solution.py:347
  579.6 178.8 %copy-start.40 = (s32[2048]{0:T(1024)}, s32[2048]{0:T(1024)S(1)}, u32[]{:S(2)}) copy-start(s32[2048]{0:T(1024)S(1)} %pad_clamp_fusion) | copy-start | bytes 24580
  849.8 564.9 %reduce-scatter.8.cloned.1.call-start = ((), (), s32[]{:S(2)}) async-start(), calls=%async_computation.12 | async-start | bytes 31850496 | tf_op jit(solution)/shard_map/reduce_scatter | solution.py:350
  905.9 332.4 %copy-start.22 = (f32[48,7168]{1,0:T(8,128)S(1)}, f32[48,7168]{1,0:T(8,128)}, u32[]{:S(2)}) copy-start(f32[48,7168]{1,0:T(8,128)} %param.24) | copy-start | bytes 4128772
  905.9 567.9 %all-gather.10.cloned.1.call-start = ((), (), s32[]{:S(2)}) async-start(), calls=%async_computation.13 | async-start | bytes 3440640 | tf_op jit(solution)/shard_map/all_gather | solution.py:130
  1541.4 1.1 collective-permute-start
  1555.4 5.9 collective-permute-start.1
  1594.5 5.9 collective-permute-start.2
  1641.1 5.7 collective-permute-start.3
  1683.6 5.7 collective-permute-start.4
  1731.8 5.7 collective-permute-start.5
  1768.8 76.8 %all-to-all-start.5 = ((bf16[1,6,768,512]{3,1,0,2:T(8,128)(2,1)}), bf16[1,6,768,512]{3,1,0,2:T(8,128)(2,1)}, u32[]{:S(2)}, u32[]{:S(2)}) async-start(bf16[1,6,768,512]{3,1,0,2:T(8,128)(2,1)} %copy.170), calls=%async_computation.7 | async-start | bytes 12582912 | tf_op jit(solution)/shard_map/all_to_all | solution.py:395
  1788.0 63.2 %copy-start.34 = (bf16[4,128,256]{2,1,0:T(8,128)(2,1)S(1)}, bf16[4,128,256]{2,1,0:T(8,128)(2,1)}, u32[]{:S(2)}) copy-start(bf16[4,128,256]{2,1,0:T(8,128)(2,1)} %copy-done.33) | copy-start | bytes 786436
  1788.0 63.2 %copy-start.39 = (f32[1536]{0:T(1024)S(1)}, f32[1536]{0:T(1024)}, u32[]{:S(2)}) copy-start(f32[1536]{0:T(1024)} %copy-done.37) | copy-start | bytes 18436
  1845.5 177.9 %all-to-all-start.1 = ((bf16[6,320,1536]{2,0,1:T(8,128)(2,1)}), bf16[6,320,1536]{2,0,1:T(8,128)(2,1)}, u32[]{:S(2)}, u32[]{:S(2)}) async-start(bf16[6,320,1536]{2,0,1:T(8,128)(2,1)} %copy.144), calls=%async_computation.1 | async-start | bytes 15728640 | tf_op jit(solution)/shard_map/all_to_all | solution.py:236
  1851.1 220.2 %reduce-scatter.10.cloned.1.call-start = ((), (), s32[]{:S(2)}) async-start(), calls=%async_computation.15 | async-start | bytes 811008
  1859.2 246.6 %all-gather.12.cloned.1.call-start = ((), (), s32[]{:S(2)}) async-start(), calls=%async_computation.14 | async-start | bytes 3932160 | tf_op jit(solution)/shard_map/all_gather | solution.py:130
  (59 other events, 689.3 us)
Sparse Core Ops, SparseCore 0:
  11.4 230.8 all-gather.5
  244.2 162.7 all-gather.7
  849.9 388.3 reduce-scatter.5
  1242.3 172.4 reduce-scatter.7
  1416.8 56.9 all-gather.9
  1859.3 181.5 reduce-scatter.9
  2043.1 62.5 all-gather.11
where the time goes:
time: 2130 us; the launch traced here: 2120 us
  waiting for transfers between devices  1080 us (51%)
  matrix products  351 us (16%)
  blocking collectives  312 us (15%)
  local copies, waits for them, and re-layouts  186 us (9%)
  other arithmetic  137 us (6%)
  starting transfers between devices  30.3 us (1%)
    reduce_scatter x1, waiting for transfers between devices, on_device(): lax.psum_scatter(grad_dense_local, ('dp', 'expert'), scatter_dimension=0,...  332 us
    all_gather x1, blocking collectives, on_device(): lax.all_gather(norm_gains.astype(jnp.bfloat16), ('dp', 'expert'), axis=1,...  254 us
    reduce_scatter x1, waiting for transfers between devices, on_device(): lax.psum_scatter(jnp.stack([grad_weight_gate, grad_weight_up, grad_weight...  174 us
    all_to_all x1, waiting for transfers between devices, on_device(): lax.all_to_all(expert_out, 'expert', split_axis=1, concat_axis=0, tiled=T...  159 us
    all_to_all x1, waiting for transfers between devices, on_device(): lax.all_to_all(grad_received, 'expert', split_axis=1, concat_axis=0, tile...  153 us
    all_to_all x1, waiting for transfers between devices, on_device(): lax.all_to_all(outgoing, 'expert', split_axis=0, concat_axis=1, tiled=True)  120 us
    dot_general x5, matrix products, newton_schulz(): jnp.einsum('urf,ufg->urg', rounded, polynomial.astype(jnp.bfloat16), pref...  93.9 us
    dot_general x5, matrix products, newton_schulz(): jnp.einsum('urf,urg->ufg', rounded, rounded, preferred_element_type=jnp.f...  68.6 us
  transfers between devices with their start and end apart: 18, of which 14 were waited for; matrix products, arithmetic and copies ran while one was open for 14% of the time, Pallas kernels for 0%

commit v1 on v0

v1 whole, which is shorter than its diff:
```python
import functools

import jax
import jax.numpy as jnp
from jax import lax
from jax.experimental import pallas as pl
from jax.experimental.pallas import tpu as pltpu
from jax.sharding import PartitionSpec as P

HEADS = 12
HD = 128
KVH = 4
FFE = 512
FFS = 1024
NS_STEPS = 5
STEP = 10


POLY_FIRST = 3.4445
POLY_SECOND = -4.775
POLY_THIRD = 2.0315
MOMENTUM_DECAY = 0.95
LEARN_RATE = 0.6
WEIGHT_DECAY = 0.1
GAIN_RATE = 0.8
FIRST_DECAY = 0.9
SECOND_DECAY = 0.95


def norm_scale(values):
    return lax.rsqrt(jnp.mean(values * values, axis=-1, keepdims=True) + 1e-06)


def block_scores(query_block, key_block, first_row, block_rows, last_row):
    score_scale = HD ** (-0.5)
    scores = (
        jnp.einsum("qgrd,kgd->grqk", query_block, key_block, preferred_element_type=jnp.float32)
        * score_scale
    )
    allowed = jnp.arange(last_row)[None, :] <= (first_row + jnp.arange(block_rows))[:, None]
    return jnp.where(allowed, scores, -1e30)


def attend_forward(query, key_rows, value_rows, block_rows):
    length = query.shape[0]
    query_heads = query.reshape(length, KVH, HEADS // KVH, HD)
    key_heads = key_rows.reshape(length, KVH, HD)
    value_heads = value_rows.reshape(length, KVH, HD)
    scores = block_scores(query_heads, key_heads, 0, block_rows, block_rows)
    highest = jnp.max(scores, axis=-1, keepdims=True)
    raised = jnp.exp(scores - highest)
    totals = jnp.sum(raised, axis=-1, keepdims=True)
    weights = (raised / totals).astype(jnp.bfloat16)
    outputs = jnp.einsum("grqk,kgd->qgrd", weights, value_heads, preferred_element_type=jnp.float32)
    saved_stats = [(highest, totals)]
    attended = outputs.reshape(length, HEADS * HD)
    return (attended.astype(jnp.bfloat16), saved_stats)


def attend_backward(query, key_rows, value_rows, grad_attended, saved_stats, block_rows):
    length = query.shape[0]
    score_scale = HD ** (-0.5)
    query_heads = query.reshape(length, KVH, HEADS // KVH, HD)
    grad_heads = grad_attended.reshape(length, KVH, HEADS // KVH, HD)
    key_heads = key_rows.reshape(length, KVH, HD)
    value_heads = value_rows.reshape(length, KVH, HD)
    grad_key = jnp.zeros((length, KVH, HD), jnp.float32)
    grad_value = jnp.zeros((length, KVH, HD), jnp.float32)
    query_parts = []
    for block_index, first_row in enumerate(range(0, length, block_rows)):
        last_row = first_row + block_rows
        scores = block_scores(query_heads, key_heads, first_row, block_rows, last_row)
        highest, totals = saved_stats[block_index]
        weights = jnp.exp(scores - highest) / totals
        grad_weights = jnp.einsum(
            "qgrd,kgd->grqk", grad_heads, value_heads, preferred_element_type=jnp.float32
        )
        inner_sum = jnp.sum(weights * grad_weights, axis=-1, keepdims=True)
        grad_scores = (weights * (grad_weights - inner_sum)).astype(jnp.bfloat16)
        query_parts.append(
            jnp.einsum("grqk,kgd->qgrd", grad_scores, key_heads, preferred_element_type=jnp.float32)
            * score_scale
        )
        grad_key = grad_key.at[:last_row].add(
            jnp.einsum(
                "grqk,qgrd->kgd", grad_scores, query_heads, preferred_element_type=jnp.float32
            )
            * score_scale
        )
        grad_value = grad_value.at[:last_row].add(
            jnp.einsum(
                "grqk,qgrd->kgd",
                weights.astype(jnp.bfloat16),
                grad_heads,
                preferred_element_type=jnp.float32,
            )
        )
    grad_query = query_parts[0].reshape(length, HEADS * HD)
    return (
        grad_query.astype(jnp.bfloat16),
        grad_key.reshape(length, KVH * HD).astype(jnp.bfloat16),
        grad_value.reshape(length, KVH * HD).astype(jnp.bfloat16),
    )


MIB = 2**20
GRAD_STEP = 11
SLOTS = 8
MESH = pl.DeviceIdType.MESH


def matmul(left, right):
    return jnp.dot(left, right, preferred_element_type=jnp.float32)


def matmul_nt(left, right):
    return lax.dot_general(left, right, (((1,), (1,)), ((), ())), preferred_element_type=jnp.float32)


def matmul_tn(left, right):
    return lax.dot_general(left, right, (((0,), (0,)), ((), ())), preferred_element_type=jnp.float32)


def newton_schulz_unit(moment_ref, orthogonal_ref, current, low, identity):
    columns, rows = current.shape
    step = 256
    parts = [pl.ds(index * step, step) for index in range(rows // step)]
    identity[...] = jnp.where(
        lax.broadcasted_iota(jnp.int32, identity.shape, 0)
        == lax.broadcasted_iota(jnp.int32, identity.shape, 1),
        1.0,
        0.0,
    ).astype(jnp.bfloat16)
    squares = jnp.zeros((1, columns), jnp.float32)
    for part in parts:
        values = moment_ref[part, :].astype(jnp.float32)
        squares = squares + jnp.sum(values * values, axis=0, keepdims=True)
    scale = 1.0 / (jnp.sqrt(jnp.sum(squares, axis=1, keepdims=True)) + 1e-07)
    for part in parts:
        scaled = matmul_nt(identity[...], moment_ref[part, :]) * scale
        current[:, part] = scaled
        low[:, part] = scaled.astype(jnp.bfloat16)

    def polynomial():
        gram = matmul_nt(low[...], low[...])
        gram_low = gram.astype(jnp.bfloat16)
        return (POLY_SECOND * gram + POLY_THIRD * matmul(gram_low, gram_low)).astype(jnp.bfloat16)

    @pl.loop(0, NS_STEPS - 1)
    def _(index):
        weights = polynomial()
        for part in parts:
            updated = POLY_FIRST * current[:, part] + matmul(weights, low[:, part])
            current[:, part] = updated
            low[:, part] = updated.astype(jnp.bfloat16)

    weights = polynomial()
    for part in parts:
        updated = POLY_FIRST * current[:, part] + matmul(weights, low[:, part])
        orthogonal_ref[part, :] = updated.T.astype(jnp.bfloat16)


def newton_schulz_kernel(moment_ref, orthogonal_ref, current, low, identity):
    newton_schulz_unit(moment_ref.at[0], orthogonal_ref.at[0], current, low, identity)


def newton_schulz(units):
    count, rows, columns = units.shape
    return pl.pallas_call(
        newton_schulz_kernel,
        grid=(count,),
        in_specs=[pl.BlockSpec((1, rows, columns), lambda unit: (unit, 0, 0))],
        out_specs=pl.BlockSpec((1, rows, columns), lambda unit: (unit, 0, 0)),
        out_shape=jax.ShapeDtypeStruct(units.shape, jnp.bfloat16),
        scratch_shapes=[
            pltpu.VMEM((columns, rows), jnp.float32),
            pltpu.VMEM((columns, rows), jnp.bfloat16),
            pltpu.VMEM((columns, columns), jnp.bfloat16),
        ],
        compiler_params=pltpu.CompilerParams(vmem_limit_bytes=48 * MIB),
        cost_estimate=pl.CostEstimate(
            flops=count * NS_STEPS * 2 * columns * columns * (2 * rows + columns),
            bytes_accessed=count * rows * columns * 4,
            transcendentals=0,
        ),
        name="newton_schulz",
    )(units)


def experts_kernel(
    tokens_ref,
    cotangent_ref,
    place_ref,
    gate_ref,
    weights_ref,
    routed_ref,
    grad_tokens_ref,
    received,
    grad_returned,
    act_ref,
    grad_gate_ref,
    grad_up_ref,
    routed_sum,
    grad_sum,
    chosen,
    weighted,
    grad_received,
):
    expert = pl.program_id(0)
    sequences, slots, length = chosen.shape

    @pl.when(expert == 0)
    def _():
        routed_sum[...] = jnp.zeros_like(routed_sum)
        grad_sum[...] = jnp.zeros_like(grad_sum)

    slot_weights = []
    for sequence in range(sequences):
        rows = pl.ds(sequence * length, length)
        spots = pl.ds(sequence * slots, slots)
        place = place_ref[0, sequence : sequence + 1, :]
        gate = gate_ref[0, sequence : sequence + 1, :]
        hot = lax.broadcasted_iota(jnp.int32, (slots, length), 0) == place
        slot_weight = jnp.sum(jnp.where(hot, gate, 0.0), axis=1, keepdims=True)
        slot_weights.append(slot_weight)
        hot_low = jnp.where(hot, 1.0, 0.0).astype(jnp.bfloat16)
        chosen[sequence] = hot_low
        received[0, spots, :] = matmul(hot_low, tokens_ref[rows, :]).astype(jnp.bfloat16)
        grad_returned[0, spots, :] = (
            matmul(hot_low, cotangent_ref[rows, :]) * slot_weight
        ).astype(jnp.bfloat16)
    tokens = received[0]
    grad_out = grad_returned[0]
    gate_pre = matmul(tokens, weights_ref[0, 0])
    up_pre = matmul(tokens, weights_ref[0, 1])
    gate_sig = jax.nn.sigmoid(gate_pre)
    gate_act = gate_pre * gate_sig
    act = (gate_act * up_pre).astype(jnp.bfloat16)
    act_ref[0] = act
    out = matmul_nt(act, weights_ref[0, 2]).astype(jnp.bfloat16).astype(jnp.float32)
    for sequence in range(sequences):
        spots = slice(sequence * slots, (sequence + 1) * slots)
        weighted[spots, :] = (out[spots] * slot_weights[sequence]).astype(jnp.bfloat16)
    grad_act = matmul(grad_out, weights_ref[0, 2])
    grad_gate = (grad_act * up_pre * gate_sig * (1.0 + gate_pre * (1.0 - gate_sig))).astype(
        jnp.bfloat16
    )
    grad_up = (grad_act * gate_act).astype(jnp.bfloat16)
    grad_gate_ref[0] = grad_gate
    grad_up_ref[0] = grad_up
    grad_received[...] = (
        matmul_nt(grad_gate, weights_ref[0, 0]) + matmul_nt(grad_up, weights_ref[0, 1])
    ).astype(jnp.bfloat16)
    for sequence in range(sequences):
        rows = pl.ds(sequence * length, length)
        spots = pl.ds(sequence * slots, slots)
        routed_sum[rows, :] += matmul_tn(chosen[sequence], weighted[spots, :])
        grad_sum[rows, :] += matmul_tn(chosen[sequence], grad_received[spots, :])

    @pl.when(expert == pl.num_programs(0) - 1)
    def _():
        routed_ref[...] = routed_sum[...].astype(jnp.bfloat16)
        grad_tokens_ref[...] = grad_sum[...].astype(jnp.bfloat16)


def run_experts(tokens, cotangents, place, gates, weights, capacity):
    experts, sequences, length = place.shape
    total, width = tokens.shape
    hidden = weights.shape[-1]
    slots = -(-capacity // 16) * 16
    spots = sequences * slots
    whole = pl.BlockSpec((total, width), lambda expert: (0, 0))
    table = pl.BlockSpec((1, sequences, length), lambda expert: (expert, 0, 0))
    matrices = pl.BlockSpec((1, 3, width, hidden), lambda expert: (expert, 0, 0, 0))
    wide = pl.BlockSpec((1, spots, width), lambda expert: (expert, 0, 0))
    narrow = pl.BlockSpec((1, spots, hidden), lambda expert: (expert, 0, 0))
    return pl.pallas_call(
        experts_kernel,
        grid=(experts,),
        in_specs=[whole, whole, table, table, matrices],
        out_specs=[whole, whole, wide, wide, narrow, narrow, narrow],
        out_shape=[
            *[jax.ShapeDtypeStruct((total, width), jnp.bfloat16)] * 2,
            *[jax.ShapeDtypeStruct((experts, spots, width), jnp.bfloat16)] * 2,
            *[jax.ShapeDtypeStruct((experts, spots, hidden), jnp.bfloat16)] * 3,
        ],
        scratch_shapes=[
            pltpu.VMEM((total, width), jnp.float32),
            pltpu.VMEM((total, width), jnp.float32),
            pltpu.VMEM((sequences, slots, length), jnp.bfloat16),
            pltpu.VMEM((spots, width), jnp.bfloat16),
            pltpu.VMEM((spots, width), jnp.bfloat16),
        ],
        compiler_params=pltpu.CompilerParams(vmem_limit_bytes=63 * MIB),
        cost_estimate=pl.CostEstimate(
            flops=experts * (12 * spots * width * hidden + 8 * spots * length * width),
            bytes_accessed=2 * weights.size + 16 * tokens.size,
            transcendentals=experts * spots * hidden,
        ),
        name="experts",
    )(tokens, cotangents, place, gates, weights)


def expert_grads_kernel(
    received_ref, grad_returned_ref, act_ref, grad_gate_ref, grad_up_ref, grad_weights_ref
):
    received, grad_returned = received_ref[0], grad_returned_ref[0]
    grad_weights_ref[0, 0] = matmul_tn(received, grad_gate_ref[0]).astype(jnp.bfloat16)
    grad_weights_ref[0, 1] = matmul_tn(received, grad_up_ref[0]).astype(jnp.bfloat16)
    grad_weights_ref[0, 2] = matmul_tn(grad_returned, act_ref[0]).astype(jnp.bfloat16)


def expert_grads(received, grad_returned, act, grad_gate, grad_up):
    experts, spots, width = received.shape
    hidden = act.shape[-1]
    wide = pl.BlockSpec((1, spots, width), lambda expert: (expert, 0, 0))
    narrow = pl.BlockSpec((1, spots, hidden), lambda expert: (expert, 0, 0))
    return pl.pallas_call(
        expert_grads_kernel,
        grid=(experts,),
        in_specs=[wide, wide, narrow, narrow, narrow],
        out_specs=pl.BlockSpec((1, 3, width, hidden), lambda expert: (expert, 0, 0, 0)),
        out_shape=jax.ShapeDtypeStruct((experts, 3, width, hidden), jnp.bfloat16),
        compiler_params=pltpu.CompilerParams(vmem_limit_bytes=48 * MIB),
        name="expert_grads",
    )(received, grad_returned, act, grad_gate, grad_up)


def grouped_experts(tokens, cotangents, place, gates, weights, capacity):
    experts, sequences, length = place.shape
    group = min(4, sequences)
    routed, grad_tokens, saved = [], [], []
    for first in range(0, sequences, group):
        rows = slice(first * length, (first + group) * length)
        part = slice(first, first + group)
        routed_part, grad_part, *kept = run_experts(
            tokens[rows], cotangents[rows], place[:, part], gates[:, part], weights, capacity
        )
        routed.append(routed_part)
        grad_tokens.append(grad_part)
        saved.append(kept)

    def joined(parts):
        return parts[0] if len(parts) == 1 else jnp.concatenate(parts, 0)

    return joined(routed), joined(grad_tokens), saved


def flipped(index, bit):
    unit = 2**bit
    return index + unit * (1 - 2 * ((index // unit) % 2))


class Links:
    def __init__(self, semaphores):
        self.semaphores = semaphores
        self.taken = 0
        self.dp = lax.axis_index("dp")
        self.z = lax.axis_index("expert")
        self.upper = self.z // 2
        self.position = self.z * (1 - 2 * self.upper) + 3 * self.upper
        self.step = 1 - 2 * self.upper
        self.core = (flipped(self.dp, 0), self.z)
        self.along_x = (flipped(self.dp, 1), self.z)
        self.along_y = (flipped(self.dp, 2), self.z)
        self.inward = (self.dp, self.z + self.step)
        self.outward = (self.dp, self.z - self.step)
        self.further = (self.dp, self.z + 2 * self.step)
        self.pending = []

    def order(self, index):
        near = (self.position + index) % 2 if index < 2 else index
        return near * self.step + 3 * self.upper

    def take(self, count=1):
        first = self.taken
        self.taken += count
        return first

    def barrier(self):
        barrier = pltpu.get_barrier_semaphore()
        for device in (self.core, self.along_x, self.along_y, self.inward, self.further):
            pl.semaphore_signal(barrier, inc=1, device_id=device, device_id_type=MESH)

        @pl.when(self.position == 1)
        def _():
            pl.semaphore_signal(barrier, inc=1, device_id=self.outward, device_id_type=MESH)

        pl.semaphore_wait(barrier, 5 + self.position)

    def copy_with(self, source, target, send, receive, device):
        return pltpu.make_async_remote_copy(
            src_ref=source,
            dst_ref=target,
            send_sem=send,
            recv_sem=receive,
            device_id=device,
            device_id_type=MESH,
        )

    def copy(self, source, target, send, receive, device):
        return self.copy_with(
            source, target, self.semaphores.at[send], self.semaphores.at[receive], device
        )

    def send(self, source, target, receive, device, position=None):
        copy = self.copy(source, target, self.take(), receive, device)
        if position is None:
            copy.start()
        else:
            pl.when(self.position == position)(copy.start)
        self.pending.append((copy, position))

    def arrived(self, region, receive):
        self.copy(region, region, receive, receive, self.core).wait_recv()

    def finish(self):
        for copy, position in self.pending:
            if position is None:
                copy.wait_send()
            else:
                pl.when(self.position == position)(copy.wait_send)


class LineGather:
    def __init__(self, links, region, own=None):
        self.links, self.region = links, region
        self.receives = links.take(4)
        self.own = region(links.z) if own is None else own

    def start(self):
        links = self.links
        target, receive = self.region(links.z), self.receives + links.z
        links.send(self.own, target, receive, links.further)
        links.send(self.own, target, receive, links.inward)
        links.send(self.own, target, receive, links.outward, 1)

    def relay(self):
        links = self.links
        source = links.order(3)
        block = self.region(source)

        @pl.when(links.position == 1)
        def _():
            links.arrived(block, self.receives + source)

        links.send(block, block, self.receives + source, links.outward, 1)

    def arrive(self, index):
        links = self.links
        source = links.order(index)

        def wait():
            links.arrived(self.region(source), self.receives + source)

        if index < 3:
            wait()
        else:
            pl.when(links.position == 0)(wait)


class PlaneGather:
    def __init__(self, links, region, parity, own=None):
        self.links, self.region, self.parity = links, region, parity
        self.receives = links.take(7)
        self.own = region(links.dp) if own is None else own

    def start(self):
        links, first = self.links, self.receives
        target = self.region(links.dp)
        links.send(self.own, target, first, links.along_x)
        links.send(self.own, target, first + 1, links.along_y)
        links.send(self.own, target, first + 2, links.core)

    def forward(self):
        links, first = self.links, self.receives
        across = self.region(flipped(links.dp, 1))
        links.arrived(across, first)
        if self.parity == 0:
            links.send(across, across, first + 3, links.along_y)
        links.send(across, across, first + 4, links.core)
        along = self.region(flipped(links.dp, 2))
        links.arrived(along, first + 1)
        if self.parity == 1:
            links.send(along, along, first + 3, links.along_x)
        links.send(along, along, first + 5, links.core)

    def last(self):
        links, first = self.links, self.receives
        corner = self.region(flipped(flipped(links.dp, 1), 2))
        links.arrived(corner, first + 3)
        links.send(corner, corner, first + 6, links.core)

    def complete(self):
        links, first = self.links, self.receives
        other = flipped(links.dp, 0)
        links.arrived(self.region(other), first + 2)
        links.arrived(self.region(flipped(other, 1)), first + 4)
        links.arrived(self.region(flipped(other, 2)), first + 5)
        links.arrived(self.region(flipped(flipped(other, 1), 2)), first + 6)


ANY = pl.BlockSpec(memory_space=pl.ANY)


def front_kernel(
    stripe_ref,
    gates_ref,
    masters_ref,
    hidden_ref,
    cotangent_ref,
    dense_ref,
    weights_ref,
    cotangents_ref,
    tokens_ref,
    routed_parts_ref,
    grad_parts_ref,
    received_ref,
    grad_returned_ref,
    act_ref,
    grad_gate_ref,
    grad_up_ref,
    normed_attend_ref,
    projected_ref,
    attended_ref,
    residual_ref,
    scale_ref,
    normed_mixer_ref,
    shared_act_ref,
    grad_shared_pre_ref,
    grad_shared_ref,
    base_ref,
    gains_ref,
    matrices,
    extra,
    all_gates,
    places,
    my_gates,
    chosen,
    slot_gates,
    forward_slots,
    backward_slots,
    narrow,
    masters,
    rounded,
    semaphores,
    shard_out,
    shard_in,
    local,
    load_sems,
    expert_sems,
):
    links = Links(semaphores)
    stripe, columns = stripe_ref.shape
    length, width = hidden_ref.shape
    panels, rows, hidden = masters_ref.shape
    experts = panels // 3
    slots = chosen.shape[1] // experts
    first_panels = 8
    middle = first_panels * hidden + extra.shape[1]
    halves = ((0, middle), (middle, columns - middle))
    query_width = HEADS * HD
    kv_width = KVH * HD
    ahead = 4

    def dense_region(dp, z, half):
        first, count = halves[half]
        row = pl.multiple_of((dp * 4 + z) * stripe, stripe)
        return dense_ref.at[pl.ds(row, stripe), pl.ds(first, count)]

    def own(half):
        first, count = halves[half]
        return stripe_ref.at[:, pl.ds(first, count)]

    def sequence(ref, z):
        return ref.at[pl.ds(pl.multiple_of(z * length, length), length), :]

    def shard_region(dp, panel):
        return weights_ref.at[panel, pl.ds(pl.multiple_of(dp * rows, rows), rows), :]

    lines = [
        LineGather(links, functools.partial(dense_region, links.dp, half=half), own(half))
        for half in range(2)
    ]
    cotangents = LineGather(links, functools.partial(sequence, cotangents_ref), cotangent_ref)
    tokens = LineGather(links, functools.partial(sequence, tokens_ref), normed_mixer_ref)
    gates = LineGather(links, lambda z: all_gates.at[z], gates_ref)
    planes = [
        [
            PlaneGather(
                links,
                functools.partial(dense_region, z=links.order(index), half=half),
                index % 2,
                own(half) if index == 0 else None,
            )
            for index in range(4)
        ]
        for half in range(2)
    ]

    def shard_copy(kind, panel, source_dp, device):
        block = shard_region(source_dp, panel)
        return links.copy_with(
            block, block, shard_out.at[kind, panel], shard_in.at[kind, panel], device
        )

    dp = links.dp
    dp_core, dp_x, dp_y = flipped(dp, 0), flipped(dp, 1), flipped(dp, 2)
    dp_corner = flipped(dp_x, 2)

    def hop(kind, panel):
        source, device = (
            (dp, links.along_x),
            (dp, links.along_y),
            (dp, links.core),
            None,
            (dp_x, links.core),
            (dp_y, links.core),
            (dp_corner, links.core),
        )[kind]
        return shard_copy(kind, panel, source, device)

    def corner_copy(panel, parity):
        if parity == 0:
            return shard_copy(3, panel, dp_x, links.along_y)
        return shard_copy(3, panel, dp_y, links.along_x)

    def shard_arrived(kind, panel, source_dp):
        shard_copy(kind, panel, source_dp, links.core).wait_recv()

    def shard_start(panel):
        for kind in range(3):
            hop(kind, panel).start()

    def shard_forward(panel):
        shard_arrived(0, panel, dp_x)
        pl.when(panel % 2 == 0)(corner_copy(panel, 0).start)
        hop(4, panel).start()
        shard_arrived(1, panel, dp_y)
        pl.when(panel % 2 == 1)(corner_copy(panel, 1).start)
        hop(5, panel).start()

    def shard_last(panel):
        shard_arrived(3, panel, dp_corner)
        hop(6, panel).start()

    def shard_complete(panel):
        shard_arrived(2, panel, dp_core)
        shard_arrived(4, panel, flipped(dp_core, 1))
        shard_arrived(5, panel, flipped(dp_core, 2))
        shard_arrived(6, panel, flipped(flipped(dp_core, 1), 2))

    def shard_finish(panel):
        for kind in (0, 1, 2, 4, 5, 6):
            hop(kind, panel).wait_send()
        corner_copy(panel, 0).wait_send()

    def exchange(panel):
        shard_forward(panel)
        if panel + ahead < panels:
            shard_start(panel + ahead)
        if panel >= 2:
            shard_last(panel - 2)

    local_copies = [
        pltpu.make_async_copy(source, target, local.at[index])
        for index, (source, target) in enumerate(
            (
                (
                    stripe_ref,
                    dense_ref.at[
                        pl.ds(pl.multiple_of((links.dp * 4 + links.z) * stripe, stripe), stripe), :
                    ],
                ),
                (gates_ref, all_gates.at[links.z]),
                (cotangent_ref, sequence(cotangents_ref, links.z)),
            )
        )
    ]
    token_copy = pltpu.make_async_copy(
        normed_mixer_ref, sequence(tokens_ref, links.z), local.at[3]
    )

    def dense_column(panel):
        return panel * hidden + (0 if panel < first_panels else extra.shape[1])

    loads = [
        pltpu.make_async_copy(
            dense_ref.at[:, pl.ds(dense_column(panel), hidden)],
            matrices.at[panel],
            load_sems.at[panel],
        )
        for panel in range(14)
    ]
    extra_load = pltpu.make_async_copy(
        dense_ref.at[:, pl.ds(first_panels * hidden, extra.shape[1])], extra, load_sems.at[14]
    )

    def master_load(panel):
        return pltpu.make_async_copy(
            masters_ref.at[panel], masters.at[panel % 2], expert_sems.at[0, panel % 2]
        )

    def master_store(panel):
        return pltpu.make_async_copy(
            rounded.at[panel % 2], shard_region(dp, panel), expert_sems.at[1, panel % 2]
        )

    master_load(0).start()
    links.barrier()
    lines[0].start()
    planes[0][0].start()
    lines[1].start()
    gates.start()
    for copy in local_copies:
        copy.start()

    def round_masters(first, last):
        @pl.loop(first, last)
        def _(panel):
            master_load(panel).wait()

            @pl.when(panel + 1 < panels)
            def _():
                master_load(panel + 1).start()

            @pl.when(panel >= 2)
            def _():
                master_store(panel - 2).wait()

            rounded[panel % 2] = masters[panel % 2].astype(jnp.bfloat16)
            master_store(panel).start()

    lines[0].arrive(1)
    planes[0][1].start()
    lines[0].arrive(2)
    planes[0][2].start()
    round_masters(0, panels // 2)
    planes[0][0].forward()
    lines[0].relay()
    lines[0].arrive(3)
    planes[0][3].start()
    planes[0][1].forward()
    lines[1].relay()
    round_masters(panels // 2, panels)
    for panel in (panels - 2, panels - 1):
        master_store(panel).wait()
    planes[1][0].start()
    planes[0][2].forward()
    lines[1].arrive(1)
    planes[1][1].start()
    planes[0][3].forward()
    cotangents.start()
    gates.relay()
    lines[1].arrive(2)
    planes[1][2].start()
    for plane in planes[0]:
        plane.last()
    planes[1][0].forward()
    for plane in planes[0]:
        plane.complete()
    local_copies[0].wait()
    extra_load.start()
    for copy in loads[:first_panels]:
        copy.start()

    rows_step = 32

    def norm_rows(source, gain, scale_out, target):
        @pl.loop(0, length // rows_step)
        def _(index):
            part = pl.ds(index * rows_step, rows_step)
            values = source[part, :].astype(jnp.float32)
            scale = lax.rsqrt(jnp.mean(values * values, axis=-1, keepdims=True) + 1e-06)
            if scale_out is not None:
                scale_out[part, :] = scale
            target[part, :] = (values * scale * gains_ref[gain : gain + 1, :]).astype(jnp.bfloat16)

    def project():
        extra_load.wait()
        gains_ref[...] = extra[...].astype(jnp.float32).T[:8, :]
        norm_rows(hidden_ref, 0, None, normed_attend_ref)
        for panel in range(5):
            loads[panel].wait()
            projected_ref[:, panel * hidden : (panel + 1) * hidden] = matmul(
                normed_attend_ref[...], matrices[panel]
            ).astype(jnp.bfloat16)

    def attend(group):
        key_rows = projected_ref[:, query_width + group * HD : query_width + (group + 1) * HD]
        value_first = query_width + kv_width + group * HD
        value_rows = projected_ref[:, value_first : value_first + HD]
        row = lax.broadcasted_iota(jnp.int32, (length, length), 0)
        column = lax.broadcasted_iota(jnp.int32, (length, length), 1)
        per_group = HEADS // KVH
        for head in range(group * per_group, (group + 1) * per_group):
            spot = slice(head * HD, (head + 1) * HD)
            scores = matmul_nt(projected_ref[:, spot], key_rows) * HD ** (-0.5)
            scores = jnp.where(column <= row, scores, -1e30)
            raised = jnp.exp(scores - jnp.max(scores, axis=-1, keepdims=True))
            shares = (raised / jnp.sum(raised, axis=-1, keepdims=True)).astype(jnp.bfloat16)
            attended_ref[:, spot] = matmul(shares, value_rows).astype(jnp.bfloat16)

    def join():
        for part in range(3):
            loads[5 + part].wait()
            update = matmul_nt(
                attended_ref[:, part * hidden : (part + 1) * hidden], matrices[5 + part]
            )
            if part == 0:
                residual_ref[...] = hidden_ref[...].astype(jnp.float32) + update
            else:
                residual_ref[...] += update
        norm_rows(residual_ref, 1, scale_ref, normed_mixer_ref)
        tokens.start()
        token_copy.start()

    def shared(part):
        spot = slice(part * hidden, (part + 1) * hidden)
        for panel in (8, 10, 12):
            loads[panel + part].wait()
        gate = matmul(normed_mixer_ref[...], matrices[8 + part])
        up = matmul(normed_mixer_ref[...], matrices[10 + part])
        sig = jax.nn.sigmoid(gate)
        gate_act = gate * sig
        shared_act_ref[:, spot] = (gate_act * up).astype(jnp.bfloat16)
        grad_act = matmul(cotangent_ref[...], matrices[12 + part])
        grad_shared_pre_ref[:, spot] = (
            grad_act * up * sig * (1.0 + gate * (1.0 - sig))
        ).astype(jnp.bfloat16)
        up_spot = slice((2 + part) * hidden, (3 + part) * hidden)
        grad_shared_pre_ref[:, up_spot] = (grad_act * gate_act).astype(jnp.bfloat16)

    def shared_back(part):
        spot = slice(part * hidden, (part + 1) * hidden)
        up_spot = slice((2 + part) * hidden, (3 + part) * hidden)
        grad = matmul_nt(grad_shared_pre_ref[:, spot], matrices[8 + part]) + matmul_nt(
            grad_shared_pre_ref[:, up_spot], matrices[10 + part]
        )
        out = matmul_nt(shared_act_ref[:, spot], matrices[12 + part])
        if part == 0:
            grad_shared_ref[...] = grad
            base_ref[...] = residual_ref[...] + out
        else:
            grad_shared_ref[...] += grad
            base_ref[...] += out

    def place_slots():
        local_copies[1].wait()
        before = (
            lax.broadcasted_iota(jnp.int32, (length, length), 0)
            < lax.broadcasted_iota(jnp.int32, (length, length), 1)
        )
        earlier_mask = jnp.where(before, 1.0, 0.0).astype(jnp.bfloat16)
        for source in range(4):
            gate = all_gates[source, links.z]
            hot = gate > 0.0
            earlier = matmul(jnp.where(hot, 1.0, 0.0).astype(jnp.bfloat16), earlier_mask)
            place = jnp.where(hot, earlier, -1.0).astype(jnp.int32)
            for expert in range(experts):
                places[expert, source : source + 1, :] = place[expert : expert + 1, :]
                my_gates[expert, source : source + 1, :] = gate[expert : expert + 1, :]

    project()
    lines[1].arrive(3)
    planes[1][3].start()
    planes[1][1].forward()
    attend(0)
    attend(1)
    planes[1][2].forward()
    for panel in range(2):
        shard_start(panel)
    attend(2)
    attend(3)
    planes[1][3].forward()
    cotangents.relay()
    join()
    for panel in range(2, ahead):
        shard_start(panel)
    for plane in planes[1]:
        plane.last()
    for index in range(1, 4):
        gates.arrive(index)
    place_slots()
    for plane in planes[1]:
        plane.complete()
    for copy in loads[first_panels:]:
        copy.start()
    exchange(0)
    shared(0)
    exchange(1)
    shared(1)
    exchange(2)
    shared_back(0)
    exchange(3)
    shared_back(1)
    exchange(4)
    tokens.relay()
    for panel in range(5, 11):
        exchange(panel)
    for index in range(1, 4):
        cotangents.arrive(index)
        tokens.arrive(index)
    local_copies[2].wait()
    token_copy.wait()
    token_loads = [
        pltpu.make_async_copy(
            source.at[:, pl.ds(part * hidden, hidden)],
            matrices.at[first + part, pl.ds(0, 4 * length)],
            load_sems.at[first + part],
        )
        for first, source in ((6, tokens_ref), (9, cotangents_ref))
        for part in range(3)
    ]
    for copy in token_loads:
        copy.start()
    slot_iota = lax.broadcasted_iota(jnp.int32, (slots, length), 0)
    for source in range(4):
        for expert in range(experts):
            hot = slot_iota == places[expert, source : source + 1, :]
            chosen[source, expert * slots : (expert + 1) * slots, :] = jnp.where(
                hot, 1.0, 0.0
            ).astype(jnp.bfloat16)
            slot_gates[expert, source * slots : (source + 1) * slots, :] = jnp.sum(
                jnp.where(hot, my_gates[expert, source : source + 1, :], 0.0),
                axis=1,
                keepdims=True,
            )
    exchange(11)
    for copy in token_loads:
        copy.wait()

    @pl.loop(0, 4)
    def _(source):
        part = pl.ds(source * length, length)
        spots = pl.ds(pl.multiple_of(source * slots, slots), slots)
        for block in range(3):
            spot = pl.ds(block * hidden, hidden)
            token_slots = matmul(chosen[source], matrices[6 + block, part, :])
            grad_slots = matmul(chosen[source], matrices[9 + block, part, :])
            for expert in range(experts):
                rows_of = slice(expert * slots, (expert + 1) * slots)
                forward_slots[expert, spots, spot] = token_slots[rows_of].astype(jnp.bfloat16)
                backward_slots[expert, spots, spot] = (
                    grad_slots[rows_of] * slot_gates[expert, spots, :]
                ).astype(jnp.bfloat16)

    def slot_stores(expert):
        return [
            pltpu.make_async_copy(
                source.at[expert], target.at[expert], expert_sems.at[2 + index, expert]
            )
            for index, (source, target) in enumerate(
                ((forward_slots, received_ref), (backward_slots, grad_returned_ref))
            )
        ]

    def narrow_stores(expert):
        buffer = expert % 2
        return [
            pltpu.make_async_copy(
                narrow.at[buffer, index], target.at[expert], expert_sems.at[4 + buffer, index]
            )
            for index, target in enumerate((act_ref, grad_gate_ref, grad_up_ref))
        ]

    def weight_loads(expert):
        buffer = expert % 2
        return [
            pltpu.make_async_copy(
                weights_ref.at[3 * expert + matrix],
                matrices.at[3 * buffer + matrix],
                expert_sems.at[6 + buffer, matrix],
            )
            for matrix in range(3)
        ]

    def fetch(expert):
        for matrix, copy in enumerate(weight_loads(expert)):
            shard_complete(3 * expert + matrix)
            copy.start()

    for expert in range(experts):
        for copy in slot_stores(expert):
            copy.start()
    fetch(0)

    @pl.loop(0, experts)
    def _(expert):
        buffer = expert % 2
        loaded = weight_loads(expert)

        @pl.when(expert >= 2)
        def _():
            for copy in narrow_stores(expert - 2):
                copy.wait()

        received = forward_slots[expert]
        grad_out = backward_slots[expert]
        loaded[0].wait()
        gate_pre = matmul(received, matrices[3 * buffer])
        loaded[1].wait()
        up_pre = matmul(received, matrices[3 * buffer + 1])
        loaded[2].wait()
        grad_act = matmul(grad_out, matrices[3 * buffer + 2])
        gate_sig = jax.nn.sigmoid(gate_pre)
        gate_act = gate_pre * gate_sig
        act = (gate_act * up_pre).astype(jnp.bfloat16)
        grad_gate = (grad_act * up_pre * gate_sig * (1.0 + gate_pre * (1.0 - gate_sig))).astype(
            jnp.bfloat16
        )
        grad_up = (grad_act * gate_act).astype(jnp.bfloat16)
        narrow[buffer, 0] = act
        narrow[buffer, 1] = grad_gate
        narrow[buffer, 2] = grad_up
        for copy in narrow_stores(expert):
            copy.start()
        for copy in slot_stores(expert):
            copy.wait()
        for block in range(3):
            rows_of = pl.ds(block * hidden, hidden)
            spot = pl.ds(block * hidden, hidden)
            out = matmul_nt(act, matrices[3 * buffer + 2, rows_of, :]).astype(jnp.bfloat16)
            forward_slots[expert, :, spot] = (
                out.astype(jnp.float32) * slot_gates[expert]
            ).astype(jnp.bfloat16)
            backward_slots[expert, :, spot] = (
                matmul_nt(grad_gate, matrices[3 * buffer, rows_of, :])
                + matmul_nt(grad_up, matrices[3 * buffer + 1, rows_of, :])
            ).astype(jnp.bfloat16)

        for done, todo in enumerate(((12,), (13,), (14,), (15, 16), (17,))):

            @pl.when(expert == done)
            def _():
                for panel in todo:
                    exchange(panel)
                if done == 4:
                    shard_last(panels - 2)
                    shard_last(panels - 1)

        @pl.when(expert + 1 < experts)
        def _():
            fetch(expert + 1)

    for expert in (experts - 2, experts - 1):
        for copy in narrow_stores(expert):
            copy.wait()
    out_copies = []
    for first, values, target in ((0, backward_slots, grad_parts_ref), (3, forward_slots, routed_parts_ref)):
        for block in range(3):
            spot = slice(block * hidden, (block + 1) * hidden)
            for source in range(4):
                slots_of = jnp.concatenate(
                    [
                        values[expert, source * slots : (source + 1) * slots, spot]
                        for expert in range(experts)
                    ],
                    0,
                )
                matrices[first + block, source * length : (source + 1) * length, :] = matmul_tn(
                    chosen[source], slots_of
                ).astype(jnp.bfloat16)
            out_copies.append(
                pltpu.make_async_copy(
                    matrices.at[first + block, pl.ds(0, 4 * length)],
                    target.at[:, pl.ds(block * hidden, hidden)],
                    load_sems.at[first + block],
                )
            )
            out_copies[-1].start()
    for copy in out_copies:
        copy.wait()

    @pl.loop(0, panels)
    def _(panel):
        shard_finish(panel)

    links.finish()


def front(stripe, gates, masters, hidden_in, cotangent, slots):
    length, width = cotangent.shape
    stripe_rows, columns = stripe.shape
    panels, rows, hidden = masters.shape
    experts = panels // 3
    low, full = jnp.bfloat16, jnp.float32
    vmem = pl.BlockSpec(memory_space=pltpu.VMEM)
    query_width = HEADS * HD
    spots = 4 * slots
    return pl.pallas_call(
        front_kernel,
        in_specs=[ANY] * 3 + [vmem] * 2,
        out_specs=[ANY] * 11 + [vmem] * 11,
        out_shape=[
            jax.ShapeDtypeStruct((stripe_rows * 32, columns), low),
            jax.ShapeDtypeStruct((panels, rows * 8, hidden), low),
            *[jax.ShapeDtypeStruct((length * 4, width), low)] * 4,
            *[jax.ShapeDtypeStruct((experts, spots, width), low)] * 2,
            *[jax.ShapeDtypeStruct((experts, spots, hidden), low)] * 3,
            jax.ShapeDtypeStruct((length, width), low),
            jax.ShapeDtypeStruct((length, query_width + 2 * KVH * HD), low),
            jax.ShapeDtypeStruct((length, query_width), low),
            jax.ShapeDtypeStruct((length, width), full),
            jax.ShapeDtypeStruct((length, 1), full),
            jax.ShapeDtypeStruct((length, width), low),
            jax.ShapeDtypeStruct((length, FFS), low),
            jax.ShapeDtypeStruct((length, 2 * FFS), low),
            jax.ShapeDtypeStruct((length, width), full),
            jax.ShapeDtypeStruct((length, width), full),
            jax.ShapeDtypeStruct((8, width), full),
        ],
        scratch_shapes=[
            pltpu.VMEM((14, width, hidden), low),
            pltpu.VMEM((width, 128), low),
            pltpu.VMEM((4, 4, 8, length), full),
            pltpu.VMEM((experts, 4, length), jnp.int32),
            pltpu.VMEM((experts, 4, length), full),
            pltpu.VMEM((4, experts * slots, length), low),
            pltpu.VMEM((experts, spots, 1), full),
            pltpu.VMEM((experts, spots, width), low),
            pltpu.VMEM((experts, spots, width), low),
            pltpu.VMEM((2, 3, spots, hidden), low),
            pltpu.VMEM((2, rows, hidden), full),
            pltpu.VMEM((2, rows, hidden), low),
            pltpu.SemaphoreType.DMA((170,)),
            pltpu.SemaphoreType.DMA((7, panels)),
            pltpu.SemaphoreType.DMA((7, panels)),
            pltpu.SemaphoreType.DMA((4,)),
            pltpu.SemaphoreType.DMA((15,)),
            pltpu.SemaphoreType.DMA((8, 6)),
        ],
        compiler_params=pltpu.CompilerParams(
            collective_id=1, has_side_effects=True, vmem_limit_bytes=63 * MIB
        ),
        name="front",
    )(stripe, gates, masters, hidden_in, cotangent)


def scatter_kernel(
    grad_parts_ref,
    routed_parts_ref,
    received_ref,
    grad_returned_ref,
    act_ref,
    grad_gate_ref,
    grad_up_ref,
    dense_ref,
    normed_mixer_ref,
    cotangent_ref,
    normed_attend_ref,
    attended_ref,
    grad_shared_pre_ref,
    shared_act_ref,
    residual_ref,
    scale_ref,
    gain_ref,
    grad_shared_ref,
    projected_ref,
    hidden_ref,
    gain_attend_ref,
    expert_sum_ref,
    stripes_ref,
    routed_received_ref,
    grad_input_ref,
    grad_gain_ref,
    grad_gain_attend_ref,
    ring,
    pair_sum,
    corner_x,
    corner_y,
    side_x,
    side_y,
    staged,
    wide,
    narrow,
    left,
    right,
    out_weights,
    grad_tokens,
    grad_attended,
    grad_pair,
    grad_residual_ref,
    key_weights,
    line_out,
    line_in,
    pair_sems,
    slot_sems,
    line_sems,
    token_sems,
    load_sems,
    free,
):
    dp, z = lax.axis_index("dp"), lax.axis_index("expert")
    core, chip = dp % 2, dp // 2
    chip_x, chip_y = flipped(chip, 0), flipped(chip, 1)
    chip_corner = flipped(chip_x, 1)
    device_core = (flipped(dp, 0), z)
    device_x = (flipped(dp, 1), z)
    device_y = (flipped(dp, 2), z)
    others = [(dp, (z + turn) % 4) for turn in range(1, 4)]
    slots = pair_sum.shape[0]
    experts = received_ref.shape[0]
    expert_panels = 3 * experts
    dense_panels = right.shape[0]
    panels = expert_panels + dense_panels
    length, width = residual_ref.shape
    share, hidden = staged.shape[1:]
    half = share // 2
    stripe = share // 4
    query_width = HEADS * HD
    kv_width = KVH * HD
    block = width // 4

    def remote(source, target, send, receive, device):
        return pltpu.make_async_remote_copy(
            src_ref=source,
            dst_ref=target,
            send_sem=send,
            recv_sem=receive,
            device_id=device,
            device_id_type=MESH,
        )

    barrier = pltpu.get_barrier_semaphore()
    for device in (device_core, device_x, device_y, *others):
        pl.semaphore_signal(barrier, inc=1, device_id=device, device_id_type=MESH)
    pl.semaphore_wait(barrier, 6)

    def token_copies(source, target, first):
        return [
            remote(
                source.at[pl.ds(pl.multiple_of(device[1] * length, length), length), :],
                target.at[turn],
                token_sems.at[first + turn],
                token_sems.at[first + 3 + turn],
                device,
            )
            for turn, device in enumerate(others)
        ]

    grad_copies = token_copies(grad_parts_ref, grad_tokens, 0)
    routed_copies = token_copies(routed_parts_ref, routed_received_ref, 6)
    for copy in grad_copies:
        copy.start()

    def expert_loads(expert):
        buffer = expert % 2
        return [
            pltpu.make_async_copy(source.at[expert], target, load_sems.at[buffer, index])
            for index, (source, target) in enumerate(
                (
                    (received_ref, wide.at[buffer, 0]),
                    (grad_returned_ref, wide.at[buffer, 1]),
                    (grad_gate_ref, narrow.at[buffer, 0]),
                    (grad_up_ref, narrow.at[buffer, 1]),
                    (act_ref, narrow.at[buffer, 2]),
                )
            )
        ]

    for copy in expert_loads(0):
        copy.start()

    def columns(ref, panel):
        return ref.at[:, pl.ds(panel * hidden, hidden)]

    sources = [
        (normed_mixer_ref, left.at[0]),
        (cotangent_ref, left.at[1]),
        (normed_attend_ref, left.at[3]),
        *[(columns(grad_shared_pre_ref, panel), right.at[panel]) for panel in range(4)],
        *[(columns(shared_act_ref, panel), right.at[4 + panel]) for panel in range(2)],
        *[(columns(attended_ref, panel), right.at[6 + panel]) for panel in range(3)],
        (dense_ref.at[:, pl.ds(query_width + 2 * kv_width, query_width)], out_weights),
        (dense_ref.at[:, pl.ds(query_width, 2 * kv_width)], key_weights),
        (
            grad_parts_ref.at[pl.ds(pl.multiple_of(z * length, length), length), :],
            grad_tokens.at[3],
        ),
    ]
    dense_loads = [
        pltpu.make_async_copy(source, target, load_sems.at[2 + index // 5, index % 5])
        for index, (source, target) in enumerate(sources)
    ]
    for copy in dense_loads:
        copy.start()
    query_load = pltpu.make_async_copy(
        dense_ref.at[:, pl.ds(0, query_width)], out_weights, pair_sems.at[4]
    )

    def fill(pair, left_ref, right_value):
        for chip_index in range(4):
            part = matmul_tn(left_ref[:, chip_index * block : (chip_index + 1) * block], right_value)
            ring[pair, chip_index] = part.astype(jnp.bfloat16).reshape(2, share, hidden)

    def total(first, *more):
        result = first.astype(jnp.float32)
        for value in more:
            result = result + value.astype(jnp.float32)
        return result

    def pair_copy(panel):
        pair, slot = panel % 2, panel % slots
        return remote(
            ring.at[pair, :, 1 - core],
            pair_sum.at[slot],
            pair_sems.at[pair],
            slot_sems.at[0, slot],
            device_core,
        )

    def corner_copies(panel):
        slot = panel % slots
        return (
            remote(
                pair_sum.at[slot, chip_corner, pl.ds(0, half)],
                corner_x.at[slot],
                slot_sems.at[1, slot],
                slot_sems.at[2, slot],
                device_x,
            ),
            remote(
                pair_sum.at[slot, chip_corner, pl.ds(half, half)],
                corner_y.at[slot],
                slot_sems.at[3, slot],
                slot_sems.at[4, slot],
                device_y,
            ),
        )

    def side_copies(panel):
        slot = panel % slots
        return (
            remote(
                pair_sum.at[slot, chip_x],
                side_x.at[slot],
                slot_sems.at[5, slot],
                slot_sems.at[6, slot],
                device_x,
            ),
            remote(
                pair_sum.at[slot, chip_y],
                side_y.at[slot],
                slot_sems.at[7, slot],
                slot_sems.at[8, slot],
                device_y,
            ),
        )

    def line_copies(panel):
        return [
            remote(
                line_out.at[panel, device[1]],
                line_in.at[panel, turn],
                line_sems.at[0, panel, turn],
                line_sems.at[1, panel, turn],
                device,
            )
            for turn, device in enumerate(others)
        ]

    def staged_copy(panel):
        return pltpu.make_async_copy(
            staged.at[panel % 2], expert_sum_ref.at[panel], pair_sems.at[2 + panel % 2]
        )

    def post(panel):
        @pl.when(panel >= slots)
        def _():
            pl.semaphore_wait(free.at[0], 1)

        pair_copy(panel).start()

    def sum_pair(panel):
        pair, slot = panel % 2, panel % slots
        pair_copy(panel).wait()
        for chip_index in range(4):
            pair_sum[slot, chip_index] = total(
                pair_sum[slot, chip_index], ring[pair, chip_index, core]
            ).astype(jnp.bfloat16)

        @pl.when(panel >= slots)
        def _():
            pl.semaphore_wait(free.at[1], 1)
            pl.semaphore_wait(free.at[2], 1)

        for copy in corner_copies(panel):
            copy.start()

    def sum_corner(panel):
        slot = panel % slots
        for copy in corner_copies(panel):
            copy.wait_recv()
        pair_sum[slot, chip_y, :half] = total(
            pair_sum[slot, chip_y, :half], corner_x[slot]
        ).astype(jnp.bfloat16)
        pair_sum[slot, chip_x, half:] = total(
            pair_sum[slot, chip_x, half:], corner_y[slot]
        ).astype(jnp.bfloat16)
        for copy in side_copies(panel):
            copy.start()

    def sum_sides(panel):
        slot = panel % slots
        for copy in corner_copies(panel):
            copy.wait_send()
        for copy in side_copies(panel):
            copy.wait()
        value = total(pair_sum[slot, chip], side_x[slot], side_y[slot]).astype(jnp.bfloat16)

        @pl.when(panel < expert_panels)
        def _():
            @pl.when(panel >= 2)
            def _():
                staged_copy(panel - 2).wait()

            staged[panel % 2] = value
            staged_copy(panel).start()

        @pl.when(panel >= expert_panels)
        def _():
            index = panel - expert_panels
            line_out[index] = value.reshape(4, stripe, hidden)
            for copy in line_copies(index):
                copy.start()

        @pl.when(panel < panels - slots)
        def _():
            for index, device in enumerate((device_core, device_x, device_y)):
                pl.semaphore_signal(
                    free.at[index], inc=1, device_id=device, device_id_type=MESH
                )

    def residual_backward(part):
        if part == 0:
            for copy in dense_loads:
                copy.wait()
            for copy in grad_copies:
                copy.wait()
            for copy in routed_copies:
                copy.start()
            grad_gain_ref[...] = jnp.zeros_like(grad_gain_ref)
        rows_step = 32
        steps = length // rows_step // 2

        @pl.loop(part * steps, (part + 1) * steps)
        def _(index):
            rows = pl.ds(index * rows_step, rows_step)
            grad_normed = (
                total(
                    grad_tokens[3, rows, :],
                    grad_tokens[0, rows, :],
                    grad_tokens[1, rows, :],
                    grad_tokens[2, rows, :],
                )
                + grad_shared_ref[rows, :]
            )
            residual, scale = residual_ref[rows, :], scale_ref[rows, :]
            grad_scaled = grad_normed * gain_ref[...]
            mean = jnp.mean(grad_scaled * residual, axis=-1, keepdims=True)
            grad_residual = (
                left[1, rows, :].astype(jnp.float32)
                + scale * grad_scaled
                - residual * (scale * scale * scale) * mean
            )
            grad_residual_ref[rows, :] = grad_residual
            left[2, rows, :] = grad_residual.astype(jnp.bfloat16)
            grad_gain_ref[...] += jnp.sum(grad_normed * residual * scale, axis=0, keepdims=True)

    def attended_backward():
        grad_attended[...] = matmul(left[2], out_weights[...]).astype(jnp.bfloat16)
        query_load.start()

    def query_backward():
        query_load.wait()
        for part in range(3):
            update = matmul_nt(right[9 + part], out_weights[:, part * hidden : (part + 1) * hidden])
            if part == 0:
                grad_input_ref[...] = update
            else:
                grad_input_ref[...] += update

    def key_backward():
        for part in range(2):
            grad_input_ref[...] += matmul_nt(
                right[12 + part], key_weights[:, part * hidden : (part + 1) * hidden]
            )

    def input_backward():
        grad_gain_attend_ref[...] = jnp.zeros_like(grad_gain_attend_ref)
        rows_step = 32

        @pl.loop(0, length // rows_step)
        def _(index):
            rows = pl.ds(index * rows_step, rows_step)
            values, grad_normed = hidden_ref[rows, :].astype(jnp.float32), grad_input_ref[rows, :]
            scale = lax.rsqrt(jnp.mean(values * values, axis=-1, keepdims=True) + 1e-06)
            grad_scaled = grad_normed * gain_attend_ref[...]
            mean = jnp.mean(grad_scaled * values, axis=-1, keepdims=True)
            grad_input_ref[rows, :] = (
                grad_residual_ref[rows, :]
                + scale * grad_scaled
                - values * (scale * scale * scale) * mean
            )
            grad_gain_attend_ref[...] += jnp.sum(
                grad_normed * values * scale, axis=0, keepdims=True
            )

    def attention_backward(head):
        score_scale = HD ** (-0.5)
        per_group = HEADS // KVH
        heads_wide = hidden // HD
        group = head // per_group
        key_rows = projected_ref[:, query_width + group * HD : query_width + (group + 1) * HD]
        value_first = query_width + kv_width + group * HD
        value_rows = projected_ref[:, value_first : value_first + HD]
        row = lax.broadcasted_iota(jnp.int32, (length, length), 0)
        column = lax.broadcasted_iota(jnp.int32, (length, length), 1)
        spot = slice(head * HD, (head + 1) * HD)
        query, grad_out = projected_ref[:, spot], grad_attended[:, spot]
        scores = jnp.where(column <= row, matmul_nt(query, key_rows) * score_scale, -1e30)
        raised = jnp.exp(scores - jnp.max(scores, axis=-1, keepdims=True))
        weights = raised / jnp.sum(raised, axis=-1, keepdims=True)
        grad_weights = matmul_nt(grad_out, value_rows)
        inner = jnp.sum(weights * grad_weights, axis=-1, keepdims=True)
        grad_scores = (weights * (grad_weights - inner)).astype(jnp.bfloat16)
        grad_query = matmul(grad_scores, key_rows) * score_scale
        place = slice(head % heads_wide * HD, (head % heads_wide + 1) * HD)
        right[9 + head // heads_wide, :, place] = grad_query.astype(jnp.bfloat16)
        grad_key = matmul_tn(grad_scores, query)
        grad_value = matmul_tn(weights.astype(jnp.bfloat16), grad_out)
        if head % per_group > 0:
            grad_key = grad_key + grad_pair[0]
            grad_value = grad_value + grad_pair[1]
        if head % per_group < per_group - 1:
            grad_pair[0] = grad_key
            grad_pair[1] = grad_value
        else:
            place = slice(group * HD, (group + 1) * HD)
            right[12, :, place] = (grad_key * score_scale).astype(jnp.bfloat16)
            right[13, :, place] = grad_value.astype(jnp.bfloat16)

    @pl.loop(0, panels + 5)
    def _(step):
        @pl.when(step < expert_panels)
        def _():
            expert, matrix = step // 3, step % 3

            @pl.when(matrix == 0)
            def _():
                for copy in expert_loads(expert):
                    copy.wait()

                @pl.when(expert + 1 < experts)
                def _():
                    for copy in expert_loads(expert + 1):
                        copy.start()

            fill(step % 2, wide.at[expert % 2, matrix // 2], narrow[expert % 2, matrix])

        backward = [
            *[functools.partial(residual_backward, part) for part in range(2)],
            attended_backward,
            *[functools.partial(attention_backward, head) for head in range(HEADS)],
            query_backward,
            key_backward,
            input_backward,
        ]
        for index, call in enumerate(backward):
            pl.when(step == GRAD_STEP + index)(call)

        @pl.when((step >= expert_panels) & (step < panels))
        def _():
            panel = step - expert_panels
            which = jnp.where(panel < 4, 0, jnp.where(panel < 6, 1, jnp.where(panel < 9, 2, 3)))
            fill(step % 2, left.at[which], right[panel])

        @pl.when(step < panels)
        def _():
            post(step)

        @pl.when((step >= 1) & (step < panels + 1))
        def _():
            sum_pair(step - 1)

        @pl.when((step >= 3) & (step < panels + 3))
        def _():
            sum_corner(step - 3)

        @pl.when(step >= 5)
        def _():
            sum_sides(step - 5)

    for panel in (expert_panels - 2, expert_panels - 1):
        staged_copy(panel).wait()

    @pl.loop(0, dense_panels)
    def _(panel):
        for copy in line_copies(panel):
            copy.wait()
        stripes_ref[panel] = total(
            line_out[panel, z], line_in[panel, 0], line_in[panel, 1], line_in[panel, 2]
        )

    for copy in routed_copies:
        copy.wait()


def scatter_grads(
    grad_parts,
    routed_parts,
    saved,
    dense_all,
    normed_mixer,
    cotangent,
    normed_attend,
    attended,
    grad_shared_pre,
    shared_act,
    residual,
    scale,
    gain,
    grad_shared,
    projected,
    hidden_in,
    gain_attend,
):
    experts, spots, width = saved[0].shape
    hidden = saved[2].shape[-1]
    length = residual.shape[0]
    share = width // 8
    stripe = share // 4
    dense_panels = 14
    low = jnp.bfloat16
    vmem = pl.BlockSpec(memory_space=pltpu.VMEM)
    return pl.pallas_call(
        scatter_kernel,
        in_specs=[ANY] * 14 + [vmem] * 7,
        out_specs=[ANY, vmem, ANY, vmem, vmem, vmem],
        out_shape=[
            jax.ShapeDtypeStruct((3 * experts, share, hidden), low),
            jax.ShapeDtypeStruct((dense_panels, stripe, hidden), jnp.float32),
            jax.ShapeDtypeStruct((3, length, width), low),
            jax.ShapeDtypeStruct((length, width), jnp.float32),
            jax.ShapeDtypeStruct((1, width), jnp.float32),
            jax.ShapeDtypeStruct((1, width), jnp.float32),
        ],
        scratch_shapes=[
            pltpu.VMEM((2, 4, 2, share, hidden), low),
            pltpu.VMEM((SLOTS, 4, share, hidden), low),
            pltpu.VMEM((SLOTS, share // 2, hidden), low),
            pltpu.VMEM((SLOTS, share // 2, hidden), low),
            pltpu.VMEM((SLOTS, share, hidden), low),
            pltpu.VMEM((SLOTS, share, hidden), low),
            pltpu.VMEM((2, share, hidden), low),
            pltpu.VMEM((2, 2, spots, width), low),
            pltpu.VMEM((2, 3, spots, hidden), low),
            pltpu.VMEM((4, length, width), low),
            pltpu.VMEM((dense_panels, length, hidden), low),
            pltpu.VMEM((width, HEADS * HD), low),
            pltpu.VMEM((4, length, width), low),
            pltpu.VMEM((length, HEADS * HD), low),
            pltpu.VMEM((2, length, HD), jnp.float32),
            pltpu.VMEM((length, width), jnp.float32),
            pltpu.VMEM((width, 2 * KVH * HD), low),
            pltpu.VMEM((dense_panels, 4, stripe, hidden), low),
            pltpu.VMEM((dense_panels, 3, stripe, hidden), low),
            pltpu.SemaphoreType.DMA((5,)),
            pltpu.SemaphoreType.DMA((9, SLOTS)),
            pltpu.SemaphoreType.DMA((2, dense_panels, 3)),
            pltpu.SemaphoreType.DMA((12,)),
            pltpu.SemaphoreType.DMA((5, 5)),
            pltpu.SemaphoreType.REGULAR((3,)),
        ],
        compiler_params=pltpu.CompilerParams(
            collective_id=3, has_side_effects=True, vmem_limit_bytes=62 * MIB
        ),
        name="scatter_grads",
    )(
        grad_parts,
        routed_parts,
        *saved,
        dense_all,
        normed_mixer,
        cotangent,
        normed_attend,
        attended,
        grad_shared_pre,
        shared_act,
        residual,
        scale,
        gain,
        grad_shared,
        projected,
        hidden_in,
        gain_attend,
    )


def muon_kernel(
    expert_ref,
    dense_ref,
    expert_out_ref,
    dense_out_ref,
    dense_back,
    moments,
    units,
    orthogonal,
    current,
    low,
    identity,
    line_sems,
    out_sems,
    in_sems,
    back_out_sems,
    back_in_sems,
    load_sems,
):
    dp, z = lax.axis_index("dp"), lax.axis_index("expert")
    count, share, _ = moments.shape
    first, dense_count = 10, 4
    stripe = dense_ref.shape[1]
    others = [(dp, (z + turn) % 4) for turn in range(1, 4)]
    peers = [((dp + turn) % 8, z) for turn in range(1, 8)]

    def remote(source, target, send, receive, device):
        return pltpu.make_async_remote_copy(
            src_ref=source,
            dst_ref=target,
            send_sem=send,
            recv_sem=receive,
            device_id=device,
            device_id_type=MESH,
        )

    def share_of(index):
        return pl.ds(pl.multiple_of(index * share, share), share)

    def stripe_of(index):
        return pl.ds(pl.multiple_of(index * stripe, stripe), stripe)

    barrier = pltpu.get_barrier_semaphore()
    for device in (*others, *peers):
        pl.semaphore_signal(barrier, inc=1, device_id=device, device_id_type=MESH)
    dense_rows = pl.ds(first, dense_count)
    loads = [
        pltpu.make_async_copy(
            expert_ref.at[pl.ds(0, first)], moments.at[pl.ds(0, first)], load_sems.at[0]
        ),
        pltpu.make_async_copy(
            expert_ref.at[pl.ds(first, count - first - dense_count)],
            moments.at[pl.ds(first + dense_count, count - first - dense_count)],
            load_sems.at[1],
        ),
        pltpu.make_async_copy(
            dense_ref.at[pl.ds(z * dense_count, dense_count)],
            moments.at[dense_rows, stripe_of(z)],
            load_sems.at[2],
        ),
    ]
    for copy in loads:
        copy.start()
    pl.semaphore_wait(barrier, len(others) + len(peers))
    line_copies = [
        remote(
            dense_ref.at[pl.ds(device[1] * dense_count, dense_count)],
            moments.at[dense_rows, stripe_of(z)],
            line_sems.at[0, turn],
            line_sems.at[1, turn],
            device,
        )
        for turn, device in enumerate(others)
    ]
    line_back = [
        remote(
            dense_back.at[:, stripe_of(device[1])],
            dense_out_ref.at[pl.ds(z * dense_count, dense_count)],
            line_sems.at[2, turn],
            line_sems.at[3, turn],
            device,
        )
        for turn, device in enumerate(others)
    ]
    own_back = pltpu.make_async_copy(
        dense_back.at[:, stripe_of(z)],
        dense_out_ref.at[pl.ds(z * dense_count, dense_count)],
        load_sems.at[2],
    )

    def out_copy(slot, turn):
        owner = peers[turn][0]
        return remote(
            moments.at[8 * slot + owner],
            units.at[slot, share_of(dp)],
            out_sems.at[slot, turn],
            in_sems.at[slot],
            peers[turn],
        )

    def own_copy(slot):
        return pltpu.make_async_copy(
            moments.at[8 * slot + dp], units.at[slot, share_of(dp)], load_sems.at[3 + slot]
        )

    def is_dense(slot, owner):
        unit = 8 * slot + owner
        return (unit >= first) & (unit < first + dense_count)

    def expert_place(slot, owner):
        unit = 8 * slot + owner
        return expert_out_ref.at[jnp.where(unit < first, unit, unit - dense_count)]

    def dense_place(slot, owner):
        return dense_back.at[8 * slot + owner - first]

    def back_copy(place, slot, turn):
        return remote(
            orthogonal.at[slot, share_of(peers[turn][0])],
            place(slot, dp),
            back_out_sems.at[slot, turn],
            back_in_sems.at[slot, dp],
            peers[turn],
        )

    def own_back_copy(place, slot):
        return pltpu.make_async_copy(
            orthogonal.at[slot, share_of(dp)], place(slot, dp), load_sems.at[3 + slot]
        )

    def send_back(place, slot):
        for turn in range(7):
            back_copy(place, slot, turn).start()
        own_back_copy(place, slot).start()

    def exists(slot, owner):
        return 8 * slot + owner < count

    def send_slot(slot):
        for turn in range(7):
            pl.when(exists(slot, peers[turn][0]))(out_copy(slot, turn).start)
        pl.when(exists(slot, dp))(own_copy(slot).start)

    for copy in line_copies:
        copy.start()
    loads[0].wait()
    send_slot(0)
    loads[1].wait()
    loads[2].wait()
    for copy in line_copies:
        copy.wait()
    send_slot(1)
    send_slot(2)

    @pl.loop(0, 3)
    def _(slot):
        @pl.when(exists(slot, dp))
        def _():
            own_copy(slot).wait()
            arrived = units.at[slot, pl.ds(0, 7 * share)]
            remote(arrived, arrived, in_sems.at[slot], in_sems.at[slot], peers[0]).wait_recv()
            newton_schulz_unit(units.at[slot], orthogonal.at[slot], current, low, identity)

            @pl.when(is_dense(slot, dp))
            def _():
                send_back(dense_place, slot)

            @pl.when(jnp.logical_not(is_dense(slot, dp)))
            def _():
                send_back(expert_place, slot)

    def own_back_wait(slot):
        def wait():
            pltpu.make_async_copy(
                orthogonal.at[slot, share_of(dp)], expert_out_ref.at[0], load_sems.at[3 + slot]
            ).wait()

        return wait

    def wait_back(slot):
        for turn in range(7):
            owner = peers[turn][0]

            @pl.when(exists(slot, owner))
            def _():
                block = expert_out_ref.at[0]
                semaphore = back_in_sems.at[slot, owner]
                remote(block, block, semaphore, semaphore, peers[0]).wait_recv()

        pl.when(exists(slot, dp))(own_back_wait(slot))

    wait_back(1)
    for copy in line_back:
        copy.start()
    own_back.start()
    wait_back(0)
    wait_back(2)
    for slot in range(3):
        for turn in range(7):
            pl.when(exists(slot, peers[turn][0]))(out_copy(slot, turn).wait_send)

        @pl.when(exists(slot, dp))
        def _():
            for turn in range(7):
                back_copy(expert_place, slot, turn).wait_send()

    for copy in line_back:
        copy.wait()
    own_back.wait()


def muon(expert_units, dense_units):
    experts, share, columns = expert_units.shape
    panels, stripe, _ = dense_units.shape
    count = experts + panels // 4
    low = jnp.bfloat16
    return pl.pallas_call(
        muon_kernel,
        in_specs=[ANY] * 2,
        out_specs=[ANY] * 2,
        out_shape=[
            jax.ShapeDtypeStruct(expert_units.shape, low),
            jax.ShapeDtypeStruct(dense_units.shape, low),
        ],
        scratch_shapes=[
            pltpu.VMEM((panels // 4, share, columns), low),
            pltpu.VMEM((count, share, columns), low),
            pltpu.VMEM((3, 8 * share, columns), low),
            pltpu.VMEM((3, 8 * share, columns), low),
            pltpu.VMEM((columns, 8 * share), jnp.float32),
            pltpu.VMEM((columns, 8 * share), low),
            pltpu.VMEM((columns, columns), low),
            pltpu.SemaphoreType.DMA((4, 3)),
            pltpu.SemaphoreType.DMA((3, 7)),
            pltpu.SemaphoreType.DMA((3,)),
            pltpu.SemaphoreType.DMA((3, 7)),
            pltpu.SemaphoreType.DMA((3, 8)),
            pltpu.SemaphoreType.DMA((6,)),
        ],
        compiler_params=pltpu.CompilerParams(
            collective_id=4, has_side_effects=True, vmem_limit_bytes=56 * MIB
        ),
        name="muon",
    )(expert_units, dense_units)


def update_kernel(weights_ref, orthogonal_ref, new_ref):
    keep_factor = 1.0 - LEARN_RATE * WEIGHT_DECAY
    new_ref[...] = keep_factor * weights_ref[...] - LEARN_RATE * orthogonal_ref[...].astype(
        jnp.float32
    )


def updated_weights(weights, orthogonal):
    panels, rows, columns = orthogonal.shape
    group = 3
    block = pl.BlockSpec((group, rows, columns), lambda index: (index, 0, 0))
    return pl.pallas_call(
        update_kernel,
        grid=(panels // group,),
        in_specs=[block, block],
        out_specs=block,
        out_shape=jax.ShapeDtypeStruct(orthogonal.shape, jnp.float32),
        name="update",
    )(weights.reshape(orthogonal.shape), orthogonal).reshape(weights.shape)


def on_device(
    hidden_in,
    cotangent,
    routes,
    route_weights,
    dense_weights,
    dense_momentum,
    expert_weights,
    expert_momentum,
    norm_gains,
    gain_first,
    gain_second,
):
    length, width = hidden_in.shape
    topk_count = routes.shape[1]
    local_experts = expert_weights.shape[0]
    expert_size = lax.axis_size("expert")
    dp_size = lax.axis_size("dp")
    expert_count = local_experts * expert_size
    capacity = 5 * length * topk_count // (4 * expert_count)
    block_rows = min(512, length)
    query_width = HEADS * HD
    kv_width = KVH * HD
    qkv_end = query_width + 2 * kv_width
    shared_base = 2 * query_width + 2 * kv_width
    gate_table = jnp.sum(
        jnp.where(
            routes.T[None, :, :] == jnp.arange(expert_count, dtype=jnp.int32)[:, None, None],
            route_weights.T[None, :, :],
            0.0,
        ),
        axis=1,
    )
    direct = dp_size == 8 and expert_size == 4
    inputs = hidden_in.astype(jnp.float32)
    scale_attend = norm_scale(inputs)
    if direct:
        stripe_rows = dense_weights.shape[0]
        extra = jnp.zeros((stripe_rows, 128 - norm_gains.shape[0]), jnp.float32)
        plane_gates = gate_table.reshape(expert_size, local_experts, length)
        (
            dense_all,
            _,
            _,
            _,
            routed_parts,
            grad_parts,
            *saved,
            normed_attend,
            projected,
            attended,
            residual,
            scale_mixer,
            normed_mixer,
            shared_act,
            grad_shared_pre,
            grad_shared,
            base_out,
            gains_all,
        ) = front(
            jnp.concatenate(
                [
                    dense_weights[:, :shared_base],
                    norm_gains.T,
                    extra,
                    dense_weights[:, shared_base:],
                ],
                1,
            ).astype(jnp.bfloat16),
            jnp.pad(plane_gates, ((0, 0), (0, 8 - local_experts), (0, 0))),
            expert_weights.reshape(-1, *expert_weights.shape[2:]),
            hidden_in,
            cotangent,
            -(-capacity // 16) * 16,
        )
        gain_attend, gain_mixer = gains_all[0], gains_all[1]
    else:
        gate_tables = lax.all_gather(gate_table, "expert", axis=0, tiled=False)
        cotangents = lax.all_gather(cotangent, "expert", axis=0, tiled=True)
        dense_all, gains_all = (
            lax.all_gather(
                dense_weights.astype(jnp.bfloat16), ("dp", "expert"), axis=0, tiled=True
            ),
            lax.all_gather(norm_gains.astype(jnp.bfloat16), ("dp", "expert"), axis=1, tiled=True),
        )
        gain_attend = gains_all[0].astype(jnp.float32)
        gain_mixer = gains_all[1].astype(jnp.float32)
        normed_attend = (inputs * scale_attend * gain_attend).astype(jnp.bfloat16)
        projected = jnp.dot(
            normed_attend, dense_all[:, :qkv_end], preferred_element_type=jnp.float32
        ).astype(jnp.bfloat16)
        query = projected[:, :query_width]
        key_rows = projected[:, query_width : query_width + kv_width]
        value_rows = projected[:, query_width + kv_width :]
        attended, saved_stats = attend_forward(query, key_rows, value_rows, block_rows)
        residual = inputs + jnp.einsum(
            "sq,dq->sd", attended, dense_all[:, qkv_end:shared_base], preferred_element_type=jnp.float32
        )
        scale_mixer = norm_scale(residual)
        normed_mixer = (residual * scale_mixer * gain_mixer).astype(jnp.bfloat16)
        expert_all = lax.all_gather(expert_weights.astype(jnp.bfloat16), "dp", axis=2, tiled=True)
        tokens = lax.all_gather(normed_mixer, "expert", axis=0, tiled=True)
        shared_pre = jnp.dot(
            normed_mixer,
            dense_all[:, shared_base : shared_base + 2 * FFS],
            preferred_element_type=jnp.float32,
        )
        shared_gate = shared_pre[:, :FFS]
        shared_up = shared_pre[:, FFS:]
        shared_act = (jax.nn.silu(shared_gate) * shared_up).astype(jnp.bfloat16)
        shared_out = jnp.einsum(
            "sf,df->sd",
            shared_act,
            dense_all[:, shared_base + 2 * FFS : shared_base + 3 * FFS],
            preferred_element_type=jnp.float32,
        )
        grad_shared_act = jnp.dot(
            cotangent,
            dense_all[:, shared_base + 2 * FFS : shared_base + 3 * FFS],
            preferred_element_type=jnp.float32,
        )
        shared_sig = jax.nn.sigmoid(shared_gate)
        grad_shared_pre = jnp.concatenate(
            [
                grad_shared_act * shared_up * shared_sig * (1.0 + shared_gate * (1.0 - shared_sig)),
                grad_shared_act * jax.nn.silu(shared_gate),
            ],
            1,
        ).astype(jnp.bfloat16)
        grad_shared = jnp.einsum(
            "sf,df->sd",
            grad_shared_pre,
            dense_all[:, shared_base : shared_base + 2 * FFS],
            preferred_element_type=jnp.float32,
        )
        base_out = residual + shared_out
        my_gates = lax.dynamic_slice_in_dim(
            gate_tables, lax.axis_index("expert") * local_experts, local_experts, 1
        ).transpose(1, 0, 2)
        hot = my_gates > 0.0
        earlier = jnp.einsum(
            "est,ut->esu",
            hot.astype(jnp.bfloat16),
            jnp.tril(jnp.ones((length, length), jnp.bfloat16), -1),
            preferred_element_type=jnp.float32,
        ).astype(jnp.int32)
        place = jnp.where(hot, earlier, -1)
        routed_parts, grad_parts, saved = grouped_experts(
            tokens, cotangents, place, my_gates, expert_all, capacity
        )
    if direct:
        (
            expert_sum,
            dense_sum,
            routed_received,
            grad_inputs,
            grad_gain_mixer,
            grad_gain_attend,
        ) = scatter_grads(
            grad_parts,
            routed_parts,
            saved,
            dense_all,
            normed_mixer,
            cotangent,
            normed_attend,
            attended,
            grad_shared_pre,
            shared_act,
            residual,
            scale_mixer,
            gain_mixer[None, :],
            grad_shared,
            projected,
            hidden_in,
            gain_attend[None, :],
        )
        routed = lax.dynamic_slice_in_dim(
            routed_parts, lax.axis_index("expert") * length, length, 0
        ).astype(jnp.float32)
        routed = routed + jnp.sum(routed_received.astype(jnp.float32), axis=0)
        expert_grad = expert_sum.reshape(expert_weights.shape).astype(jnp.float32)
        dense_grad = (
            jnp.concatenate([dense_sum[9:], dense_sum[6:9], dense_sum[:6]], 0)
            .transpose(1, 0, 2)
            .reshape(dense_weights.shape)
        )
        grad_gain_mixer, grad_gain_attend = grad_gain_mixer[0], grad_gain_attend[0]
    else:
        routed = lax.psum_scatter(routed_parts, "expert", scatter_dimension=0, tiled=True)
        grad_routed = lax.psum_scatter(grad_parts, "expert", scatter_dimension=0, tiled=True)
        expert_parts = [expert_grads(*kept) for kept in saved]
        expert_grad = lax.psum_scatter(
            sum(part.astype(jnp.float32) for part in expert_parts).astype(jnp.bfloat16),
            "dp",
            scatter_dimension=2,
            tiled=True,
        ).astype(jnp.float32)
        grad_normed = grad_routed.astype(jnp.float32) + grad_shared
        grad_scaled = grad_normed * gain_mixer
        grad_residual = (
            cotangent.astype(jnp.float32)
            + scale_mixer * grad_scaled
            - residual * scale_mixer**3 * jnp.mean(grad_scaled * residual, axis=-1, keepdims=True)
        )
        grad_gain_mixer = jnp.sum(grad_normed * residual * scale_mixer, axis=0)
        grad_attn_low = grad_residual.astype(jnp.bfloat16)
        grad_attended = jnp.dot(
            grad_attn_low, dense_all[:, qkv_end:shared_base], preferred_element_type=jnp.float32
        ).astype(jnp.bfloat16)
        grad_query, grad_key, grad_value = attend_backward(
            query, key_rows, value_rows, grad_attended, saved_stats, block_rows
        )
        grad_projected = jnp.concatenate([grad_query, grad_key, grad_value], 1)
        dense_parts = [
            jnp.einsum("sd,sf->df", left, right, preferred_element_type=jnp.float32)
            for left, right in (
                (normed_attend, grad_projected),
                (grad_attn_low, attended),
                (normed_mixer, grad_shared_pre),
                (cotangent, shared_act),
            )
        ]
        dense_grad = lax.psum_scatter(
            jnp.concatenate([part.astype(jnp.bfloat16) for part in dense_parts], 1),
            ("dp", "expert"),
            scatter_dimension=0,
            tiled=True,
        ).astype(jnp.float32)
        grad_normed_attend = jnp.einsum(
            "sc,dc->sd", grad_projected, dense_all[:, :qkv_end], preferred_element_type=jnp.float32
        )
        grad_scaled_attend = grad_normed_attend * gain_attend
        grad_inputs = (
            grad_residual
            + scale_attend * grad_scaled_attend
            - inputs * scale_attend**3 * jnp.mean(grad_scaled_attend * inputs, axis=-1, keepdims=True)
        )
        grad_gain_attend = jnp.sum(grad_normed_attend * inputs * scale_attend, axis=0)
    block_out = (base_out + routed.astype(jnp.float32)).astype(jnp.bfloat16)
    gain_grad = lax.psum_scatter(
        jnp.stack([grad_gain_attend, grad_gain_mixer], 0),
        ("dp", "expert"),
        scatter_dimension=1,
        tiled=True,
    )
    dense_moment = MOMENTUM_DECAY * dense_momentum + dense_grad
    expert_moment = MOMENTUM_DECAY * expert_momentum + expert_grad
    stripe, dense_columns = dense_weights.shape
    row_count = stripe * expert_size
    dense_total = dense_columns // FFE
    dense_share = -(-dense_total // expert_size)
    dense_padded = jnp.pad(
        dense_moment.astype(jnp.bfloat16),
        ((0, 0), (0, dense_share * expert_size * FFE - dense_columns)),
    ).reshape(stripe, dense_share * expert_size, FFE).transpose(1, 0, 2)
    expert_units = expert_moment.astype(jnp.bfloat16).reshape(-1, row_count, FFE)
    if direct:
        orth_expert, orth_stripe = muon(expert_units, dense_padded)
    else:
        dense_units = lax.all_to_all(
            dense_padded, "expert", split_axis=0, concat_axis=1, tiled=True
        )
        expert_unit_count = expert_units.shape[0]
        base_count = expert_unit_count + dense_share
        unit_count = -(-base_count // dp_size) * dp_size
        all_units = jnp.concatenate(
            [
                expert_units,
                dense_units,
                jnp.zeros((unit_count - base_count, row_count, FFE), jnp.bfloat16),
            ],
            0,
        )
        owned = lax.all_to_all(all_units, "dp", split_axis=0, concat_axis=1, tiled=True)
        orthogonal = newton_schulz(owned)
        orth_units = lax.all_to_all(orthogonal, "dp", split_axis=1, concat_axis=0, tiled=True)
        orth_expert = orth_units[:expert_unit_count]
        orth_stripe = lax.all_to_all(
            orth_units[expert_unit_count:base_count],
            "expert",
            split_axis=1,
            concat_axis=0,
            tiled=True,
        )
    orth_stripe = (
        orth_stripe[:dense_total]
        .transpose(1, 0, 2)
        .reshape(stripe, dense_columns)
        .astype(jnp.float32)
    )
    keep_factor = 1.0 - LEARN_RATE * WEIGHT_DECAY
    dense_new = keep_factor * dense_weights - LEARN_RATE * orth_stripe
    expert_new = updated_weights(expert_weights, orth_expert)
    first_new = FIRST_DECAY * gain_first + (1.0 - FIRST_DECAY) * gain_grad
    second_new = SECOND_DECAY * gain_second + (1.0 - SECOND_DECAY) * gain_grad * gain_grad
    step_ratio = (
        first_new
        / (1.0 - FIRST_DECAY**STEP)
        / (jnp.sqrt(second_new / (1.0 - SECOND_DECAY**STEP)) + 1e-08)
    )
    gain_new = norm_gains - GAIN_RATE * step_ratio
    return (
        block_out,
        grad_inputs,
        dense_grad,
        dense_moment,
        dense_new,
        expert_grad,
        expert_moment,
        expert_new,
        gain_grad,
        first_new,
        second_new,
        gain_new,
    )


def solution(mesh):
    in_specs = (
        P(("dp", "expert"), None),
        P(("dp", "expert"), None),
        P(("dp", "expert"), None),
        P(("dp", "expert"), None),
        P(("dp", "expert"), None),
        P(("dp", "expert"), None),
        P("expert", None, "dp", None),
        P("expert", None, "dp", None),
        P(None, ("dp", "expert")),
        P(None, ("dp", "expert")),
        P(None, ("dp", "expert")),
    )
    out_specs = (
        P(("dp", "expert"), None),
        P(("dp", "expert"), None),
        P(("dp", "expert"), None),
        P(("dp", "expert"), None),
        P(("dp", "expert"), None),
        P("expert", None, "dp", None),
        P("expert", None, "dp", None),
        P("expert", None, "dp", None),
        P(None, ("dp", "expert")),
        P(None, ("dp", "expert")),
        P(None, ("dp", "expert")),
        P(None, ("dp", "expert")),
    )
    return jax.shard_map(
        on_device, mesh=mesh, in_specs=in_specs, out_specs=out_specs, check_vma=False
    )
```

time: 2130 us -> 675 us (0.32)
  waiting for transfers between devices: 1080 us -> 0.02 us
  Pallas kernels: 0 us -> 614 us
  matrix products: 351 us -> 0 us
  blocking collectives: 312 us -> 0 us
  local copies, waits for them, and re-layouts: 186 us -> 13.2 us
  other arithmetic: 137 us -> 21.3 us
  starting transfers between devices: 30.3 us -> 0.04 us
    pallas_call x0 -> x4, Pallas kernels: none -> 614 us  [the longest x1 267 us: front(): pl.pallas_call(front_kernel, in_specs=[ANY] * 3 + [vmem] * 2, out_specs=[...]
    reduce_scatter x2 -> x0, waiting for transfers between devices: 506 us -> none  [the longest x1 332 us: on_device(): lax.psum_scatter(grad_dense_local, ('dp', 'expert'), scatter_dimension=0,...]
    all_to_all x5 -> x0, waiting for transfers between devices: 489 us -> none  [the longest x1 159 us: on_device(): lax.all_to_all(expert_out, 'expert', split_axis=1, concat_axis=0, tiled=T...]
    dot_general x38 -> x0, matrix products: 348 us -> none  [the longest x5 93.9 us: newton_schulz(): jnp.einsum('urf,ufg->urg', rounded, polynomial.astype(jnp.bfloat16), pref...]
    all_gather x1 -> x0, blocking collectives: 254 us -> none  [on_device(): lax.all_gather(norm_gains.astype(jnp.bfloat16), ('dp', 'expert'), axis=1,...]
    all_gather x4 -> x0, waiting for transfers between devices: 61.1 us -> none  [the longest x2 61.1 us: rows_over_expert(): lax.all_gather(shortened(values), 'expert', axis=0, tiled=True)]
    all_to_all x1 -> x0, blocking collectives: 58.1 us -> none  [on_device(): lax.all_to_all(outgoing_units.astype(jnp.bfloat16), 'dp', split_axis=0, c...]
    convert_element_type x10 -> x0, local copies, waits for them, and re-layouts: 56.8 us -> none  [the longest x1 9.31 us: on_device(): picked = returned.reshape(slot_total, width)[slots].reshape(length, topk_...]
  transfers between devices with their start and end apart: 18 -> 1, of which waited for: 14 -> 0; matrix products, arithmetic and copies ran while one was open for 14% -> 3% of each run, Pallas kernels for 0% -> 17%
where the time goes in v1:
time: 675 us; the launch traced here: 664 us
  Pallas kernels  614 us (91%)
  other arithmetic  21.3 us (3%)
  between operations  14.7 us (2%)
  local copies, waits for them, and re-layouts  13.2 us (2%)
    pallas_call x1, Pallas kernels, front(): pl.pallas_call(front_kernel, in_specs=[ANY] * 3 + [vmem] * 2, out_specs=[...  267 us
    pallas_call x1, Pallas kernels, scatter_grads(): pl.pallas_call(scatter_kernel, in_specs=[ANY] * 14 + [vmem] * 7, out_spec...  233 us
    pallas_call x1, Pallas kernels, muon(): pl.pallas_call(muon_kernel, in_specs=[ANY] * 2, out_specs=[ANY] * 2, out_...  106 us
  transfers between devices with their start and end apart: 1, of which 0 were waited for; matrix products, arithmetic and copies ran while one was open for 3% of the time, Pallas kernels for 17%

profile of v1, /device:TPU:0, one launch (start us, length us, event | category | flops | bytes accessed | tf_op | source)
XLA Modules:
  0.0 663.5 jit_solution(512131783061707438)
XLA Ops:
  7.3 1.4 convert.13
  8.9 0.6 pad.8.gates_ref
  9.5 1.0 concatenate.7.stripe_ref
  10.5 267.4 %front.1 = (bf16[1536,7296]{1,0:T(8,128)(2,1)}, bf16[18,1536,512]{2,1,0:T(8,128)(2,1)}, bf16[1024,1536]{1,0:T(8,128)(2,1)}, bf16[1024,1536]{1,0:T(8,128)(2,1)}, ...) custom-call(bf16[48,7296]{1,0:T(8,128)(2,1)} %concatenate.7.stripe_r, ...), custom_call_target="tpu_custom_call" | custom-call | tf_op jit(solution)/shard_map/front/pallas_call | solution.py:1091
  277.9 1.5 fusion.4
  279.4 232.5 %scatter_grads.1 = (bf16[18,192,512]{2,1,0:T(8,128)(2,1)}, f32[14,48,512]{2,1,0:T(8,128)}, bf16[3,256,1536]{2,1,0:T(8,128)(2,1)}, f32[256,1536]{1,0:T(8,128)}, f32[1,1536]{1,0:T(1,128)}, /*index=5*/f32[1,1536]{1,0:T(1,128)}) custom-call(bf16[1024,1536]{1,0:T(8,128)(2,1)} %get-tuple-element.41.grad_parts_ref, ...), custom_call_target="tpu_custom_call" | custom-call | tf_op jit(solution)/shard_map/scatter_grads/pallas_call | solution.py:1637
  511.9 0.8 pad_maximum_fusion
  512.8 1.2 copy.36
  514.4 1.7 copy-done.6
  516.1 1.3 fusion.2
  517.4 1.0 copy.42
  518.4 0.5 copy-done.2
  518.9 11.8 %fusion.3 = (bf16[6,3,192,512]{3,2,1,0:T(8,128)(2,1)}, f32[6,3,192,512]{3,2,1,0:T(8,128)}, f32[6,3,192,512]{3,2,1,0:T(8,128)}) fusion(f32[6,3,192,512]{3,2,1,0:T(8,128)} %param.18, bf16[6,3,192,512]{3,2,1,0:T(8,128)(2,1)S(1)} %bitcast.32), kind=kLoop, calls=%fused_computation.17 | loop fusion | flops 7077888 | bytes 28311552 | tf_op jit(solution)/shard_map/convert_element_type | solution.py:2224
  530.7 106.2 %muon.1 = (bf16[18,192,512]{2,1,0:T(8,128)(2,1)}, bf16[16,48,512]{2,1,0:T(8,128)(2,1)}) custom-call(bf16[18,192,512]{2,1,0:T(8,128)(2,1)} %bitcast.27, bf16[16,48,512]{2,1,0:T(8,128)(2,1)} %bitcast.35), custom_call_target="tpu_custom_call" | custom-call | tf_op jit(solution)/shard_map/muon/pallas_call | solution.py:1917
  636.9 1.3 multiply_bitcast_fusion
  638.3 1.2 copy-done
  639.5 1.2 multiply_subtract_fusion
  640.7 0.9 copy-done.3
  642.0 1.0 copy-done.4
  643.1 2.4 add_convert_fusion
  645.4 8.3 %update.1 = f32[18,192,512]{2,1,0:T(8,128)} custom-call(f32[18,192,512]{2,1,0:T(8,128)} %bitcast.26, bf16[18,192,512]{2,1,0:T(8,128)(2,1)} %get-tuple-element.63.orthogonal_ref), custom_call_target="tpu_custom_call" | custom-call | tf_op jit(solution)/shard_map/update/pallas_call | solution.py:1958
  653.7 0.8 copy.37
  654.5 0.6 multiply_subtract_fusion.1
  655.1 1.1 copy.44
  (41 shorter events, 1.2 us)
Async XLA Ops:
  7.2 1.6 copy-start.11
  7.2 1.7 copy-start.9
  7.2 1.7 copy-start.8
  7.2 646.5 %reduce-scatter.4.cloned.1.call-start = ((), (), s32[]{:S(2)}) async-start(), calls=%async_computation.1 | async-start | bytes 811008
  511.9 2.1 copy-start.7
  514.2 1.8 copy-start.6
  514.4 3.0 copy-start.1
  516.1 2.8 copy-start.2
  638.1 1.3 copy-start
  639.5 2.2 copy-start.3
  641.7 1.4 copy-start.4
  645.4 9.1 %copy-start.12 = (f32[2,48]{1,0:T(2,128)S(1)}, f32[2,48]{1,0:T(2,128)}, u32[]{:S(2)}) copy-start(f32[2,48]{1,0:T(2,128)} %param.21) | copy-start | bytes 1156
  645.4 9.1 %copy-start.13 = (f32[2,48]{1,0:T(2,128)S(1)}, f32[2,48]{1,0:T(2,128)}, u32[]{:S(2)}) copy-start(f32[2,48]{1,0:T(2,128)} %param.20) | copy-start | bytes 1156
  645.4 9.7 %copy-start.5 = (f32[256,1536]{1,0:T(8,128)S(1)}, f32[256,1536]{1,0:T(8,128)}, u32[]{:S(2)}) copy-start(f32[256,1536]{1,0:T(8,128)} %get-tuple-element.89) | copy-start | bytes 4718596
  654.5 1.7 copy-start.10
Sparse Core Ops, SparseCore 0:
  514.1 110.3 reduce-scatter.3

commit v2 on v1

--- a/solution.py
+++ b/solution.py
@@ -104,7 +104,7 @@
 
 
 MIB = 2**20
-GRAD_STEP = 11
+GRAD_STEP = 14
 SLOTS = 8
 MESH = pl.DeviceIdType.MESH
 
@@ -531,24 +531,28 @@
     grad_shared_ref,
     base_ref,
     gains_ref,
+    shared_sum_ref,
     matrices,
     extra,
     all_gates,
     places,
     my_gates,
     chosen,
-    slot_gates,
     forward_slots,
     backward_slots,
     narrow,
-    masters,
-    rounded,
+    pair_sum,
+    corner_x,
+    corner_y,
+    side_x,
+    side_y,
     semaphores,
     shard_out,
     shard_in,
     local,
     load_sems,
     expert_sems,
+    shared_sems,
 ):
     links = Links(semaphores)
     stripe, columns = stripe_ref.shape
@@ -659,8 +663,8 @@
         shard_forward(panel)
         if panel + ahead < panels:
             shard_start(panel + ahead)
-        if panel >= 2:
-            shard_last(panel - 2)
+        if panel >= 3:
+            shard_last(panel - 3)
 
     local_copies = [
         pltpu.make_async_copy(source, target, local.at[index])
@@ -696,14 +700,21 @@
         dense_ref.at[:, pl.ds(first_panels * hidden, extra.shape[1])], extra, load_sems.at[14]
     )
 
+    def half_columns(panel):
+        return pl.ds(pl.multiple_of(panel % 2 * hidden, hidden), hidden)
+
     def master_load(panel):
         return pltpu.make_async_copy(
-            masters_ref.at[panel], masters.at[panel % 2], expert_sems.at[0, panel % 2]
+            masters_ref.at[panel],
+            grad_shared_ref.at[pl.ds(0, rows), half_columns(panel)],
+            expert_sems.at[0, panel % 2],
         )
 
     def master_store(panel):
         return pltpu.make_async_copy(
-            rounded.at[panel % 2], shard_region(dp, panel), expert_sems.at[1, panel % 2]
+            shared_act_ref.at[pl.ds(0, rows), half_columns(panel)],
+            shard_region(dp, panel),
+            expert_sems.at[1, panel % 2],
         )
 
     master_load(0).start()
@@ -728,23 +739,29 @@
             def _():
                 master_store(panel - 2).wait()
 
-            rounded[panel % 2] = masters[panel % 2].astype(jnp.bfloat16)
+            shared_act_ref[:rows, half_columns(panel)] = grad_shared_ref[
+                :rows, half_columns(panel)
+            ].astype(jnp.bfloat16)
             master_store(panel).start()
 
     lines[0].arrive(1)
     planes[0][1].start()
     lines[0].arrive(2)
     planes[0][2].start()
-    round_masters(0, panels // 2)
+    round_masters(0, panels // 3)
+    for panel in range(2):
+        shard_start(panel)
     planes[0][0].forward()
     lines[0].relay()
     lines[0].arrive(3)
     planes[0][3].start()
     planes[0][1].forward()
     lines[1].relay()
-    round_masters(panels // 2, panels)
+    round_masters(panels // 3, panels)
     for panel in (panels - 2, panels - 1):
         master_store(panel).wait()
+    for panel in range(2, ahead):
+        shard_start(panel)
     planes[1][0].start()
     planes[0][2].forward()
     lines[1].arrive(1)
@@ -861,6 +878,93 @@
                 places[expert, source : source + 1, :] = place[expert : expert + 1, :]
                 my_gates[expert, source : source + 1, :] = gate[expert : expert + 1, :]
 
+    core, chip = dp % 2, dp // 2
+    chip_x, chip_y = flipped(chip, 0), flipped(chip, 1)
+    chip_corner = flipped(chip_x, 1)
+    shared_panels = pair_sum.shape[0]
+    half = rows // 2
+    quarter = width // 4
+
+    ring = matrices.at[13]
+
+    def ring_rows(index, which):
+        return pl.ds(pl.multiple_of((2 * index + which) * rows, rows), rows)
+
+    def pair_copy(panel, index):
+        return links.copy_with(
+            ring.at[ring_rows(index, 1 - core)],
+            pair_sum.at[panel, index],
+            shared_sems.at[0, 0, panel],
+            shared_sems.at[1, 0, panel],
+            links.core,
+        )
+
+    def shared_copy(kind, panel):
+        source, target, device = (
+            (pair_sum.at[panel], pair_sum.at[panel], links.core),
+            (pair_sum.at[panel, chip_corner, pl.ds(0, half)], corner_x.at[panel], links.along_x),
+            (pair_sum.at[panel, chip_corner, pl.ds(half, half)], corner_y.at[panel], links.along_y),
+            (pair_sum.at[panel, chip_x], side_x.at[panel], links.along_x),
+            (pair_sum.at[panel, chip_y], side_y.at[panel], links.along_y),
+        )[kind]
+        return links.copy_with(
+            source, target, shared_sems.at[0, kind, panel], shared_sems.at[1, kind, panel], device
+        )
+
+    def shared_fill(panel):
+        left_ref = normed_mixer_ref if panel < 4 else cotangent_ref
+        right_ref = grad_shared_pre_ref if panel < 4 else shared_act_ref
+        first = (panel if panel < 4 else panel - 4) * hidden
+        right = right_ref[:, first : first + hidden]
+        for index in range(4):
+            part = matmul_tn(left_ref[:, index * quarter : (index + 1) * quarter], right)
+            ring[index * quarter : (index + 1) * quarter, :] = part.astype(jnp.bfloat16)
+        for index in range(4):
+            pair_copy(panel, index).start()
+
+    def shared_pair(panel):
+        shared_copy(0, panel).wait()
+        for index in range(4):
+            pair_sum[panel, index] = (
+                pair_sum[panel, index].astype(jnp.float32)
+                + ring[ring_rows(index, core), :].astype(jnp.float32)
+            ).astype(jnp.bfloat16)
+
+    def shared_corners(panel):
+        for kind in (1, 2):
+            shared_copy(kind, panel).start()
+
+    def shared_sides(panel):
+        for kind in (1, 2):
+            shared_copy(kind, panel).wait()
+        pair_sum[panel, chip_y, :half] = (
+            pair_sum[panel, chip_y, :half].astype(jnp.float32)
+            + corner_x[panel].astype(jnp.float32)
+        ).astype(jnp.bfloat16)
+        pair_sum[panel, chip_x, half:] = (
+            pair_sum[panel, chip_x, half:].astype(jnp.float32)
+            + corner_y[panel].astype(jnp.float32)
+        ).astype(jnp.bfloat16)
+        for kind in (3, 4):
+            shared_copy(kind, panel).start()
+
+    def shared_total(panel):
+        for kind in (3, 4):
+            shared_copy(kind, panel).wait()
+        value = (
+            pair_sum[panel, chip].astype(jnp.float32)
+            + side_x[panel].astype(jnp.float32)
+            + side_y[panel].astype(jnp.float32)
+        )
+        matrices[12, pl.ds(panel % 2 * rows, rows), :] = value.astype(jnp.bfloat16)
+
+    def shared_store(panel):
+        return pltpu.make_async_copy(
+            matrices.at[12, pl.ds(panel % 2 * rows, rows)],
+            shared_sum_ref.at[panel],
+            local.at[4 + panel % 2],
+        )
+
     project()
     lines[1].arrive(3)
     planes[1][3].start()
@@ -868,15 +972,11 @@
     attend(0)
     attend(1)
     planes[1][2].forward()
-    for panel in range(2):
-        shard_start(panel)
     attend(2)
     attend(3)
     planes[1][3].forward()
     cotangents.relay()
     join()
-    for panel in range(2, ahead):
-        shard_start(panel)
     for plane in planes[1]:
         plane.last()
     for index in range(1, 4):
@@ -895,9 +995,14 @@
     exchange(3)
     shared_back(1)
     exchange(4)
+    shared_fill(0)
     tokens.relay()
     for panel in range(5, 11):
         exchange(panel)
+        shared_pair(panel - 5)
+        shared_corners(panel - 5)
+        if panel < 10:
+            shared_fill(panel - 4)
     for index in range(1, 4):
         cotangents.arrive(index)
         tokens.arrive(index)
@@ -915,17 +1020,19 @@
     for copy in token_loads:
         copy.start()
     slot_iota = lax.broadcasted_iota(jnp.int32, (slots, length), 0)
+
+    def slot_gate(expert, source):
+        hot = slot_iota == places[expert, pl.ds(source, 1), :]
+        return jnp.sum(
+            jnp.where(hot, my_gates[expert, pl.ds(source, 1), :], 0.0), axis=1, keepdims=True
+        )
+
     for source in range(4):
         for expert in range(experts):
             hot = slot_iota == places[expert, source : source + 1, :]
             chosen[source, expert * slots : (expert + 1) * slots, :] = jnp.where(
                 hot, 1.0, 0.0
             ).astype(jnp.bfloat16)
-            slot_gates[expert, source * slots : (source + 1) * slots, :] = jnp.sum(
-                jnp.where(hot, my_gates[expert, source : source + 1, :], 0.0),
-                axis=1,
-                keepdims=True,
-            )
     exchange(11)
     for copy in token_loads:
         copy.wait()
@@ -934,6 +1041,7 @@
     def _(source):
         part = pl.ds(source * length, length)
         spots = pl.ds(pl.multiple_of(source * slots, slots), slots)
+        slot_gates = [slot_gate(expert, source) for expert in range(experts)]
         for block in range(3):
             spot = pl.ds(block * hidden, hidden)
             token_slots = matmul(chosen[source], matrices[6 + block, part, :])
@@ -942,7 +1050,7 @@
                 rows_of = slice(expert * slots, (expert + 1) * slots)
                 forward_slots[expert, spots, spot] = token_slots[rows_of].astype(jnp.bfloat16)
                 backward_slots[expert, spots, spot] = (
-                    grad_slots[rows_of] * slot_gates[expert, spots, :]
+                    grad_slots[rows_of] * slot_gates[expert]
                 ).astype(jnp.bfloat16)
 
     def slot_stores(expert):
@@ -1017,27 +1125,40 @@
             copy.start()
         for copy in slot_stores(expert):
             copy.wait()
+        slot_gates = jnp.concatenate([slot_gate(expert, source) for source in range(4)], 0)
         for block in range(3):
             rows_of = pl.ds(block * hidden, hidden)
             spot = pl.ds(block * hidden, hidden)
             out = matmul_nt(act, matrices[3 * buffer + 2, rows_of, :]).astype(jnp.bfloat16)
             forward_slots[expert, :, spot] = (
-                out.astype(jnp.float32) * slot_gates[expert]
+                out.astype(jnp.float32) * slot_gates
             ).astype(jnp.bfloat16)
             backward_slots[expert, :, spot] = (
                 matmul_nt(grad_gate, matrices[3 * buffer, rows_of, :])
                 + matmul_nt(grad_up, matrices[3 * buffer + 1, rows_of, :])
             ).astype(jnp.bfloat16)
 
-        for done, todo in enumerate(((12,), (13,), (14,), (15, 16), (17,))):
+        later = (
+            (lambda: exchange(12), lambda: shared_sides(0)),
+            (lambda: exchange(13), lambda: shared_sides(1)),
+            (lambda: exchange(14), lambda: shared_sides(2)),
+            (lambda: exchange(15), lambda: exchange(16), lambda: shard_last(14)),
+            (
+                lambda: shard_forward(17),
+                lambda: shared_sides(3),
+                lambda: shared_sides(4),
+                lambda: shared_sides(5),
+                lambda: shard_last(15),
+                lambda: shard_last(16),
+                lambda: shard_last(17),
+            ),
+        )
+        for done, calls in enumerate(later):
 
             @pl.when(expert == done)
             def _():
-                for panel in todo:
-                    exchange(panel)
-                if done == 4:
-                    shard_last(panels - 2)
-                    shard_last(panels - 1)
+                for call in calls:
+                    call()
 
         @pl.when(expert + 1 < experts)
         def _():
@@ -1069,12 +1190,19 @@
                 )
             )
             out_copies[-1].start()
-    for copy in out_copies:
-        copy.wait()
-
     @pl.loop(0, panels)
     def _(panel):
         shard_finish(panel)
+
+    for panel in range(shared_panels):
+        if panel >= 2:
+            shared_store(panel - 2).wait()
+        shared_total(panel)
+        shared_store(panel).start()
+    for panel in (shared_panels - 2, shared_panels - 1):
+        shared_store(panel).wait()
+    for copy in out_copies:
+        copy.wait()
 
     links.finish()
 
@@ -1091,7 +1219,7 @@
     return pl.pallas_call(
         front_kernel,
         in_specs=[ANY] * 3 + [vmem] * 2,
-        out_specs=[ANY] * 11 + [vmem] * 11,
+        out_specs=[ANY] * 11 + [vmem] * 11 + [ANY],
         out_shape=[
             jax.ShapeDtypeStruct((stripe_rows * 32, columns), low),
             jax.ShapeDtypeStruct((panels, rows * 8, hidden), low),
@@ -1109,6 +1237,7 @@
             jax.ShapeDtypeStruct((length, width), full),
             jax.ShapeDtypeStruct((length, width), full),
             jax.ShapeDtypeStruct((8, width), full),
+            jax.ShapeDtypeStruct((6, rows, hidden), low),
         ],
         scratch_shapes=[
             pltpu.VMEM((14, width, hidden), low),
@@ -1117,18 +1246,21 @@
             pltpu.VMEM((experts, 4, length), jnp.int32),
             pltpu.VMEM((experts, 4, length), full),
             pltpu.VMEM((4, experts * slots, length), low),
-            pltpu.VMEM((experts, spots, 1), full),
             pltpu.VMEM((experts, spots, width), low),
             pltpu.VMEM((experts, spots, width), low),
             pltpu.VMEM((2, 3, spots, hidden), low),
-            pltpu.VMEM((2, rows, hidden), full),
-            pltpu.VMEM((2, rows, hidden), low),
+            pltpu.VMEM((6, 4, rows, hidden), low),
+            pltpu.VMEM((6, rows // 2, hidden), low),
+            pltpu.VMEM((6, rows // 2, hidden), low),
+            pltpu.VMEM((6, rows, hidden), low),
+            pltpu.VMEM((6, rows, hidden), low),
             pltpu.SemaphoreType.DMA((170,)),
             pltpu.SemaphoreType.DMA((7, panels)),
             pltpu.SemaphoreType.DMA((7, panels)),
-            pltpu.SemaphoreType.DMA((4,)),
+            pltpu.SemaphoreType.DMA((6,)),
             pltpu.SemaphoreType.DMA((15,)),
             pltpu.SemaphoreType.DMA((8, 6)),
+            pltpu.SemaphoreType.DMA((2, 5, 6)),
         ],
         compiler_params=pltpu.CompilerParams(
             collective_id=1, has_side_effects=True, vmem_limit_bytes=63 * MIB
@@ -1139,19 +1271,16 @@
 
 def scatter_kernel(
     grad_parts_ref,
-    routed_parts_ref,
     received_ref,
     grad_returned_ref,
     act_ref,
     grad_gate_ref,
     grad_up_ref,
     dense_ref,
-    normed_mixer_ref,
+    shared_sum_ref,
     cotangent_ref,
     normed_attend_ref,
     attended_ref,
-    grad_shared_pre_ref,
-    shared_act_ref,
     residual_ref,
     scale_ref,
     gain_ref,
@@ -1161,7 +1290,6 @@
     gain_attend_ref,
     expert_sum_ref,
     stripes_ref,
-    routed_received_ref,
     grad_input_ref,
     grad_gain_ref,
     grad_gain_attend_ref,
@@ -1202,8 +1330,9 @@
     slots = pair_sum.shape[0]
     experts = received_ref.shape[0]
     expert_panels = 3 * experts
-    dense_panels = right.shape[0]
-    panels = expert_panels + dense_panels
+    dense_panels = line_out.shape[0]
+    shared_panels = dense_panels - right.shape[0]
+    panels = expert_panels + right.shape[0]
     length, width = residual_ref.shape
     share, hidden = staged.shape[1:]
     half = share // 2
@@ -1227,20 +1356,16 @@
         pl.semaphore_signal(barrier, inc=1, device_id=device, device_id_type=MESH)
     pl.semaphore_wait(barrier, 6)
 
-    def token_copies(source, target, first):
-        return [
-            remote(
-                source.at[pl.ds(pl.multiple_of(device[1] * length, length), length), :],
-                target.at[turn],
-                token_sems.at[first + turn],
-                token_sems.at[first + 3 + turn],
-                device,
-            )
-            for turn, device in enumerate(others)
-        ]
-
-    grad_copies = token_copies(grad_parts_ref, grad_tokens, 0)
-    routed_copies = token_copies(routed_parts_ref, routed_received_ref, 6)
+    grad_copies = [
+        remote(
+            grad_parts_ref.at[pl.ds(pl.multiple_of(device[1] * length, length), length), :],
+            grad_tokens.at[turn],
+            token_sems.at[turn],
+            token_sems.at[3 + turn],
+            device,
+        )
+        for turn, device in enumerate(others)
+    ]
     for copy in grad_copies:
         copy.start()
 
@@ -1266,12 +1391,10 @@
         return ref.at[:, pl.ds(panel * hidden, hidden)]
 
     sources = [
-        (normed_mixer_ref, left.at[0]),
-        (cotangent_ref, left.at[1]),
-        (normed_attend_ref, left.at[3]),
-        *[(columns(grad_shared_pre_ref, panel), right.at[panel]) for panel in range(4)],
-        *[(columns(shared_act_ref, panel), right.at[4 + panel]) for panel in range(2)],
-        *[(columns(attended_ref, panel), right.at[6 + panel]) for panel in range(3)],
+        (cotangent_ref, left.at[0]),
+        (normed_attend_ref, left.at[2]),
+        *[(columns(attended_ref, panel), right.at[panel]) for panel in range(3)],
+        (shared_sum_ref, line_out.at[pl.ds(0, shared_panels)]),
         (dense_ref.at[:, pl.ds(query_width + 2 * kv_width, query_width)], out_weights),
         (dense_ref.at[:, pl.ds(query_width, 2 * kv_width)], key_weights),
         (
@@ -1351,7 +1474,7 @@
     def line_copies(panel):
         return [
             remote(
-                line_out.at[panel, device[1]],
+                line_out.at[panel, pl.ds(pl.multiple_of(device[1] * stripe, stripe), stripe)],
                 line_in.at[panel, turn],
                 line_sems.at[0, panel, turn],
                 line_sems.at[1, panel, turn],
@@ -1420,8 +1543,8 @@
 
         @pl.when(panel >= expert_panels)
         def _():
-            index = panel - expert_panels
-            line_out[index] = value.reshape(4, stripe, hidden)
+            index = panel - expert_panels + shared_panels
+            line_out[index] = value
             for copy in line_copies(index):
                 copy.start()
 
@@ -1438,8 +1561,6 @@
                 copy.wait()
             for copy in grad_copies:
                 copy.wait()
-            for copy in routed_copies:
-                copy.start()
             grad_gain_ref[...] = jnp.zeros_like(grad_gain_ref)
         rows_step = 32
         steps = length // rows_step // 2
@@ -1460,22 +1581,22 @@
             grad_scaled = grad_normed * gain_ref[...]
             mean = jnp.mean(grad_scaled * residual, axis=-1, keepdims=True)
             grad_residual = (
-                left[1, rows, :].astype(jnp.float32)
+                left[0, rows, :].astype(jnp.float32)
                 + scale * grad_scaled
                 - residual * (scale * scale * scale) * mean
             )
             grad_residual_ref[rows, :] = grad_residual
-            left[2, rows, :] = grad_residual.astype(jnp.bfloat16)
+            left[1, rows, :] = grad_residual.astype(jnp.bfloat16)
             grad_gain_ref[...] += jnp.sum(grad_normed * residual * scale, axis=0, keepdims=True)
 
     def attended_backward():
-        grad_attended[...] = matmul(left[2], out_weights[...]).astype(jnp.bfloat16)
+        grad_attended[...] = matmul(left[1], out_weights[...]).astype(jnp.bfloat16)
         query_load.start()
 
     def query_backward():
         query_load.wait()
         for part in range(3):
-            update = matmul_nt(right[9 + part], out_weights[:, part * hidden : (part + 1) * hidden])
+            update = matmul_nt(right[3 + part], out_weights[:, part * hidden : (part + 1) * hidden])
             if part == 0:
                 grad_input_ref[...] = update
             else:
@@ -1484,7 +1605,7 @@
     def key_backward():
         for part in range(2):
             grad_input_ref[...] += matmul_nt(
-                right[12 + part], key_weights[:, part * hidden : (part + 1) * hidden]
+                right[6 + part], key_weights[:, part * hidden : (part + 1) * hidden]
             )
 
     def input_backward():
@@ -1527,7 +1648,7 @@
         grad_scores = (weights * (grad_weights - inner)).astype(jnp.bfloat16)
         grad_query = matmul(grad_scores, key_rows) * score_scale
         place = slice(head % heads_wide * HD, (head % heads_wide + 1) * HD)
-        right[9 + head // heads_wide, :, place] = grad_query.astype(jnp.bfloat16)
+        right[3 + head // heads_wide, :, place] = grad_query.astype(jnp.bfloat16)
         grad_key = matmul_tn(grad_scores, query)
         grad_value = matmul_tn(weights.astype(jnp.bfloat16), grad_out)
         if head % per_group > 0:
@@ -1538,8 +1659,12 @@
             grad_pair[1] = grad_value
         else:
             place = slice(group * HD, (group + 1) * HD)
-            right[12, :, place] = (grad_key * score_scale).astype(jnp.bfloat16)
-            right[13, :, place] = grad_value.astype(jnp.bfloat16)
+            right[6, :, place] = (grad_key * score_scale).astype(jnp.bfloat16)
+            right[7, :, place] = grad_value.astype(jnp.bfloat16)
+
+    def two_heads_backward(head):
+        attention_backward(head)
+        attention_backward(head + 1)
 
     @pl.loop(0, panels + 5)
     def _(step):
@@ -1562,7 +1687,7 @@
         backward = [
             *[functools.partial(residual_backward, part) for part in range(2)],
             attended_backward,
-            *[functools.partial(attention_backward, head) for head in range(HEADS)],
+            *[functools.partial(two_heads_backward, head) for head in range(0, HEADS, 2)],
             query_backward,
             key_backward,
             input_backward,
@@ -1573,8 +1698,13 @@
         @pl.when((step >= expert_panels) & (step < panels))
         def _():
             panel = step - expert_panels
-            which = jnp.where(panel < 4, 0, jnp.where(panel < 6, 1, jnp.where(panel < 9, 2, 3)))
-            fill(step % 2, left.at[which], right[panel])
+            fill(step % 2, left.at[jnp.where(panel < 3, 1, 2)], right[panel])
+
+        @pl.when(step == GRAD_STEP + 1)
+        def _():
+            for panel in range(shared_panels):
+                for copy in line_copies(panel):
+                    copy.start()
 
         @pl.when(step < panels)
         def _():
@@ -1600,24 +1730,19 @@
         for copy in line_copies(panel):
             copy.wait()
         stripes_ref[panel] = total(
-            line_out[panel, z], line_in[panel, 0], line_in[panel, 1], line_in[panel, 2]
-        )
-
-    for copy in routed_copies:
-        copy.wait()
+            line_out[panel, pl.ds(pl.multiple_of(z * stripe, stripe), stripe), :],
+            line_in[panel, 0], line_in[panel, 1], line_in[panel, 2]
+        )
 
 
 def scatter_grads(
     grad_parts,
-    routed_parts,
     saved,
     dense_all,
-    normed_mixer,
+    shared_sum,
     cotangent,
     normed_attend,
     attended,
-    grad_shared_pre,
-    shared_act,
     residual,
     scale,
     gain,
@@ -1636,12 +1761,11 @@
     vmem = pl.BlockSpec(memory_space=pltpu.VMEM)
     return pl.pallas_call(
         scatter_kernel,
-        in_specs=[ANY] * 14 + [vmem] * 7,
-        out_specs=[ANY, vmem, ANY, vmem, vmem, vmem],
+        in_specs=[ANY] * 11 + [vmem] * 7,
+        out_specs=[ANY, vmem, vmem, vmem, vmem],
         out_shape=[
             jax.ShapeDtypeStruct((3 * experts, share, hidden), low),
             jax.ShapeDtypeStruct((dense_panels, stripe, hidden), jnp.float32),
-            jax.ShapeDtypeStruct((3, length, width), low),
             jax.ShapeDtypeStruct((length, width), jnp.float32),
             jax.ShapeDtypeStruct((1, width), jnp.float32),
             jax.ShapeDtypeStruct((1, width), jnp.float32),
@@ -1656,20 +1780,20 @@
             pltpu.VMEM((2, share, hidden), low),
             pltpu.VMEM((2, 2, spots, width), low),
             pltpu.VMEM((2, 3, spots, hidden), low),
-            pltpu.VMEM((4, length, width), low),
-            pltpu.VMEM((dense_panels, length, hidden), low),
+            pltpu.VMEM((3, length, width), low),
+            pltpu.VMEM((8, length, hidden), low),
             pltpu.VMEM((width, HEADS * HD), low),
             pltpu.VMEM((4, length, width), low),
             pltpu.VMEM((length, HEADS * HD), low),
             pltpu.VMEM((2, length, HD), jnp.float32),
             pltpu.VMEM((length, width), jnp.float32),
             pltpu.VMEM((width, 2 * KVH * HD), low),
-            pltpu.VMEM((dense_panels, 4, stripe, hidden), low),
+            pltpu.VMEM((dense_panels, share, hidden), low),
             pltpu.VMEM((dense_panels, 3, stripe, hidden), low),
             pltpu.SemaphoreType.DMA((5,)),
             pltpu.SemaphoreType.DMA((9, SLOTS)),
             pltpu.SemaphoreType.DMA((2, dense_panels, 3)),
-            pltpu.SemaphoreType.DMA((12,)),
+            pltpu.SemaphoreType.DMA((6,)),
             pltpu.SemaphoreType.DMA((5, 5)),
             pltpu.SemaphoreType.REGULAR((3,)),
         ],
@@ -1679,15 +1803,12 @@
         name="scatter_grads",
     )(
         grad_parts,
-        routed_parts,
         *saved,
         dense_all,
-        normed_mixer,
+        shared_sum,
         cotangent,
         normed_attend,
         attended,
-        grad_shared_pre,
-        shared_act,
         residual,
         scale,
         gain,
@@ -1701,8 +1822,10 @@
 def muon_kernel(
     expert_ref,
     dense_ref,
+    routed_parts_ref,
     expert_out_ref,
     dense_out_ref,
+    routed_received_ref,
     dense_back,
     moments,
     units,
@@ -1841,6 +1964,17 @@
             pl.when(exists(slot, peers[turn][0]))(out_copy(slot, turn).start)
         pl.when(exists(slot, dp))(own_copy(slot).start)
 
+    length = routed_received_ref.shape[1]
+    routed_copies = [
+        remote(
+            routed_parts_ref.at[pl.ds(pl.multiple_of(device[1] * length, length), length), :],
+            routed_received_ref.at[turn],
+            line_sems.at[4, turn],
+            line_sems.at[5, turn],
+            device,
+        )
+        for turn, device in enumerate(others)
+    ]
     for copy in line_copies:
         copy.start()
     loads[0].wait()
@@ -1851,6 +1985,8 @@
         copy.wait()
     send_slot(1)
     send_slot(2)
+    for copy in routed_copies:
+        copy.start()
 
     @pl.loop(0, 3)
     def _(slot):
@@ -1907,20 +2043,23 @@
     for copy in line_back:
         copy.wait()
     own_back.wait()
-
-
-def muon(expert_units, dense_units):
+    for copy in routed_copies:
+        copy.wait()
+
+
+def muon(expert_units, dense_units, routed_parts):
     experts, share, columns = expert_units.shape
     panels, stripe, _ = dense_units.shape
     count = experts + panels // 4
     low = jnp.bfloat16
     return pl.pallas_call(
         muon_kernel,
-        in_specs=[ANY] * 2,
-        out_specs=[ANY] * 2,
+        in_specs=[ANY] * 3,
+        out_specs=[ANY] * 3,
         out_shape=[
             jax.ShapeDtypeStruct(expert_units.shape, low),
             jax.ShapeDtypeStruct(dense_units.shape, low),
+            jax.ShapeDtypeStruct((3, routed_parts.shape[0] // 4, routed_parts.shape[1]), low),
         ],
         scratch_shapes=[
             pltpu.VMEM((panels // 4, share, columns), low),
@@ -1930,7 +2069,7 @@
             pltpu.VMEM((columns, 8 * share), jnp.float32),
             pltpu.VMEM((columns, 8 * share), low),
             pltpu.VMEM((columns, columns), low),
-            pltpu.SemaphoreType.DMA((4, 3)),
+            pltpu.SemaphoreType.DMA((6, 3)),
             pltpu.SemaphoreType.DMA((3, 7)),
             pltpu.SemaphoreType.DMA((3,)),
             pltpu.SemaphoreType.DMA((3, 7)),
@@ -1941,7 +2080,7 @@
             collective_id=4, has_side_effects=True, vmem_limit_bytes=56 * MIB
         ),
         name="muon",
-    )(expert_units, dense_units)
+    )(expert_units, dense_units, routed_parts)
 
 
 def update_kernel(weights_ref, orthogonal_ref, new_ref):
@@ -2024,6 +2163,7 @@
             grad_shared,
             base_out,
             gains_all,
+            shared_sum,
         ) = front(
             jnp.concatenate(
                 [
@@ -2119,21 +2259,17 @@
         (
             expert_sum,
             dense_sum,
-            routed_received,
             grad_inputs,
             grad_gain_mixer,
             grad_gain_attend,
         ) = scatter_grads(
             grad_parts,
-            routed_parts,
             saved,
             dense_all,
-            normed_mixer,
+            shared_sum,
             cotangent,
             normed_attend,
             attended,
-            grad_shared_pre,
-            shared_act,
             residual,
             scale_mixer,
             gain_mixer[None, :],
@@ -2142,10 +2278,6 @@
             hidden_in,
             gain_attend[None, :],
         )
-        routed = lax.dynamic_slice_in_dim(
-            routed_parts, lax.axis_index("expert") * length, length, 0
-        ).astype(jnp.float32)
-        routed = routed + jnp.sum(routed_received.astype(jnp.float32), axis=0)
         expert_grad = expert_sum.reshape(expert_weights.shape).astype(jnp.float32)
         dense_grad = (
             jnp.concatenate([dense_sum[9:], dense_sum[6:9], dense_sum[:6]], 0)
@@ -2204,7 +2336,6 @@
             - inputs * scale_attend**3 * jnp.mean(grad_scaled_attend * inputs, axis=-1, keepdims=True)
         )
         grad_gain_attend = jnp.sum(grad_normed_attend * inputs * scale_attend, axis=0)
-    block_out = (base_out + routed.astype(jnp.float32)).astype(jnp.bfloat16)
     gain_grad = lax.psum_scatter(
         jnp.stack([grad_gain_attend, grad_gain_mixer], 0),
         ("dp", "expert"),
@@ -2223,7 +2354,11 @@
     ).reshape(stripe, dense_share * expert_size, FFE).transpose(1, 0, 2)
     expert_units = expert_moment.astype(jnp.bfloat16).reshape(-1, row_count, FFE)
     if direct:
-        orth_expert, orth_stripe = muon(expert_units, dense_padded)
+        orth_expert, orth_stripe, routed_received = muon(expert_units, dense_padded, routed_parts)
+        routed = lax.dynamic_slice_in_dim(
+            routed_parts, lax.axis_index("expert") * length, length, 0
+        ).astype(jnp.float32)
+        routed = routed + jnp.sum(routed_received.astype(jnp.float32), axis=0)
     else:
         dense_units = lax.all_to_all(
             dense_padded, "expert", split_axis=0, concat_axis=1, tiled=True
@@ -2256,6 +2391,7 @@
         .reshape(stripe, dense_columns)
         .astype(jnp.float32)
     )
+    block_out = (base_out + routed.astype(jnp.float32)).astype(jnp.bfloat16)
     keep_factor = 1.0 - LEARN_RATE * WEIGHT_DECAY
     dense_new = keep_factor * dense_weights - LEARN_RATE * orth_stripe
     expert_new = updated_weights(expert_weights, orth_expert)

time: 675 us -> 644 us (0.954)
  Pallas kernels: 614 us -> 588 us
    pallas_call x2, Pallas kernels: 339 us -> 291 us  [the longest x1 185 us: scatter_grads(): pl.pallas_call(scatter_kernel, in_specs=[ANY] * 11 + [vmem] * 7, out_spec...]
    pallas_call x1, Pallas kernels: 267 us -> 288 us  [front(): pl.pallas_call(front_kernel, in_specs=[ANY] * 3 + [vmem] * 2, out_specs=[...]
  transfers between devices with their start and end apart: 1 -> 1, of which waited for: 0 -> 0; matrix products, arithmetic and copies ran while one was open for 3% -> 3% of each run, Pallas kernels for 17% -> 18%
where the time goes in v2:
time: 644 us; the launch traced here: 637 us
  Pallas kernels  588 us (91%)
  other arithmetic  21.3 us (3%)
  between operations  14.5 us (2%)
  local copies, waits for them, and re-layouts  13.2 us (2%)
    pallas_call x1, Pallas kernels, front(): pl.pallas_call(front_kernel, in_specs=[ANY] * 3 + [vmem] * 2, out_specs=[...  288 us
    pallas_call x1, Pallas kernels, scatter_grads(): pl.pallas_call(scatter_kernel, in_specs=[ANY] * 11 + [vmem] * 7, out_spec...  185 us
    pallas_call x1, Pallas kernels, muon(): pl.pallas_call(muon_kernel, in_specs=[ANY] * 3, out_specs=[ANY] * 3, out_...  106 us
  transfers between devices with their start and end apart: 1, of which 0 were waited for; matrix products, arithmetic and copies ran while one was open for 3% of the time, Pallas kernels for 18%

profile of v2, /device:TPU:0, one launch (start us, length us, event | category | flops | bytes accessed | tf_op | source)
XLA Modules:
  0.0 636.5 jit_solution(6160485985641778368)
XLA Ops:
  7.3 1.4 convert.13
  8.9 0.6 pad.8.gates_ref
  9.5 1.0 concatenate.7.stripe_ref
  10.5 288.5 %front.1 = (bf16[1536,7296]{1,0:T(8,128)(2,1)}, bf16[18,1536,512]{2,1,0:T(8,128)(2,1)}, bf16[1024,1536]{1,0:T(8,128)(2,1)}, bf16[1024,1536]{1,0:T(8,128)(2,1)}, ...) custom-call(bf16[48,7296]{1,0:T(8,128)(2,1)} %concatenate.7.stripe_r, ...), custom_call_target="tpu_custom_call" | custom-call | tf_op jit(solution)/shard_map/front/pallas_call | solution.py:1219
  299.0 1.5 fusion.4
  300.5 184.6 %scatter_grads.1 = (bf16[18,192,512]{2,1,0:T(8,128)(2,1)}, f32[14,48,512]{2,1,0:T(8,128)}, f32[256,1536]{1,0:T(8,128)}, f32[1,1536]{1,0:T(1,128)}, f32[1,1536]{1,0:T(1,128)}) custom-call(bf16[1024,1536]{1,0:T(8,128)(2,1)} %get-tuple-element.39.grad_parts_ref, bf16[6,320,1536]{2,1,0:T(8,128)(2,1)} %get-tuple-element.40.received_ref, ...), custom_call_target="tpu_custom_call" | custom-call | tf_op jit(solution)/shard_map/scatter_grads/pallas_call | solution.py:1762
  485.1 0.8 pad_maximum_fusion
  485.9 1.2 copy.36
  487.5 1.7 copy-done.6
  489.2 1.3 fusion.2
  490.5 1.0 copy.42
  491.5 0.5 copy-done.2
  492.0 11.8 %fusion.3 = (bf16[6,3,192,512]{3,2,1,0:T(8,128)(2,1)}, f32[6,3,192,512]{3,2,1,0:T(8,128)}, f32[6,3,192,512]{3,2,1,0:T(8,128)}) fusion(f32[6,3,192,512]{3,2,1,0:T(8,128)} %param.18, bf16[6,3,192,512]{3,2,1,0:T(8,128)(2,1)S(1)} %bitcast.32), kind=kLoop, calls=%fused_computation.17 | loop fusion | flops 7077888 | bytes 28311552 | tf_op jit(solution)/shard_map/convert_element_type | solution.py:2355
  503.8 106.3 %muon.1 = (bf16[18,192,512]{2,1,0:T(8,128)(2,1)}, bf16[16,48,512]{2,1,0:T(8,128)(2,1)}, bf16[3,256,1536]{2,1,0:T(8,128)(2,1)}) custom-call(bf16[18,192,512]{2,1,0:T(8,128)(2,1)} %bitcast.27, bf16[16,48,512]{2,1,0:T(8,128)(2,1)} %bitcast.33, bf16[1024,1536]{1,0:T(8,128)(2,1)} %get-tuple-element.38.routed_parts_ref), custom_call_target="tpu_custom_call" | custom-call | tf_op jit(solution)/shard_map/muon/pallas_call | solution.py:2055
  610.0 1.3 multiply_bitcast_fusion
  611.5 1.2 copy-done
  612.7 1.2 multiply_subtract_fusion
  613.9 0.9 copy-done.3
  615.2 1.0 copy-done.4
  616.3 2.4 add_convert_fusion
  618.7 8.3 %update.1 = f32[18,192,512]{2,1,0:T(8,128)} custom-call(f32[18,192,512]{2,1,0:T(8,128)} %bitcast.26, bf16[18,192,512]{2,1,0:T(8,128)(2,1)} %get-tuple-element.59.orthogonal_ref), custom_call_target="tpu_custom_call" | custom-call | tf_op jit(solution)/shard_map/update/pallas_call | solution.py:2097
  626.9 0.8 copy.37
  627.7 0.6 multiply_subtract_fusion.1
  628.3 1.1 copy.44
  (41 shorter events, 1.2 us)
Async XLA Ops:
  7.2 1.6 copy-start.11
  7.2 1.7 copy-start.9
  7.2 1.7 copy-start.8
  7.2 619.7 %reduce-scatter.4.cloned.1.call-start = ((), (), s32[]{:S(2)}) async-start(), calls=%async_computation.1 | async-start | bytes 811008
  485.0 2.1 copy-start.7
  487.4 1.8 copy-start.6
  487.5 3.0 copy-start.1
  489.2 2.8 copy-start.2
  611.3 1.4 copy-start
  612.7 2.2 copy-start.3
  614.9 1.4 copy-start.4
  618.6 9.1 %copy-start.12 = (f32[2,48]{1,0:T(2,128)S(1)}, f32[2,48]{1,0:T(2,128)}, u32[]{:S(2)}) copy-start(f32[2,48]{1,0:T(2,128)} %param.21) | copy-start | bytes 1156
  618.6 9.1 %copy-start.13 = (f32[2,48]{1,0:T(2,128)S(1)}, f32[2,48]{1,0:T(2,128)}, u32[]{:S(2)}) copy-start(f32[2,48]{1,0:T(2,128)} %param.20) | copy-start | bytes 1156
  618.7 9.7 %copy-start.5 = (f32[256,1536]{1,0:T(8,128)S(1)}, f32[256,1536]{1,0:T(8,128)}, u32[]{:S(2)}) copy-start(f32[256,1536]{1,0:T(8,128)} %get-tuple-element.85) | copy-start | bytes 4718596
  627.7 1.7 copy-start.10
Sparse Core Ops, SparseCore 0:
  487.2 131.3 reduce-scatter.3

commit v3 on v2

--- a/solution.py
+++ b/solution.py
@@ -1288,11 +1288,13 @@
     projected_ref,
     hidden_ref,
     gain_attend_ref,
+    momentum_ref,
     expert_sum_ref,
-    stripes_ref,
+    dense_grad_ref,
+    dense_moment_ref,
+    dense_units_ref,
     grad_input_ref,
     grad_gain_ref,
-    grad_gain_attend_ref,
     ring,
     pair_sum,
     corner_x,
@@ -1587,7 +1589,9 @@
             )
             grad_residual_ref[rows, :] = grad_residual
             left[1, rows, :] = grad_residual.astype(jnp.bfloat16)
-            grad_gain_ref[...] += jnp.sum(grad_normed * residual * scale, axis=0, keepdims=True)
+            grad_gain_ref[1:2, :] += jnp.sum(
+                grad_normed * residual * scale, axis=0, keepdims=True
+            )
 
     def attended_backward():
         grad_attended[...] = matmul(left[1], out_weights[...]).astype(jnp.bfloat16)
@@ -1609,7 +1613,6 @@
             )
 
     def input_backward():
-        grad_gain_attend_ref[...] = jnp.zeros_like(grad_gain_attend_ref)
         rows_step = 32
 
         @pl.loop(0, length // rows_step)
@@ -1624,7 +1627,7 @@
                 + scale * grad_scaled
                 - values * (scale * scale * scale) * mean
             )
-            grad_gain_attend_ref[...] += jnp.sum(
+            grad_gain_ref[0:1, :] += jnp.sum(
                 grad_normed * values * scale, axis=0, keepdims=True
             )
 
@@ -1725,14 +1728,23 @@
     for panel in (expert_panels - 2, expert_panels - 1):
         staged_copy(panel).wait()
 
-    @pl.loop(0, dense_panels)
-    def _(panel):
+    for panel in range(dense_panels):
         for copy in line_copies(panel):
             copy.wait()
-        stripes_ref[panel] = total(
+        place = panel + 8 if panel < 6 else panel - 1 if panel < 9 else panel - 9
+        spot = slice(place * hidden, (place + 1) * hidden)
+        grad = total(
             line_out[panel, pl.ds(pl.multiple_of(z * stripe, stripe), stripe), :],
-            line_in[panel, 0], line_in[panel, 1], line_in[panel, 2]
-        )
+            line_in[panel, 0],
+            line_in[panel, 1],
+            line_in[panel, 2],
+        )
+        moment = MOMENTUM_DECAY * momentum_ref[:, spot] + grad
+        dense_grad_ref[:, spot] = grad
+        dense_moment_ref[:, spot] = moment
+        dense_units_ref[place] = moment.astype(jnp.bfloat16)
+    for panel in range(dense_panels, dense_units_ref.shape[0]):
+        dense_units_ref[panel] = jnp.zeros_like(dense_units_ref[panel])
 
 
 def scatter_grads(
@@ -1750,6 +1762,7 @@
     projected,
     hidden_in,
     gain_attend,
+    dense_momentum,
 ):
     experts, spots, width = saved[0].shape
     hidden = saved[2].shape[-1]
@@ -1761,14 +1774,15 @@
     vmem = pl.BlockSpec(memory_space=pltpu.VMEM)
     return pl.pallas_call(
         scatter_kernel,
-        in_specs=[ANY] * 11 + [vmem] * 7,
-        out_specs=[ANY, vmem, vmem, vmem, vmem],
+        in_specs=[ANY] * 11 + [vmem] * 8,
+        out_specs=[ANY] + [vmem] * 5,
         out_shape=[
             jax.ShapeDtypeStruct((3 * experts, share, hidden), low),
-            jax.ShapeDtypeStruct((dense_panels, stripe, hidden), jnp.float32),
+            jax.ShapeDtypeStruct(dense_momentum.shape, jnp.float32),
+            jax.ShapeDtypeStruct(dense_momentum.shape, jnp.float32),
+            jax.ShapeDtypeStruct((16, stripe, hidden), low),
             jax.ShapeDtypeStruct((length, width), jnp.float32),
-            jax.ShapeDtypeStruct((1, width), jnp.float32),
-            jax.ShapeDtypeStruct((1, width), jnp.float32),
+            jax.ShapeDtypeStruct((2, width), jnp.float32),
         ],
         scratch_shapes=[
             pltpu.VMEM((2, 4, 2, share, hidden), low),
@@ -1816,6 +1830,7 @@
         projected,
         hidden_in,
         gain_attend,
+        dense_momentum,
     )
 
 
@@ -1823,9 +1838,13 @@
     expert_ref,
     dense_ref,
     routed_parts_ref,
+    base_ref,
+    dense_weights_ref,
     expert_out_ref,
+    block_out_ref,
+    dense_new_ref,
     dense_out_ref,
-    routed_received_ref,
+    routed,
     dense_back,
     moments,
     units,
@@ -1964,11 +1983,17 @@
             pl.when(exists(slot, peers[turn][0]))(out_copy(slot, turn).start)
         pl.when(exists(slot, dp))(own_copy(slot).start)
 
-    length = routed_received_ref.shape[1]
+    length = base_ref.shape[0]
+    own_routed = pltpu.make_async_copy(
+        routed_parts_ref.at[pl.ds(pl.multiple_of(z * length, length), length), :],
+        routed.at[3],
+        load_sems.at[6],
+    )
+    own_routed.start()
     routed_copies = [
         remote(
             routed_parts_ref.at[pl.ds(pl.multiple_of(device[1] * length, length), length), :],
-            routed_received_ref.at[turn],
+            routed.at[turn],
             line_sems.at[4, turn],
             line_sems.at[5, turn],
             device,
@@ -2030,6 +2055,19 @@
         copy.start()
     own_back.start()
     wait_back(0)
+    own_routed.wait()
+    for copy in routed_copies:
+        copy.wait()
+    rows_step = 32
+
+    @pl.loop(0, length // rows_step)
+    def _(index):
+        part = pl.ds(index * rows_step, rows_step)
+        total = base_ref[part, :]
+        for source in (3, 0, 1, 2):
+            total = total + routed[source, part, :].astype(jnp.float32)
+        block_out_ref[part, :] = total.astype(jnp.bfloat16)
+
     wait_back(2)
     for slot in range(3):
         for turn in range(7):
@@ -2043,25 +2081,33 @@
     for copy in line_back:
         copy.wait()
     own_back.wait()
-    for copy in routed_copies:
-        copy.wait()
-
-
-def muon(expert_units, dense_units, routed_parts):
+    keep_factor = 1.0 - LEARN_RATE * WEIGHT_DECAY
+    columns = current.shape[0]
+    for panel in range(dense_new_ref.shape[1] // columns):
+        spot = slice(panel * columns, (panel + 1) * columns)
+        dense_new_ref[:, spot] = keep_factor * dense_weights_ref[:, spot] - LEARN_RATE * (
+            dense_out_ref[panel].astype(jnp.float32)
+        )
+
+
+def muon(expert_units, dense_units, routed_parts, base_out, dense_weights):
     experts, share, columns = expert_units.shape
     panels, stripe, _ = dense_units.shape
     count = experts + panels // 4
     low = jnp.bfloat16
+    vmem = pl.BlockSpec(memory_space=pltpu.VMEM)
     return pl.pallas_call(
         muon_kernel,
-        in_specs=[ANY] * 3,
-        out_specs=[ANY] * 3,
+        in_specs=[ANY] * 3 + [vmem] * 2,
+        out_specs=[ANY] + [vmem] * 2,
         out_shape=[
             jax.ShapeDtypeStruct(expert_units.shape, low),
-            jax.ShapeDtypeStruct(dense_units.shape, low),
-            jax.ShapeDtypeStruct((3, routed_parts.shape[0] // 4, routed_parts.shape[1]), low),
+            jax.ShapeDtypeStruct(base_out.shape, low),
+            jax.ShapeDtypeStruct(dense_weights.shape, jnp.float32),
         ],
         scratch_shapes=[
+            pltpu.VMEM(dense_units.shape, low),
+            pltpu.VMEM((4, *base_out.shape), low),
             pltpu.VMEM((panels // 4, share, columns), low),
             pltpu.VMEM((count, share, columns), low),
             pltpu.VMEM((3, 8 * share, columns), low),
@@ -2074,13 +2120,38 @@
             pltpu.SemaphoreType.DMA((3,)),
             pltpu.SemaphoreType.DMA((3, 7)),
             pltpu.SemaphoreType.DMA((3, 8)),
-            pltpu.SemaphoreType.DMA((6,)),
+            pltpu.SemaphoreType.DMA((7,)),
         ],
         compiler_params=pltpu.CompilerParams(
             collective_id=4, has_side_effects=True, vmem_limit_bytes=56 * MIB
         ),
         name="muon",
-    )(expert_units, dense_units, routed_parts)
+    )(expert_units, dense_units, routed_parts, base_out, dense_weights)
+
+
+def moments_kernel(momentum_ref, sum_ref, grad_ref, moment_ref, units_ref):
+    grad = sum_ref[...].astype(jnp.float32)
+    moment = MOMENTUM_DECAY * momentum_ref[...] + grad
+    grad_ref[...] = grad
+    moment_ref[...] = moment
+    units_ref[...] = moment.astype(jnp.bfloat16)
+
+
+def moments(momentum, grad_sum):
+    panels, rows, columns = grad_sum.shape
+    group = 3
+    block = pl.BlockSpec((group, rows, columns), lambda index: (index, 0, 0))
+    full = jax.ShapeDtypeStruct(grad_sum.shape, jnp.float32)
+    grad, moment, units = pl.pallas_call(
+        moments_kernel,
+        grid=(panels // group,),
+        in_specs=[block] * 2,
+        out_specs=[block] * 3,
+        out_shape=[full, full, jax.ShapeDtypeStruct(grad_sum.shape, jnp.bfloat16)],
+        compiler_params=pltpu.CompilerParams(vmem_limit_bytes=32 * MIB),
+        name="moments",
+    )(momentum.reshape(grad_sum.shape), grad_sum)
+    return grad.reshape(momentum.shape), moment.reshape(momentum.shape), units
 
 
 def update_kernel(weights_ref, orthogonal_ref, new_ref):
@@ -2092,7 +2163,7 @@
 
 def updated_weights(weights, orthogonal):
     panels, rows, columns = orthogonal.shape
-    group = 3
+    group = 6
     block = pl.BlockSpec((group, rows, columns), lambda index: (index, 0, 0))
     return pl.pallas_call(
         update_kernel,
@@ -2100,6 +2171,7 @@
         in_specs=[block, block],
         out_specs=block,
         out_shape=jax.ShapeDtypeStruct(orthogonal.shape, jnp.float32),
+        compiler_params=pltpu.CompilerParams(vmem_limit_bytes=32 * MIB),
         name="update",
     )(weights.reshape(orthogonal.shape), orthogonal).reshape(weights.shape)
 
@@ -2258,10 +2330,11 @@
     if direct:
         (
             expert_sum,
-            dense_sum,
+            dense_grad,
+            dense_moment,
+            dense_units,
             grad_inputs,
-            grad_gain_mixer,
-            grad_gain_attend,
+            grad_gains,
         ) = scatter_grads(
             grad_parts,
             saved,
@@ -2277,14 +2350,12 @@
             projected,
             hidden_in,
             gain_attend[None, :],
-        )
-        expert_grad = expert_sum.reshape(expert_weights.shape).astype(jnp.float32)
-        dense_grad = (
-            jnp.concatenate([dense_sum[9:], dense_sum[6:9], dense_sum[:6]], 0)
-            .transpose(1, 0, 2)
-            .reshape(dense_weights.shape)
-        )
-        grad_gain_mixer, grad_gain_attend = grad_gain_mixer[0], grad_gain_attend[0]
+            dense_momentum,
+        )
+        expert_grad, expert_moment, expert_units = moments(expert_momentum, expert_sum)
+        orth_expert, block_out, dense_new = muon(
+            expert_units, dense_units, routed_parts, base_out, dense_weights
+        )
     else:
         routed = lax.psum_scatter(routed_parts, "expert", scatter_dimension=0, tiled=True)
         grad_routed = lax.psum_scatter(grad_parts, "expert", scatter_dimension=0, tiled=True)
@@ -2336,30 +2407,19 @@
             - inputs * scale_attend**3 * jnp.mean(grad_scaled_attend * inputs, axis=-1, keepdims=True)
         )
         grad_gain_attend = jnp.sum(grad_normed_attend * inputs * scale_attend, axis=0)
-    gain_grad = lax.psum_scatter(
-        jnp.stack([grad_gain_attend, grad_gain_mixer], 0),
-        ("dp", "expert"),
-        scatter_dimension=1,
-        tiled=True,
-    )
-    dense_moment = MOMENTUM_DECAY * dense_momentum + dense_grad
-    expert_moment = MOMENTUM_DECAY * expert_momentum + expert_grad
-    stripe, dense_columns = dense_weights.shape
-    row_count = stripe * expert_size
-    dense_total = dense_columns // FFE
-    dense_share = -(-dense_total // expert_size)
-    dense_padded = jnp.pad(
-        dense_moment.astype(jnp.bfloat16),
-        ((0, 0), (0, dense_share * expert_size * FFE - dense_columns)),
-    ).reshape(stripe, dense_share * expert_size, FFE).transpose(1, 0, 2)
-    expert_units = expert_moment.astype(jnp.bfloat16).reshape(-1, row_count, FFE)
-    if direct:
-        orth_expert, orth_stripe, routed_received = muon(expert_units, dense_padded, routed_parts)
-        routed = lax.dynamic_slice_in_dim(
-            routed_parts, lax.axis_index("expert") * length, length, 0
-        ).astype(jnp.float32)
-        routed = routed + jnp.sum(routed_received.astype(jnp.float32), axis=0)
-    else:
+        block_out = (base_out + routed.astype(jnp.float32)).astype(jnp.bfloat16)
+        grad_gains = jnp.stack([grad_gain_attend, grad_gain_mixer], 0)
+        dense_moment = MOMENTUM_DECAY * dense_momentum + dense_grad
+        expert_moment = MOMENTUM_DECAY * expert_momentum + expert_grad
+        stripe, dense_columns = dense_weights.shape
+        row_count = stripe * expert_size
+        dense_total = dense_columns // FFE
+        dense_share = -(-dense_total // expert_size)
+        dense_padded = jnp.pad(
+            dense_moment.astype(jnp.bfloat16),
+            ((0, 0), (0, dense_share * expert_size * FFE - dense_columns)),
+        ).reshape(stripe, dense_share * expert_size, FFE).transpose(1, 0, 2)
+        expert_units = expert_moment.astype(jnp.bfloat16).reshape(-1, row_count, FFE)
         dense_units = lax.all_to_all(
             dense_padded, "expert", split_axis=0, concat_axis=1, tiled=True
         )
@@ -2385,15 +2445,20 @@
             concat_axis=0,
             tiled=True,
         )
-    orth_stripe = (
-        orth_stripe[:dense_total]
-        .transpose(1, 0, 2)
-        .reshape(stripe, dense_columns)
-        .astype(jnp.float32)
+        orth_stripe = (
+            orth_stripe[:dense_total]
+            .transpose(1, 0, 2)
+            .reshape(stripe, dense_columns)
+            .astype(jnp.float32)
+        )
+        keep_factor = 1.0 - LEARN_RATE * WEIGHT_DECAY
+        dense_new = keep_factor * dense_weights - LEARN_RATE * orth_stripe
+    gain_grad = lax.psum_scatter(
+        grad_gains,
+        ("dp", "expert"),
+        scatter_dimension=1,
+        tiled=True,
     )
-    block_out = (base_out + routed.astype(jnp.float32)).astype(jnp.bfloat16)
-    keep_factor = 1.0 - LEARN_RATE * WEIGHT_DECAY
-    dense_new = keep_factor * dense_weights - LEARN_RATE * orth_stripe
     expert_new = updated_weights(expert_weights, orth_expert)
     first_new = FIRST_DECAY * gain_first + (1.0 - FIRST_DECAY) * gain_grad
     second_new = SECOND_DECAY * gain_second + (1.0 - SECOND_DECAY) * gain_grad * gain_grad

time: 644 us -> 642 us (level)
  other arithmetic: 21.3 us -> 2.02 us
  local copies, waits for them, and re-layouts: 13.2 us -> 23.7 us
    convert_element_type x3 -> x0, other arithmetic: 15.4 us -> none  [the longest x1 11.8 us: on_device(): expert_moment.astype(jnp.bfloat16).reshape(-1, row_count, FFE)]
    unnamed x31 -> x39, local copies, waits for them, and re-layouts: 8.58 us -> 20.4 us
    pallas_call x2 -> x3, Pallas kernels: 291 us -> 301 us  [the longest x1 186 us: scatter_grads(): pl.pallas_call(scatter_kernel, in_specs=[ANY] * 11 + [vmem] * 8, out_spec...]
  transfers between devices with their start and end apart: 1 -> 1, of which waited for: 0 -> 1; matrix products, arithmetic and copies ran while one was open for 3% -> 0% of each run, Pallas kernels for 18% -> 19%
where the time goes in v3:
time: 642 us; the launch traced here: 635 us
  Pallas kernels  593 us (92%)
  local copies, waits for them, and re-layouts  23.7 us (4%)
  between operations  14.4 us (2%)
    pallas_call x1, Pallas kernels, front(): pl.pallas_call(front_kernel, in_specs=[ANY] * 3 + [vmem] * 2, out_specs=[...  288 us
    pallas_call x1, Pallas kernels, scatter_grads(): pl.pallas_call(scatter_kernel, in_specs=[ANY] * 11 + [vmem] * 8, out_spec...  186 us
    pallas_call x1, Pallas kernels, muon(): pl.pallas_call(muon_kernel, in_specs=[ANY] * 3 + [vmem] * 2, out_specs=[A...  110 us
    unnamed x39, local copies, waits for them, and re-layouts  20.4 us
  transfers between devices with their start and end apart: 1, of which 1 were waited for; matrix products, arithmetic and copies ran while one was open for 0% of the time, Pallas kernels for 19%

profile of v3, /device:TPU:0, one launch (start us, length us, event | category | flops | bytes accessed | tf_op | source)
XLA Modules:
  0.0 635.1 jit_solution(9484771880376595917)
XLA Ops:
  7.3 1.4 convert.12
  8.9 0.6 pad.4.gates_ref
  9.5 1.0 concatenate.4.stripe_ref
  10.5 288.5 %front.1 = (bf16[1536,7296]{1,0:T(8,128)(2,1)}, bf16[18,1536,512]{2,1,0:T(8,128)(2,1)}, bf16[1024,1536]{1,0:T(8,128)(2,1)}, bf16[1024,1536]{1,0:T(8,128)(2,1)}, ...) custom-call(bf16[48,7296]{1,0:T(8,128)(2,1)} %concatenate.4.stripe_r, ...), custom_call_target="tpu_custom_call" | custom-call | tf_op jit(solution)/shard_map/front/pallas_call | solution.py:1219
  299.0 1.5 fusion.2
  300.5 185.8 %scatter_grads.1 = (bf16[18,192,512]{2,1,0:T(8,128)(2,1)}, f32[48,7168]{1,0:T(8,128)}, f32[48,7168]{1,0:T(8,128)}, bf16[16,48,512]{2,1,0:T(8,128)(2,1)}, f32[256,1536]{1,0:T(8,128)}, /*index=5*/f32[2,1536]{1,0:T(2,128)}) custom-call(bf16[1024,1536]{1,0:T(8,128)(2,1)} %get-tuple-element.41.grad_parts_ref, ...), custom_call_target="tpu_custom_call" | custom-call | tf_op jit(solution)/shard_map/scatter_grads/pallas_call | solution.py:1775
  486.3 2.0 copy.27
  488.3 3.0 copy-done
  491.4 2.0 copy-done.2
  493.4 6.1 moments.1
  499.4 1.8 copy-done.1
  501.2 109.6 %muon.1 = (bf16[18,192,512]{2,1,0:T(8,128)(2,1)}, bf16[256,1536]{1,0:T(8,128)(2,1)}, f32[48,7168]{1,0:T(8,128)}) custom-call(bf16[18,192,512]{2,1,0:T(8,128)(2,1)} %copy-done.1, bf16[16,48,512]{2,1,0:T(8,128)(2,1)} %get-tuple-element.58.dense_ref, bf16[1024,1536]{1,0:T(8,128)(2,1)} %get-tuple-element.59.routed_parts_ref, ...), custom_call_target="tpu_custom_call" | custom-call | tf_op jit(solution)/shard_map/muon/pallas_call | solution.py:2099
  610.9 2.0 copy-done.3
  612.9 3.5 update.1
  616.4 1.6 reduce-scatter.4.cloned.1.call-done
  617.9 0.8 copy.28
  619.3 2.1 copy.34
  621.4 1.1 copy.35
  622.6 0.8 copy-done.6
  623.3 1.1 copy.36
  624.4 0.8 copy-done.5
  625.2 1.1 copy.37
  626.2 0.8 copy-done.7
  627.0 1.1 copy.38
  (36 shorter events, 0.9 us)
Async XLA Ops:
  7.2 1.6 copy-start.11
  7.2 1.7 copy-start.8
  7.2 1.7 copy-start.9
  7.2 610.7 %reduce-scatter.4.cloned.1.call-start = ((), (), s32[]{:S(2)}) async-start(), calls=%async_computation.1 | async-start | bytes 811008
  486.3 124.6 %slice-start = ((s8[7077888]{0:T(1024)(128)(4,1)}), s8[2883584]{0:T(1024)(128)(4,1)S(1)}, s32[]{:S(2)}) async-start(s8[7077888]{0:T(1024)(128)(4,1)} %bitcast.11), calls=%async_computation.2 | async-start | bytes 5767168
  488.3 3.0 copy-start
  491.3 2.0 copy-start.2
  493.4 117.5 %slice-start.1 = ((s8[7077888]{0:T(1024)(128)(4,1)}), s8[4194304]{0:T(1024)(128)(4,1)S(1)}, s32[]{:S(2)}) async-start(s8[7077888]{0:T(1024)(128)(4,1)} %bitcast.11), calls=%async_computation.3 | async-start | bytes 8388608
  499.4 1.8 copy-start.1
  610.9 2.0 copy-start.3
  612.9 5.9 copy-start.12
  612.9 5.9 copy-start.13
  616.4 5.0 copy-start.4
  618.8 3.8 copy-start.10
  621.4 1.9 copy-start.6
  623.3 1.8 copy-start.5
  625.2 1.8 copy-start.7
Sparse Core Ops, SparseCore 0:
  488.5 129.4 reduce-scatter.3

commit v4 on v3

--- a/solution.py
+++ b/solution.py
@@ -520,18 +520,24 @@
     act_ref,
     grad_gate_ref,
     grad_up_ref,
+    normed_attend_out,
+    projected_out,
+    attended_out,
+    residual_out,
+    grad_shared_out,
+    base_out,
+    shared_sum_ref,
+    scale_ref,
+    gains_ref,
     normed_attend_ref,
     projected_ref,
     attended_ref,
     residual_ref,
-    scale_ref,
+    grad_shared_ref,
+    base_ref,
     normed_mixer_ref,
     shared_act_ref,
     grad_shared_pre_ref,
-    grad_shared_ref,
-    base_ref,
-    gains_ref,
-    shared_sum_ref,
     matrices,
     extra,
     all_gates,
@@ -553,6 +559,7 @@
     load_sems,
     expert_sems,
     shared_sems,
+    keep_sems,
 ):
     links = Links(semaphores)
     stripe, columns = stripe_ref.shape
@@ -862,6 +869,20 @@
             grad_shared_ref[...] += grad
             base_ref[...] += out
 
+    kept = [
+        pltpu.make_async_copy(source, target, keep_sems.at[index])
+        for index, (source, target) in enumerate(
+            (
+                (normed_attend_ref, normed_attend_out),
+                (projected_ref, projected_out),
+                (attended_ref, attended_out),
+                (residual_ref, residual_out),
+                (grad_shared_ref, grad_shared_out),
+                (base_ref, base_out),
+            )
+        )
+    ]
+
     def place_slots():
         local_copies[1].wait()
         before = (
@@ -994,6 +1015,8 @@
     shared_back(0)
     exchange(3)
     shared_back(1)
+    for copy in kept:
+        copy.start()
     exchange(4)
     shared_fill(0)
     tokens.relay()
@@ -1201,7 +1224,7 @@
         shared_store(panel).start()
     for panel in (shared_panels - 2, shared_panels - 1):
         shared_store(panel).wait()
-    for copy in out_copies:
+    for copy in (*kept, *out_copies):
         copy.wait()
 
     links.finish()
@@ -1219,7 +1242,7 @@
     return pl.pallas_call(
         front_kernel,
         in_specs=[ANY] * 3 + [vmem] * 2,
-        out_specs=[ANY] * 11 + [vmem] * 11 + [ANY],
+        out_specs=[ANY] * 18 + [vmem] * 2,
         out_shape=[
             jax.ShapeDtypeStruct((stripe_rows * 32, columns), low),
             jax.ShapeDtypeStruct((panels, rows * 8, hidden), low),
@@ -1230,16 +1253,22 @@
             jax.ShapeDtypeStruct((length, query_width + 2 * KVH * HD), low),
             jax.ShapeDtypeStruct((length, query_width), low),
             jax.ShapeDtypeStruct((length, width), full),
-            jax.ShapeDtypeStruct((length, 1), full),
-            jax.ShapeDtypeStruct((length, width), low),
-            jax.ShapeDtypeStruct((length, FFS), low),
-            jax.ShapeDtypeStruct((length, 2 * FFS), low),
             jax.ShapeDtypeStruct((length, width), full),
             jax.ShapeDtypeStruct((length, width), full),
+            jax.ShapeDtypeStruct((6, rows, hidden), low),
+            jax.ShapeDtypeStruct((length, 1), full),
             jax.ShapeDtypeStruct((8, width), full),
-            jax.ShapeDtypeStruct((6, rows, hidden), low),
         ],
         scratch_shapes=[
+            pltpu.VMEM((length, width), low),
+            pltpu.VMEM((length, query_width + 2 * KVH * HD), low),
+            pltpu.VMEM((length, query_width), low),
+            pltpu.VMEM((length, width), full),
+            pltpu.VMEM((length, width), full),
+            pltpu.VMEM((length, width), full),
+            pltpu.VMEM((length, width), low),
+            pltpu.VMEM((length, FFS), low),
+            pltpu.VMEM((length, 2 * FFS), low),
             pltpu.VMEM((14, width, hidden), low),
             pltpu.VMEM((width, 128), low),
             pltpu.VMEM((4, 4, 8, length), full),
@@ -1261,6 +1290,7 @@
             pltpu.SemaphoreType.DMA((15,)),
             pltpu.SemaphoreType.DMA((8, 6)),
             pltpu.SemaphoreType.DMA((2, 5, 6)),
+            pltpu.SemaphoreType.DMA((6,)),
         ],
         compiler_params=pltpu.CompilerParams(
             collective_id=1, has_side_effects=True, vmem_limit_bytes=63 * MIB
@@ -1281,20 +1311,20 @@
     cotangent_ref,
     normed_attend_ref,
     attended_ref,
+    residual_in,
+    grad_shared_in,
+    projected_in,
+    hidden_in,
+    scale_ref,
+    gains_ref,
+    expert_sum_ref,
+    stripes_ref,
+    grad_input_ref,
+    grad_gain_ref,
     residual_ref,
-    scale_ref,
-    gain_ref,
     grad_shared_ref,
     projected_ref,
     hidden_ref,
-    gain_attend_ref,
-    momentum_ref,
-    expert_sum_ref,
-    dense_grad_ref,
-    dense_moment_ref,
-    dense_units_ref,
-    grad_input_ref,
-    grad_gain_ref,
     ring,
     pair_sum,
     corner_x,
@@ -1397,6 +1427,10 @@
         (normed_attend_ref, left.at[2]),
         *[(columns(attended_ref, panel), right.at[panel]) for panel in range(3)],
         (shared_sum_ref, line_out.at[pl.ds(0, shared_panels)]),
+        (residual_in, residual_ref),
+        (grad_shared_in, grad_shared_ref),
+        (projected_in, projected_ref),
+        (hidden_in, hidden_ref),
         (dense_ref.at[:, pl.ds(query_width + 2 * kv_width, query_width)], out_weights),
         (dense_ref.at[:, pl.ds(query_width, 2 * kv_width)], key_weights),
         (
@@ -1580,7 +1614,7 @@
                 + grad_shared_ref[rows, :]
             )
             residual, scale = residual_ref[rows, :], scale_ref[rows, :]
-            grad_scaled = grad_normed * gain_ref[...]
+            grad_scaled = grad_normed * gains_ref[1:2, :]
             mean = jnp.mean(grad_scaled * residual, axis=-1, keepdims=True)
             grad_residual = (
                 left[0, rows, :].astype(jnp.float32)
@@ -1620,7 +1654,7 @@
             rows = pl.ds(index * rows_step, rows_step)
             values, grad_normed = hidden_ref[rows, :].astype(jnp.float32), grad_input_ref[rows, :]
             scale = lax.rsqrt(jnp.mean(values * values, axis=-1, keepdims=True) + 1e-06)
-            grad_scaled = grad_normed * gain_attend_ref[...]
+            grad_scaled = grad_normed * gains_ref[0:1, :]
             mean = jnp.mean(grad_scaled * values, axis=-1, keepdims=True)
             grad_input_ref[rows, :] = (
                 grad_residual_ref[rows, :]
@@ -1732,19 +1766,12 @@
         for copy in line_copies(panel):
             copy.wait()
         place = panel + 8 if panel < 6 else panel - 1 if panel < 9 else panel - 9
-        spot = slice(place * hidden, (place + 1) * hidden)
-        grad = total(
+        stripes_ref[place] = total(
             line_out[panel, pl.ds(pl.multiple_of(z * stripe, stripe), stripe), :],
             line_in[panel, 0],
             line_in[panel, 1],
             line_in[panel, 2],
         )
-        moment = MOMENTUM_DECAY * momentum_ref[:, spot] + grad
-        dense_grad_ref[:, spot] = grad
-        dense_moment_ref[:, spot] = moment
-        dense_units_ref[place] = moment.astype(jnp.bfloat16)
-    for panel in range(dense_panels, dense_units_ref.shape[0]):
-        dense_units_ref[panel] = jnp.zeros_like(dense_units_ref[panel])
 
 
 def scatter_grads(
@@ -1756,13 +1783,11 @@
     normed_attend,
     attended,
     residual,
-    scale,
-    gain,
     grad_shared,
     projected,
     hidden_in,
-    gain_attend,
-    dense_momentum,
+    scale,
+    gains,
 ):
     experts, spots, width = saved[0].shape
     hidden = saved[2].shape[-1]
@@ -1774,17 +1799,19 @@
     vmem = pl.BlockSpec(memory_space=pltpu.VMEM)
     return pl.pallas_call(
         scatter_kernel,
-        in_specs=[ANY] * 11 + [vmem] * 8,
-        out_specs=[ANY] + [vmem] * 5,
+        in_specs=[ANY] * 15 + [vmem] * 2,
+        out_specs=[ANY] + [vmem] * 3,
         out_shape=[
             jax.ShapeDtypeStruct((3 * experts, share, hidden), low),
-            jax.ShapeDtypeStruct(dense_momentum.shape, jnp.float32),
-            jax.ShapeDtypeStruct(dense_momentum.shape, jnp.float32),
-            jax.ShapeDtypeStruct((16, stripe, hidden), low),
+            jax.ShapeDtypeStruct((dense_panels, stripe, hidden), jnp.float32),
             jax.ShapeDtypeStruct((length, width), jnp.float32),
             jax.ShapeDtypeStruct((2, width), jnp.float32),
         ],
         scratch_shapes=[
+            pltpu.VMEM((length, width), jnp.float32),
+            pltpu.VMEM((length, width), jnp.float32),
+            pltpu.VMEM(projected.shape, low),
+            pltpu.VMEM((length, width), low),
             pltpu.VMEM((2, 4, 2, share, hidden), low),
             pltpu.VMEM((SLOTS, 4, share, hidden), low),
             pltpu.VMEM((SLOTS, share // 2, hidden), low),
@@ -1824,13 +1851,11 @@
         normed_attend,
         attended,
         residual,
-        scale,
-        gain,
         grad_shared,
         projected,
         hidden_in,
-        gain_attend,
-        dense_momentum,
+        scale,
+        gains,
     )
 
 
@@ -1838,13 +1863,9 @@
     expert_ref,
     dense_ref,
     routed_parts_ref,
-    base_ref,
-    dense_weights_ref,
     expert_out_ref,
-    block_out_ref,
-    dense_new_ref,
     dense_out_ref,
-    routed,
+    routed_received_ref,
     dense_back,
     moments,
     units,
@@ -1983,17 +2004,17 @@
             pl.when(exists(slot, peers[turn][0]))(out_copy(slot, turn).start)
         pl.when(exists(slot, dp))(own_copy(slot).start)
 
-    length = base_ref.shape[0]
+    length = routed_received_ref.shape[1]
     own_routed = pltpu.make_async_copy(
         routed_parts_ref.at[pl.ds(pl.multiple_of(z * length, length), length), :],
-        routed.at[3],
+        routed_received_ref.at[3],
         load_sems.at[6],
     )
     own_routed.start()
     routed_copies = [
         remote(
             routed_parts_ref.at[pl.ds(pl.multiple_of(device[1] * length, length), length), :],
-            routed.at[turn],
+            routed_received_ref.at[turn],
             line_sems.at[4, turn],
             line_sems.at[5, turn],
             device,
@@ -2055,19 +2076,6 @@
         copy.start()
     own_back.start()
     wait_back(0)
-    own_routed.wait()
-    for copy in routed_copies:
-        copy.wait()
-    rows_step = 32
-
-    @pl.loop(0, length // rows_step)
-    def _(index):
-        part = pl.ds(index * rows_step, rows_step)
-        total = base_ref[part, :]
-        for source in (3, 0, 1, 2):
-            total = total + routed[source, part, :].astype(jnp.float32)
-        block_out_ref[part, :] = total.astype(jnp.bfloat16)
-
     wait_back(2)
     for slot in range(3):
         for turn in range(7):
@@ -2081,33 +2089,26 @@
     for copy in line_back:
         copy.wait()
     own_back.wait()
-    keep_factor = 1.0 - LEARN_RATE * WEIGHT_DECAY
-    columns = current.shape[0]
-    for panel in range(dense_new_ref.shape[1] // columns):
-        spot = slice(panel * columns, (panel + 1) * columns)
-        dense_new_ref[:, spot] = keep_factor * dense_weights_ref[:, spot] - LEARN_RATE * (
-            dense_out_ref[panel].astype(jnp.float32)
-        )
-
-
-def muon(expert_units, dense_units, routed_parts, base_out, dense_weights):
+    own_routed.wait()
+    for copy in routed_copies:
+        copy.wait()
+
+
+def muon(expert_units, dense_units, routed_parts):
     experts, share, columns = expert_units.shape
     panels, stripe, _ = dense_units.shape
     count = experts + panels // 4
     low = jnp.bfloat16
-    vmem = pl.BlockSpec(memory_space=pltpu.VMEM)
     return pl.pallas_call(
         muon_kernel,
-        in_specs=[ANY] * 3 + [vmem] * 2,
-        out_specs=[ANY] + [vmem] * 2,
+        in_specs=[ANY] * 3,
+        out_specs=[ANY] * 3,
         out_shape=[
             jax.ShapeDtypeStruct(expert_units.shape, low),
-            jax.ShapeDtypeStruct(base_out.shape, low),
-            jax.ShapeDtypeStruct(dense_weights.shape, jnp.float32),
+            jax.ShapeDtypeStruct(dense_units.shape, low),
+            jax.ShapeDtypeStruct((4, routed_parts.shape[0] // 4, routed_parts.shape[1]), low),
         ],
         scratch_shapes=[
-            pltpu.VMEM(dense_units.shape, low),
-            pltpu.VMEM((4, *base_out.shape), low),
             pltpu.VMEM((panels // 4, share, columns), low),
             pltpu.VMEM((count, share, columns), low),
             pltpu.VMEM((3, 8 * share, columns), low),
@@ -2126,54 +2127,159 @@
             collective_id=4, has_side_effects=True, vmem_limit_bytes=56 * MIB
         ),
         name="muon",
-    )(expert_units, dense_units, routed_parts, base_out, dense_weights)
-
-
-def moments_kernel(momentum_ref, sum_ref, grad_ref, moment_ref, units_ref):
+    )(expert_units, dense_units, routed_parts)
+
+
+GROUP = 2
+
+
+def blocks_over(steps, shape, axis):
+    def place(index):
+        return tuple(
+            jnp.minimum(index, steps - 1) if position == axis else 0
+            for position in range(len(shape))
+        )
+
+    return pl.BlockSpec(shape, place)
+
+
+def moments_kernel(
+    momentum_ref,
+    sum_ref,
+    dense_momentum_ref,
+    dense_sum_ref,
+    grad_ref,
+    moment_ref,
+    units_ref,
+    dense_grad_ref,
+    dense_moment_ref,
+    dense_units_ref,
+):
     grad = sum_ref[...].astype(jnp.float32)
     moment = MOMENTUM_DECAY * momentum_ref[...] + grad
     grad_ref[...] = grad
     moment_ref[...] = moment
     units_ref[...] = moment.astype(jnp.bfloat16)
-
-
-def moments(momentum, grad_sum):
+    columns = dense_sum_ref.shape[2]
+    real = pl.program_id(0) < pl.num_programs(0) - 2
+    for panel in range(GROUP):
+        spot = slice(panel * columns, (panel + 1) * columns)
+        dense_grad = dense_sum_ref[panel]
+        dense_moment = MOMENTUM_DECAY * dense_momentum_ref[:, spot] + dense_grad
+        dense_grad_ref[:, spot] = dense_grad
+        dense_moment_ref[:, spot] = dense_moment
+        dense_units_ref[panel] = jnp.where(real, dense_moment, 0.0).astype(jnp.bfloat16)
+
+
+def moments(momentum, grad_sum, dense_momentum, dense_sum):
     panels, rows, columns = grad_sum.shape
-    group = 3
-    block = pl.BlockSpec((group, rows, columns), lambda index: (index, 0, 0))
+    dense_panels, stripe, _ = dense_sum.shape
+    steps = panels // GROUP
+    block = pl.BlockSpec((GROUP, rows, columns), lambda index: (index, 0, 0))
+    wide = blocks_over(dense_panels // GROUP, (stripe, GROUP * columns), 1)
     full = jax.ShapeDtypeStruct(grad_sum.shape, jnp.float32)
-    grad, moment, units = pl.pallas_call(
+    dense_full = jax.ShapeDtypeStruct(dense_momentum.shape, jnp.float32)
+    grad, moment, *rest = pl.pallas_call(
         moments_kernel,
-        grid=(panels // group,),
-        in_specs=[block] * 2,
-        out_specs=[block] * 3,
-        out_shape=[full, full, jax.ShapeDtypeStruct(grad_sum.shape, jnp.bfloat16)],
-        compiler_params=pltpu.CompilerParams(vmem_limit_bytes=32 * MIB),
+        grid=(steps,),
+        in_specs=[
+            block,
+            block,
+            wide,
+            blocks_over(dense_panels // GROUP, (GROUP, stripe, columns), 0),
+        ],
+        out_specs=[
+            block,
+            block,
+            block,
+            wide,
+            wide,
+            blocks_over(dense_panels // GROUP + 1, (GROUP, stripe, columns), 0),
+        ],
+        out_shape=[
+            full,
+            full,
+            jax.ShapeDtypeStruct(grad_sum.shape, jnp.bfloat16),
+            dense_full,
+            dense_full,
+            jax.ShapeDtypeStruct((dense_panels + GROUP, stripe, columns), jnp.bfloat16),
+        ],
+        compiler_params=pltpu.CompilerParams(vmem_limit_bytes=60 * MIB),
         name="moments",
-    )(momentum.reshape(grad_sum.shape), grad_sum)
-    return grad.reshape(momentum.shape), moment.reshape(momentum.shape), units
-
-
-def update_kernel(weights_ref, orthogonal_ref, new_ref):
+    )(momentum.reshape(grad_sum.shape), grad_sum, dense_momentum, dense_sum)
+    return grad.reshape(momentum.shape), moment.reshape(momentum.shape), *rest
+
+
+def update_kernel(
+    weights_ref,
+    orthogonal_ref,
+    dense_weights_ref,
+    dense_orthogonal_ref,
+    base_ref,
+    routed_ref,
+    grad_ref,
+    new_ref,
+    dense_new_ref,
+    out_ref,
+    grad_out_ref,
+):
     keep_factor = 1.0 - LEARN_RATE * WEIGHT_DECAY
     new_ref[...] = keep_factor * weights_ref[...] - LEARN_RATE * orthogonal_ref[...].astype(
         jnp.float32
     )
-
-
-def updated_weights(weights, orthogonal):
+    columns = dense_orthogonal_ref.shape[2]
+    for panel in range(GROUP):
+        spot = slice(panel * columns, (panel + 1) * columns)
+        dense_new_ref[:, spot] = keep_factor * dense_weights_ref[:, spot] - LEARN_RATE * (
+            dense_orthogonal_ref[panel].astype(jnp.float32)
+        )
+    total = base_ref[...]
+    for source in (3, 0, 1, 2):
+        total = total + routed_ref[source].astype(jnp.float32)
+    out_ref[...] = total.astype(jnp.bfloat16)
+    grad_out_ref[...] = grad_ref[...]
+
+
+def updated(weights, orthogonal, dense_weights, dense_orthogonal, base, routed, grad):
     panels, rows, columns = orthogonal.shape
-    group = 6
-    block = pl.BlockSpec((group, rows, columns), lambda index: (index, 0, 0))
-    return pl.pallas_call(
+    stripe, dense_columns = dense_weights.shape
+    length, width = base.shape
+    dense_steps = dense_columns // (GROUP * columns)
+    row_steps = 8
+    block = pl.BlockSpec((GROUP, rows, columns), lambda index: (index, 0, 0))
+    wide = blocks_over(dense_steps, (stripe, GROUP * columns), 1)
+    part = blocks_over(row_steps, (length // row_steps, width), 0)
+    new, *rest = pl.pallas_call(
         update_kernel,
-        grid=(panels // group,),
-        in_specs=[block, block],
-        out_specs=block,
-        out_shape=jax.ShapeDtypeStruct(orthogonal.shape, jnp.float32),
+        grid=(panels // GROUP,),
+        in_specs=[
+            block,
+            block,
+            wide,
+            blocks_over(dense_steps, (GROUP, stripe, columns), 0),
+            part,
+            blocks_over(row_steps, (4, length // row_steps, width), 1),
+            part,
+        ],
+        out_specs=[block, wide, part, part],
+        out_shape=[
+            jax.ShapeDtypeStruct(orthogonal.shape, jnp.float32),
+            jax.ShapeDtypeStruct(dense_weights.shape, jnp.float32),
+            jax.ShapeDtypeStruct(base.shape, jnp.bfloat16),
+            jax.ShapeDtypeStruct(base.shape, jnp.float32),
+        ],
         compiler_params=pltpu.CompilerParams(vmem_limit_bytes=32 * MIB),
         name="update",
-    )(weights.reshape(orthogonal.shape), orthogonal).reshape(weights.shape)
+    )(
+        weights.reshape(orthogonal.shape),
+        orthogonal,
+        dense_weights,
+        dense_orthogonal,
+        base,
+        routed,
+        grad,
+    )
+    return new.reshape(weights.shape), *rest
 
 
 def on_device(
@@ -2228,14 +2334,11 @@
             projected,
             attended,
             residual,
-            scale_mixer,
-            normed_mixer,
-            shared_act,
-            grad_shared_pre,
             grad_shared,
             base_out,
+            shared_sum,
+            scale_mixer,
             gains_all,
-            shared_sum,
         ) = front(
             jnp.concatenate(
                 [
@@ -2252,7 +2355,6 @@
             cotangent,
             -(-capacity // 16) * 16,
         )
-        gain_attend, gain_mixer = gains_all[0], gains_all[1]
     else:
         gate_tables = lax.all_gather(gate_table, "expert", axis=0, tiled=False)
         cotangents = lax.all_gather(cotangent, "expert", axis=0, tiled=True)
@@ -2328,14 +2430,7 @@
             tokens, cotangents, place, my_gates, expert_all, capacity
         )
     if direct:
-        (
-            expert_sum,
-            dense_grad,
-            dense_moment,
-            dense_units,
-            grad_inputs,
-            grad_gains,
-        ) = scatter_grads(
+        expert_sum, dense_sum, grad_inputs, grad_gains = scatter_grads(
             grad_parts,
             saved,
             dense_all,
@@ -2344,17 +2439,24 @@
             normed_attend,
             attended,
             residual,
-            scale_mixer,
-            gain_mixer[None, :],
             grad_shared,
             projected,
             hidden_in,
-            gain_attend[None, :],
-            dense_momentum,
-        )
-        expert_grad, expert_moment, expert_units = moments(expert_momentum, expert_sum)
-        orth_expert, block_out, dense_new = muon(
-            expert_units, dense_units, routed_parts, base_out, dense_weights
+            scale_mixer,
+            gains_all,
+        )
+        expert_grad, expert_moment, expert_units, dense_grad, dense_moment, dense_units = moments(
+            expert_momentum, expert_sum, dense_momentum, dense_sum
+        )
+        orth_expert, orth_dense, routed = muon(expert_units, dense_units, routed_parts)
+        expert_new, dense_new, block_out, grad_inputs = updated(
+            expert_weights,
+            orth_expert,
+            dense_weights,
+            orth_dense,
+            base_out,
+            routed,
+            grad_inputs,
         )
     else:
         routed = lax.psum_scatter(routed_parts, "expert", scatter_dimension=0, tiled=True)
@@ -2453,13 +2555,15 @@
         )
         keep_factor = 1.0 - LEARN_RATE * WEIGHT_DECAY
         dense_new = keep_factor * dense_weights - LEARN_RATE * orth_stripe
+        expert_new = keep_factor * expert_weights - LEARN_RATE * orth_expert.reshape(
+            expert_weights.shape
+        ).astype(jnp.float32)
     gain_grad = lax.psum_scatter(
         grad_gains,
         ("dp", "expert"),
         scatter_dimension=1,
         tiled=True,
     )
-    expert_new = updated_weights(expert_weights, orth_expert)
     first_new = FIRST_DECAY * gain_first + (1.0 - FIRST_DECAY) * gain_grad
     second_new = SECOND_DECAY * gain_second + (1.0 - SECOND_DECAY) * gain_grad * gain_grad
     step_ratio = (

time: 642 us -> 632 us (0.984)
  local copies, waits for them, and re-layouts: 23.7 us -> 12.6 us
    unnamed x39 -> x28, local copies, waits for them, and re-layouts: 20.4 us -> 10.8 us
  transfers between devices with their start and end apart: 1 -> 1, of which waited for: 1 -> 0; matrix products, arithmetic and copies ran while one was open for 0% -> 0% of each run, Pallas kernels for 19% -> 20%
where the time goes in v4:
time: 632 us; the launch traced here: 624 us
  Pallas kernels  595 us (94%)
  between operations  14.4 us (2%)
  local copies, waits for them, and re-layouts  12.6 us (2%)
    pallas_call x1, Pallas kernels, front(): pl.pallas_call(front_kernel, in_specs=[ANY] * 3 + [vmem] * 2, out_specs=[...  285 us
    pallas_call x1, Pallas kernels, scatter_grads(): pl.pallas_call(scatter_kernel, in_specs=[ANY] * 15 + [vmem] * 2, out_spec...  183 us
    pallas_call x1, Pallas kernels, muon(): pl.pallas_call(muon_kernel, in_specs=[ANY] * 3, out_specs=[ANY] * 3, out_...  106 us
    pallas_call x1, Pallas kernels, moments(): pl.pallas_call(moments_kernel, grid=(steps,), in_specs=[block, block, wid...  14.4 us
  transfers between devices with their start and end apart: 1, of which 0 were waited for; matrix products, arithmetic and copies ran while one was open for 0% of the time, Pallas kernels for 20%

profile of v4, /device:TPU:0, one launch (start us, length us, event | category | flops | bytes accessed | tf_op | source)
XLA Modules:
  0.0 624.2 jit_solution(8980974408187685159)
XLA Ops:
  7.2 0.0 reduce-scatter.4.cloned.1.call-start
  7.3 1.4 convert.12
  8.7 0.0 copy-done.10
  8.8 0.1 copy.26
  8.9 0.0 copy-done.7
  8.9 0.6 pad.4.gates_ref
  9.5 1.0 concatenate.4.stripe_ref
  10.5 285.4 %front.1 = (bf16[1536,7296]{1,0:T(8,128)(2,1)}, bf16[18,1536,512]{2,1,0:T(8,128)(2,1)}, bf16[1024,1536]{1,0:T(8,128)(2,1)}, bf16[1024,1536]{1,0:T(8,128)(2,1)}, ...) custom-call(bf16[48,7296]{1,0:T(8,128)(2,1)} %concatenate.4.stripe_r, ...), custom_call_target="tpu_custom_call" | custom-call | tf_op jit(solution)/shard_map/front/pallas_call | solution.py:1242
  296.0 182.9 %scatter_grads.1 = (bf16[18,192,512]{2,1,0:T(8,128)(2,1)}, f32[14,48,512]{2,1,0:T(8,128)}, f32[256,1536]{1,0:T(8,128)}, f32[2,1536]{1,0:T(2,128)}) custom-call(bf16[1024,1536]{1,0:T(8,128)(2,1)} %get-tuple-element.46.grad_parts_ref, bf16[6,320,1536]{2,1,0:T(8,128)(2,1)} %get-tuple-element.47.received_ref, ...), custom_call_target="tpu_custom_call" | custom-call | tf_op jit(solution)/shard_map/scatter_grads/pallas_call | solution.py:1800
  478.9 1.9 copy.27
  480.8 0.0 reduce-scatter.4.cloned.1.call-update
  480.8 14.4 %moments.1 = (f32[18,192,512]{2,1,0:T(8,128)}, f32[18,192,512]{2,1,0:T(8,128)}, bf16[18,192,512]{2,1,0:T(8,128)(2,1)}, f32[48,7168]{1,0:T(8,128)}, f32[48,7168]{1,0:T(8,128)}, /*index=5*/bf16[16,48,512]{2,1,0:T(8,128)(2,1)}) custom-call(f32[18,192,512]{2,1,0:T(8,128)} %bitcast.12, bf16[18,192,512]{2,1,0:T(8,128)(2,1)} %get-tuple-element.61.sum_ref, ...), custom_call_target="tpu_custom_call" | custom-call | tf_op jit(solution)/shard_map/moments/pallas_call | solution.py:2182
  495.2 0.0 copy-start.4
  495.2 0.0 copy-start.5
  495.2 106.3 %muon.1 = (bf16[18,192,512]{2,1,0:T(8,128)(2,1)}, bf16[16,48,512]{2,1,0:T(8,128)(2,1)}, bf16[4,256,1536]{2,1,0:T(8,128)(2,1)}) custom-call(bf16[18,192,512]{2,1,0:T(8,128)(2,1)} %get-tuple-element.63.expert_ref, bf16[16,48,512]{2,1,0:T(8,128)(2,1)} %get-tuple-element.64.dense_ref, bf16[1024,1536]{1,0:T(8,128)(2,1)} %get-tuple-element.65.routed_parts_ref), custom_call_target="tpu_custom_call" | custom-call | tf_op jit(solution)/shard_map/muon/pallas_call | solution.py:2102
  601.6 0.0 copy-start
  601.6 3.0 copy-done
  604.6 2.0 copy-done.2
  606.7 1.9 copy-done.3
  608.5 1.1 copy-done.6
  609.7 6.0 update.1
  615.7 0.8 copy.28
  616.5 0.6 multiply_subtract_fusion
  617.1 0.0 copy-done.9
  (23 shorter events, 0.1 us)
Async XLA Ops:
  7.2 1.6 copy-start.10
  7.2 1.7 copy-start.7
  7.2 1.7 copy-start.8
  7.2 608.5 %reduce-scatter.4.cloned.1.call-start = ((), (), s32[]{:S(2)}) async-start(), calls=%async_computation.1 | async-start | bytes 811008
  495.2 106.3 %copy-start.1 = (f32[48,7168]{1,0:T(8,128)S(1)}, f32[48,7168]{1,0:T(8,128)}, u32[]{:S(2)}) copy-start(f32[48,7168]{1,0:T(8,128)} %dense_weights_ref.1) | copy-start | bytes 4128772
  495.2 106.3 %copy-start.4 = (f32[256,1536]{1,0:T(8,128)S(1)}, f32[256,1536]{1,0:T(8,128)}, u32[]{:S(2)}) copy-start(f32[256,1536]{1,0:T(8,128)} %get-tuple-element.68.base_ref) | copy-start | bytes 4718596
  495.2 106.3 %copy-start.5 = (f32[256,1536]{1,0:T(8,128)S(1)}, f32[256,1536]{1,0:T(8,128)}, u32[]{:S(2)}) copy-start(f32[256,1536]{1,0:T(8,128)} %get-tuple-element.70.grad_ref) | copy-start | bytes 4718596
  601.6 3.0 copy-start
  604.6 2.0 copy-start.2
  606.6 1.9 copy-start.3
  608.5 1.1 copy-start.6
  609.7 6.9 %copy-start.11 = (f32[2,48]{1,0:T(2,128)S(1)}, f32[2,48]{1,0:T(2,128)}, u32[]{:S(2)}) copy-start(f32[2,48]{1,0:T(2,128)} %param.21) | copy-start | bytes 1156
  609.7 6.9 %copy-start.12 = (f32[2,48]{1,0:T(2,128)S(1)}, f32[2,48]{1,0:T(2,128)}, u32[]{:S(2)}) copy-start(f32[2,48]{1,0:T(2,128)} %param.20) | copy-start | bytes 1156
  616.5 0.6 copy-start.9
Sparse Core Ops, SparseCore 0:
  480.9 129.3 reduce-scatter.3

commit v5 on v4

--- a/solution.py
+++ b/solution.py
@@ -1162,12 +1162,19 @@
             ).astype(jnp.bfloat16)
 
         later = (
-            (lambda: exchange(12), lambda: shared_sides(0)),
-            (lambda: exchange(13), lambda: shared_sides(1)),
-            (lambda: exchange(14), lambda: shared_sides(2)),
-            (lambda: exchange(15), lambda: exchange(16), lambda: shard_last(14)),
+            (lambda: exchange(12),),
+            (lambda: exchange(13),),
+            (lambda: exchange(14),),
+            (
+                lambda: exchange(15),
+                lambda: exchange(16),
+                lambda: shard_last(14),
+                lambda: shared_sides(0),
+                lambda: shared_sides(1),
+            ),
             (
                 lambda: shard_forward(17),
+                lambda: shared_sides(2),
                 lambda: shared_sides(3),
                 lambda: shared_sides(4),
                 lambda: shared_sides(5),
@@ -2268,7 +2275,7 @@
             jax.ShapeDtypeStruct(base.shape, jnp.bfloat16),
             jax.ShapeDtypeStruct(base.shape, jnp.float32),
         ],
-        compiler_params=pltpu.CompilerParams(vmem_limit_bytes=32 * MIB),
+        compiler_params=pltpu.CompilerParams(vmem_limit_bytes=60 * MIB),
         name="update",
     )(
         weights.reshape(orthogonal.shape),
@@ -2558,11 +2565,12 @@
         expert_new = keep_factor * expert_weights - LEARN_RATE * orth_expert.reshape(
             expert_weights.shape
         ).astype(jnp.float32)
-    gain_grad = lax.psum_scatter(
-        grad_gains,
-        ("dp", "expert"),
-        scatter_dimension=1,
-        tiled=True,
+    gain_columns = norm_gains.shape[1]
+    gain_grad = lax.dynamic_slice_in_dim(
+        lax.psum(grad_gains, ("dp", "expert")),
+        lax.axis_index(("dp", "expert")) * gain_columns,
+        gain_columns,
+        1,
     )
     first_new = FIRST_DECAY * gain_first + (1.0 - FIRST_DECAY) * gain_grad
     second_new = SECOND_DECAY * gain_second + (1.0 - SECOND_DECAY) * gain_grad * gain_grad

time: 632 us -> 649 us (1.027)
  blocking collectives: 0 us -> 41.6 us
  between operations: 14.4 us -> 0.96 us
  local copies, waits for them, and re-layouts: 12.6 us -> 1.81 us
    psum x0 -> x1, blocking collectives: none -> 41.6 us  [on_device(): lax.psum(grad_gains, ('dp', 'expert'))]
    unnamed x28 -> x12, local copies, waits for them, and re-layouts: 10.8 us -> 0.03 us
    pallas_call x1, Pallas kernels: 6.03 us -> 13.2 us  [updated(): pl.pallas_call(update_kernel, grid=(panels // GROUP,), in_specs=[block, b...]
  transfers between devices with their start and end apart: 1 -> 0, of which waited for: 0 -> 0; matrix products, arithmetic and copies ran while one was open for 0% -> 0% of each run, Pallas kernels for 20% -> 0%
where the time goes in v5:
time: 649 us; the launch traced here: 643 us
  Pallas kernels  597 us (92%)
  blocking collectives  41.6 us (6%)
    pallas_call x1, Pallas kernels, front(): pl.pallas_call(front_kernel, in_specs=[ANY] * 3 + [vmem] * 2, out_specs=[...  281 us
    pallas_call x1, Pallas kernels, scatter_grads(): pl.pallas_call(scatter_kernel, in_specs=[ANY] * 15 + [vmem] * 2, out_spec...  184 us
    pallas_call x1, Pallas kernels, muon(): pl.pallas_call(muon_kernel, in_specs=[ANY] * 3, out_specs=[ANY] * 3, out_...  104 us
    psum x1, blocking collectives, on_device(): lax.psum(grad_gains, ('dp', 'expert'))  41.6 us
    pallas_call x1, Pallas kernels, moments(): pl.pallas_call(moments_kernel, grid=(steps,), in_specs=[block, block, wid...  14.2 us
    pallas_call x1, Pallas kernels, updated(): pl.pallas_call(update_kernel, grid=(panels // GROUP,), in_specs=[block, b...  13.2 us

profile of v5, /device:TPU:0, one launch (start us, length us, event | category | flops | bytes accessed | tf_op | source)
XLA Modules:
  0.0 643.3 jit_solution(14728938582729513006)
XLA Ops:
  0.6 0.0 copy-start.3
  0.7 0.0 copy-start.2
  0.7 0.0 copy-start.1
  0.7 1.4 convert.12
  2.2 0.0 copy-done.3
  2.2 0.1 copy.25
  2.3 1.0 concatenate.4.stripe_ref
  3.3 0.0 copy-done.2
  3.3 0.0 copy-done.1
  3.3 0.6 pad.4.gates_ref
  4.0 281.3 %front.1 = (bf16[1536,7296]{1,0:T(8,128)(2,1)}, bf16[18,1536,512]{2,1,0:T(8,128)(2,1)}, bf16[1024,1536]{1,0:T(8,128)(2,1)}, bf16[1024,1536]{1,0:T(8,128)(2,1)}, ...) custom-call(bf16[48,7296]{1,0:T(8,128)(2,1)} %concatenate.4.stripe_r, ...), custom_call_target="tpu_custom_call" | custom-call | tf_op jit(solution)/shard_map/front/pallas_call | solution.py:1249
  285.2 183.7 %scatter_grads.1 = (bf16[18,192,512]{2,1,0:T(8,128)(2,1)}, f32[14,48,512]{2,1,0:T(8,128)}, f32[256,1536]{1,0:T(8,128)}, f32[2,1536]{1,0:T(2,128)}) custom-call(bf16[1024,1536]{1,0:T(8,128)(2,1)} %get-tuple-element.46.grad_parts_ref, bf16[6,320,1536]{2,1,0:T(8,128)(2,1)} %get-tuple-element.47.received_ref, ...), custom_call_target="tpu_custom_call" | custom-call | tf_op jit(solution)/shard_map/scatter_grads/pallas_call | solution.py:1807
  468.9 14.2 %moments.1 = (f32[18,192,512]{2,1,0:T(8,128)}, f32[18,192,512]{2,1,0:T(8,128)}, bf16[18,192,512]{2,1,0:T(8,128)(2,1)}, f32[48,7168]{1,0:T(8,128)}, f32[48,7168]{1,0:T(8,128)}, /*index=5*/bf16[16,48,512]{2,1,0:T(8,128)(2,1)}) custom-call(f32[18,192,512]{2,1,0:T(8,128)} %bitcast.10, bf16[18,192,512]{2,1,0:T(8,128)(2,1)} %get-tuple-element.61.sum_ref, ...), custom_call_target="tpu_custom_call" | custom-call | tf_op jit(solution)/shard_map/moments/pallas_call | solution.py:2189
  483.1 104.4 %muon.1 = (bf16[18,192,512]{2,1,0:T(8,128)(2,1)}, bf16[16,48,512]{2,1,0:T(8,128)(2,1)}, bf16[4,256,1536]{2,1,0:T(8,128)(2,1)}) custom-call(bf16[18,192,512]{2,1,0:T(8,128)(2,1)} %get-tuple-element.63.expert_ref, bf16[16,48,512]{2,1,0:T(8,128)(2,1)} %get-tuple-element.64.dense_ref, bf16[1024,1536]{1,0:T(8,128)(2,1)} %get-tuple-element.65.routed_parts_ref), custom_call_target="tpu_custom_call" | custom-call | tf_op jit(solution)/shard_map/muon/pallas_call | solution.py:2109
  587.5 0.0 copy-start
  587.5 0.0 copy-start.4
  587.5 0.0 copy-start.5
  587.6 13.2 %update.1 = (f32[18,192,512]{2,1,0:T(8,128)}, f32[48,7168]{1,0:T(8,128)}, bf16[256,1536]{1,0:T(8,128)(2,1)}, f32[256,1536]{1,0:T(8,128)}) custom-call(f32[18,192,512]{2,1,0:T(8,128)} %bitcast.9, bf16[18,192,512]{2,1,0:T(8,128)(2,1)} %get-tuple-element.66.orthogonal_ref, f32[48,7168]{1,0:T(8,128)} %dense_weights_ref.1, ...), custom_call_target="tpu_custom_call" | custom-call | tf_op jit(solution)/shard_map/update/pallas_call | solution.py:2259
  600.8 0.0 copy-done
  600.8 41.6 %psum.7 = f32[2,1536]{1,0:T(2,128)S(1)} all-reduce(f32[2,1536]{1,0:T(2,128)S(1)} %copy-done), channel_id=1, replica_groups=mesh['dp'=8,'expert'=4] {'dp','expert'}, use_global_device_ids=true, to_apply=%region_1.2 | all-reduce | flops 3072 | bytes 24576 | tf_op jit(solution)/shard_map/psum | solution.py:2570
  642.4 0.0 copy-done.4
  642.4 0.0 copy-done.5
  642.4 0.7 multiply_subtract_fusion
  (6 shorter events, 0.1 us)
Async XLA Ops:
  0.6 1.5 copy-start.3
  0.7 2.6 copy-start.2
  0.7 2.6 copy-start.1
  587.5 13.3 %copy-start = (f32[2,1536]{1,0:T(2,128)S(1)}, f32[2,1536]{1,0:T(2,128)}, u32[]{:S(2)}) copy-start(f32[2,1536]{1,0:T(2,128)} %get-tuple-element.79) | copy-start | bytes 36868
  587.5 54.9 %copy-start.4 = (f32[2,48]{1,0:T(2,128)S(1)}, f32[2,48]{1,0:T(2,128)}, u32[]{:S(2)}) copy-start(f32[2,48]{1,0:T(2,128)} %param.21) | copy-start | bytes 1156
  587.5 54.9 %copy-start.5 = (f32[2,48]{1,0:T(2,128)S(1)}, f32[2,48]{1,0:T(2,128)}, u32[]{:S(2)}) copy-start(f32[2,48]{1,0:T(2,128)} %param.20) | copy-start | bytes 1156

commit v6 on v5

--- a/solution.py
+++ b/solution.py
@@ -2565,12 +2565,8 @@
         expert_new = keep_factor * expert_weights - LEARN_RATE * orth_expert.reshape(
             expert_weights.shape
         ).astype(jnp.float32)
-    gain_columns = norm_gains.shape[1]
-    gain_grad = lax.dynamic_slice_in_dim(
-        lax.psum(grad_gains, ("dp", "expert")),
-        lax.axis_index(("dp", "expert")) * gain_columns,
-        gain_columns,
-        1,
+    gain_grad = lax.psum_scatter(
+        grad_gains, ("dp", "expert"), scatter_dimension=1, tiled=True
     )
     first_new = FIRST_DECAY * gain_first + (1.0 - FIRST_DECAY) * gain_grad
     second_new = SECOND_DECAY * gain_second + (1.0 - SECOND_DECAY) * gain_grad * gain_grad

time: 649 us -> 629 us (0.969)
  blocking collectives: 41.6 us -> 0 us
  between operations: 0.96 us -> 14.4 us
    psum x1 -> x0, blocking collectives: 41.6 us -> none  [on_device(): lax.psum(grad_gains, ('dp', 'expert'))]
  transfers between devices with their start and end apart: 0 -> 1, of which waited for: 0 -> 0; matrix products, arithmetic and copies ran while one was open for 0% -> 0% of each run, Pallas kernels for 0% -> 22%
where the time goes in v6:
time: 629 us; the launch traced here: 620 us
  Pallas kernels  599 us (95%)
  between operations  14.4 us (2%)
    pallas_call x1, Pallas kernels, front(): pl.pallas_call(front_kernel, in_specs=[ANY] * 3 + [vmem] * 2, out_specs=[...  281 us
    pallas_call x1, Pallas kernels, scatter_grads(): pl.pallas_call(scatter_kernel, in_specs=[ANY] * 15 + [vmem] * 2, out_spec...  184 us
    pallas_call x1, Pallas kernels, muon(): pl.pallas_call(muon_kernel, in_specs=[ANY] * 3, out_specs=[ANY] * 3, out_...  106 us
    pallas_call x1, Pallas kernels, moments(): pl.pallas_call(moments_kernel, grid=(steps,), in_specs=[block, block, wid...  14.4 us
    pallas_call x1, Pallas kernels, updated(): pl.pallas_call(update_kernel, grid=(panels // GROUP,), in_specs=[block, b...  13.3 us
  transfers between devices with their start and end apart: 1, of which 0 were waited for; matrix products, arithmetic and copies ran while one was open for 0% of the time, Pallas kernels for 22%

profile of v6, /device:TPU:0, one launch (start us, length us, event | category | flops | bytes accessed | tf_op | source)
XLA Modules:
  0.0 619.9 jit_solution(10150291976537356301)
XLA Ops:
  7.2 0.0 copy-start.3
  7.2 0.0 copy-start
  7.2 0.0 copy-start.1
  7.2 0.0 reduce-scatter.4.cloned.1.call-start
  7.3 1.4 convert.12
  8.7 0.0 copy-done.3
  8.8 0.1 copy.26
  8.9 0.0 copy-done
  8.9 0.0 copy-done.1
  8.9 0.6 pad.4.gates_ref
  9.5 1.0 concatenate.4.stripe_ref
  10.5 281.3 %front.1 = (bf16[1536,7296]{1,0:T(8,128)(2,1)}, bf16[18,1536,512]{2,1,0:T(8,128)(2,1)}, bf16[1024,1536]{1,0:T(8,128)(2,1)}, bf16[1024,1536]{1,0:T(8,128)(2,1)}, ...) custom-call(bf16[48,7296]{1,0:T(8,128)(2,1)} %concatenate.4.stripe_r, ...), custom_call_target="tpu_custom_call" | custom-call | tf_op jit(solution)/shard_map/front/pallas_call | solution.py:1249
  291.8 183.7 %scatter_grads.1 = (bf16[18,192,512]{2,1,0:T(8,128)(2,1)}, f32[14,48,512]{2,1,0:T(8,128)}, f32[256,1536]{1,0:T(8,128)}, f32[2,1536]{1,0:T(2,128)}) custom-call(bf16[1024,1536]{1,0:T(8,128)(2,1)} %get-tuple-element.46.grad_parts_ref, bf16[6,320,1536]{2,1,0:T(8,128)(2,1)} %get-tuple-element.47.received_ref, ...), custom_call_target="tpu_custom_call" | custom-call | tf_op jit(solution)/shard_map/scatter_grads/pallas_call | solution.py:1807
  475.5 1.9 copy.27
  477.4 0.0 reduce-scatter.4.cloned.1.call-update
  477.4 14.4 %moments.1 = (f32[18,192,512]{2,1,0:T(8,128)}, f32[18,192,512]{2,1,0:T(8,128)}, bf16[18,192,512]{2,1,0:T(8,128)(2,1)}, f32[48,7168]{1,0:T(8,128)}, f32[48,7168]{1,0:T(8,128)}, /*index=5*/bf16[16,48,512]{2,1,0:T(8,128)(2,1)}) custom-call(f32[18,192,512]{2,1,0:T(8,128)} %bitcast.12, bf16[18,192,512]{2,1,0:T(8,128)(2,1)} %get-tuple-element.61.sum_ref, ...), custom_call_target="tpu_custom_call" | custom-call | tf_op jit(solution)/shard_map/moments/pallas_call | solution.py:2189
  491.8 106.3 %muon.1 = (bf16[18,192,512]{2,1,0:T(8,128)(2,1)}, bf16[16,48,512]{2,1,0:T(8,128)(2,1)}, bf16[4,256,1536]{2,1,0:T(8,128)(2,1)}) custom-call(bf16[18,192,512]{2,1,0:T(8,128)(2,1)} %get-tuple-element.63.expert_ref, bf16[16,48,512]{2,1,0:T(8,128)(2,1)} %get-tuple-element.64.dense_ref, bf16[1024,1536]{1,0:T(8,128)(2,1)} %get-tuple-element.65.routed_parts_ref), custom_call_target="tpu_custom_call" | custom-call | tf_op jit(solution)/shard_map/muon/pallas_call | solution.py:2109
  598.1 0.0 copy-start.4
  598.2 0.0 copy-start.5
  598.2 13.3 %update.1 = (f32[18,192,512]{2,1,0:T(8,128)}, f32[48,7168]{1,0:T(8,128)}, bf16[256,1536]{1,0:T(8,128)(2,1)}, f32[256,1536]{1,0:T(8,128)}) custom-call(f32[18,192,512]{2,1,0:T(8,128)} %bitcast.11, bf16[18,192,512]{2,1,0:T(8,128)(2,1)} %get-tuple-element.66.orthogonal_ref, f32[48,7168]{1,0:T(8,128)} %dense_weights_ref.1, ...), custom_call_target="tpu_custom_call" | custom-call | tf_op jit(solution)/shard_map/update/pallas_call | solution.py:2259
  611.4 0.0 reduce-scatter.4.cloned.1.call-done
  611.5 0.8 copy.28
  612.3 0.0 copy-done.5
  612.3 0.6 multiply_subtract_fusion
  (9 shorter events, 0.1 us)
Async XLA Ops:
  7.2 1.6 copy-start.3
  7.2 1.7 copy-start
  7.2 1.7 copy-start.1
  7.2 604.2 %reduce-scatter.4.cloned.1.call-start = ((), (), s32[]{:S(2)}) async-start(), calls=%async_computation.1 | async-start | bytes 811008
  598.1 14.1 %copy-start.4 = (f32[2,48]{1,0:T(2,128)S(1)}, f32[2,48]{1,0:T(2,128)}, u32[]{:S(2)}) copy-start(f32[2,48]{1,0:T(2,128)} %param.21) | copy-start | bytes 1156
  598.2 14.1 %copy-start.5 = (f32[2,48]{1,0:T(2,128)S(1)}, f32[2,48]{1,0:T(2,128)}, u32[]{:S(2)}) copy-start(f32[2,48]{1,0:T(2,128)} %param.20) | copy-start | bytes 1156
  612.3 0.6 copy-start.2
Sparse Core Ops, SparseCore 0:
  477.5 130.6 reduce-scatter.3

commit v7 on v6

--- a/solution.py
+++ b/solution.py
@@ -2137,7 +2137,7 @@
     )(expert_units, dense_units, routed_parts)
 
 
-GROUP = 2
+GROUP = 3
 
 
 def blocks_over(steps, shape, axis):
@@ -2151,6 +2151,7 @@
 
 
 def moments_kernel(
+    dense_panels,
     momentum_ref,
     sum_ref,
     dense_momentum_ref,
@@ -2168,13 +2169,13 @@
     moment_ref[...] = moment
     units_ref[...] = moment.astype(jnp.bfloat16)
     columns = dense_sum_ref.shape[2]
-    real = pl.program_id(0) < pl.num_programs(0) - 2
     for panel in range(GROUP):
         spot = slice(panel * columns, (panel + 1) * columns)
         dense_grad = dense_sum_ref[panel]
         dense_moment = MOMENTUM_DECAY * dense_momentum_ref[:, spot] + dense_grad
         dense_grad_ref[:, spot] = dense_grad
         dense_moment_ref[:, spot] = dense_moment
+        real = pl.program_id(0) * GROUP + panel < dense_panels
         dense_units_ref[panel] = jnp.where(real, dense_moment, 0.0).astype(jnp.bfloat16)
 
 
@@ -2182,18 +2183,19 @@
     panels, rows, columns = grad_sum.shape
     dense_panels, stripe, _ = dense_sum.shape
     steps = panels // GROUP
+    dense_steps = -(-dense_panels // GROUP)
     block = pl.BlockSpec((GROUP, rows, columns), lambda index: (index, 0, 0))
-    wide = blocks_over(dense_panels // GROUP, (stripe, GROUP * columns), 1)
+    wide = blocks_over(dense_steps, (stripe, GROUP * columns), 1)
     full = jax.ShapeDtypeStruct(grad_sum.shape, jnp.float32)
     dense_full = jax.ShapeDtypeStruct(dense_momentum.shape, jnp.float32)
     grad, moment, *rest = pl.pallas_call(
-        moments_kernel,
+        functools.partial(moments_kernel, dense_panels),
         grid=(steps,),
         in_specs=[
             block,
             block,
             wide,
-            blocks_over(dense_panels // GROUP, (GROUP, stripe, columns), 0),
+            blocks_over(dense_steps, (GROUP, stripe, columns), 0),
         ],
         out_specs=[
             block,
@@ -2201,7 +2203,7 @@
             block,
             wide,
             wide,
-            blocks_over(dense_panels // GROUP + 1, (GROUP, stripe, columns), 0),
+            blocks_over(dense_steps + 1, (GROUP, stripe, columns), 0),
         ],
         out_shape=[
             full,
@@ -2209,7 +2211,7 @@
             jax.ShapeDtypeStruct(grad_sum.shape, jnp.bfloat16),
             dense_full,
             dense_full,
-            jax.ShapeDtypeStruct((dense_panels + GROUP, stripe, columns), jnp.bfloat16),
+            jax.ShapeDtypeStruct((dense_panels + 2, stripe, columns), jnp.bfloat16),
         ],
         compiler_params=pltpu.CompilerParams(vmem_limit_bytes=60 * MIB),
         name="moments",
@@ -2251,8 +2253,8 @@
     panels, rows, columns = orthogonal.shape
     stripe, dense_columns = dense_weights.shape
     length, width = base.shape
-    dense_steps = dense_columns // (GROUP * columns)
-    row_steps = 8
+    dense_steps = -(-dense_columns // (GROUP * columns))
+    row_steps = 4
     block = pl.BlockSpec((GROUP, rows, columns), lambda index: (index, 0, 0))
     wide = blocks_over(dense_steps, (stripe, GROUP * columns), 1)
     part = blocks_over(row_steps, (length // row_steps, width), 0)

time: 629 us -> 625 us (level)
  transfers between devices with their start and end apart: 1 -> 1, of which waited for: 0 -> 0; matrix products, arithmetic and copies ran while one was open for 0% -> 0% of each run, Pallas kernels for 22% -> 21%
where the time goes in v7:
time: 625 us; the launch traced here: 616 us
  Pallas kernels  595 us (95%)
  between operations  14.4 us (2%)
    pallas_call x1, Pallas kernels, front(): pl.pallas_call(front_kernel, in_specs=[ANY] * 3 + [vmem] * 2, out_specs=[...  281 us
    pallas_call x1, Pallas kernels, scatter_grads(): pl.pallas_call(scatter_kernel, in_specs=[ANY] * 15 + [vmem] * 2, out_spec...  184 us
    pallas_call x1, Pallas kernels, muon(): pl.pallas_call(muon_kernel, in_specs=[ANY] * 3, out_specs=[ANY] * 3, out_...  106 us
    pallas_call x1, Pallas kernels, moments(): pl.pallas_call(functools.partial(moments_kernel, dense_panels), grid=(ste...  12.8 us
  transfers between devices with their start and end apart: 1, of which 0 were waited for; matrix products, arithmetic and copies ran while one was open for 0% of the time, Pallas kernels for 21%

profile of v7, /device:TPU:0, one launch (start us, length us, event | category | flops | bytes accessed | tf_op | source)
XLA Modules:
  0.0 616.1 jit_solution(8528493504270872618)
XLA Ops:
  7.2 0.0 copy-start.3
  7.2 0.0 copy-start
  7.2 0.0 copy-start.1
  7.2 0.0 reduce-scatter.4.cloned.1.call-start
  7.3 1.4 convert.12
  8.7 0.0 copy-done.3
  8.8 0.1 copy.26
  8.9 0.0 copy-done.1
  8.9 0.6 pad.4.gates_ref
  9.5 1.0 concatenate.4.stripe_ref
  10.5 281.3 %front.1 = (bf16[1536,7296]{1,0:T(8,128)(2,1)}, bf16[18,1536,512]{2,1,0:T(8,128)(2,1)}, bf16[1024,1536]{1,0:T(8,128)(2,1)}, bf16[1024,1536]{1,0:T(8,128)(2,1)}, ...) custom-call(bf16[48,7296]{1,0:T(8,128)(2,1)} %concatenate.4.stripe_r, ...), custom_call_target="tpu_custom_call" | custom-call | tf_op jit(solution)/shard_map/front/pallas_call | solution.py:1249
  291.8 183.7 %scatter_grads.1 = (bf16[18,192,512]{2,1,0:T(8,128)(2,1)}, f32[14,48,512]{2,1,0:T(8,128)}, f32[256,1536]{1,0:T(8,128)}, f32[2,1536]{1,0:T(2,128)}) custom-call(bf16[1024,1536]{1,0:T(8,128)(2,1)} %get-tuple-element.46.grad_parts_ref, bf16[6,320,1536]{2,1,0:T(8,128)(2,1)} %get-tuple-element.47.received_ref, ...), custom_call_target="tpu_custom_call" | custom-call | tf_op jit(solution)/shard_map/scatter_grads/pallas_call | solution.py:1807
  475.5 1.9 copy.27
  477.4 0.0 reduce-scatter.4.cloned.1.call-update
  477.4 12.8 %moments.1 = (f32[18,192,512]{2,1,0:T(8,128)}, f32[18,192,512]{2,1,0:T(8,128)}, bf16[18,192,512]{2,1,0:T(8,128)(2,1)}, f32[48,7168]{1,0:T(8,128)}, f32[48,7168]{1,0:T(8,128)}, /*index=5*/bf16[16,48,512]{2,1,0:T(8,128)(2,1)}) custom-call(f32[18,192,512]{2,1,0:T(8,128)} %bitcast.12, bf16[18,192,512]{2,1,0:T(8,128)(2,1)} %get-tuple-element.61.sum_ref, ...), custom_call_target="tpu_custom_call" | custom-call | tf_op jit(solution)/shard_map/moments/pallas_call | solution.py:2191
  490.2 106.3 %muon.1 = (bf16[18,192,512]{2,1,0:T(8,128)(2,1)}, bf16[16,48,512]{2,1,0:T(8,128)(2,1)}, bf16[4,256,1536]{2,1,0:T(8,128)(2,1)}) custom-call(bf16[18,192,512]{2,1,0:T(8,128)(2,1)} %get-tuple-element.63.expert_ref, bf16[16,48,512]{2,1,0:T(8,128)(2,1)} %get-tuple-element.64.dense_ref, bf16[1024,1536]{1,0:T(8,128)(2,1)} %get-tuple-element.65.routed_parts_ref), custom_call_target="tpu_custom_call" | custom-call | tf_op jit(solution)/shard_map/muon/pallas_call | solution.py:2109
  596.6 0.0 copy-start.4
  596.6 0.0 copy-start.5
  596.6 11.1 %update.1 = (f32[18,192,512]{2,1,0:T(8,128)}, f32[48,7168]{1,0:T(8,128)}, bf16[256,1536]{1,0:T(8,128)(2,1)}, f32[256,1536]{1,0:T(8,128)}) custom-call(f32[18,192,512]{2,1,0:T(8,128)} %bitcast.11, bf16[18,192,512]{2,1,0:T(8,128)(2,1)} %get-tuple-element.66.orthogonal_ref, f32[48,7168]{1,0:T(8,128)} %dense_weights_ref.1, ...), custom_call_target="tpu_custom_call" | custom-call | tf_op jit(solution)/shard_map/update/pallas_call | solution.py:2261
  607.6 0.0 reduce-scatter.4.cloned.1.call-done
  607.7 0.8 copy.28
  608.5 0.0 copy-done.4
  608.5 0.6 multiply_subtract_fusion
  609.1 0.0 copy-done.2
  (9 shorter events, 0.1 us)
Async XLA Ops:
  7.2 1.6 copy-start.3
  7.2 1.7 copy-start
  7.2 1.7 copy-start.1
  7.2 600.4 %reduce-scatter.4.cloned.1.call-start = ((), (), s32[]{:S(2)}) async-start(), calls=%async_computation.1 | async-start | bytes 811008
  596.6 11.9 %copy-start.4 = (f32[2,48]{1,0:T(2,128)S(1)}, f32[2,48]{1,0:T(2,128)}, u32[]{:S(2)}) copy-start(f32[2,48]{1,0:T(2,128)} %param.21) | copy-start | bytes 1156
  596.6 11.9 %copy-start.5 = (f32[2,48]{1,0:T(2,128)S(1)}, f32[2,48]{1,0:T(2,128)}, u32[]{:S(2)}) copy-start(f32[2,48]{1,0:T(2,128)} %param.20) | copy-start | bytes 1156
  608.5 0.6 copy-start.2
Sparse Core Ops, SparseCore 0:
  477.5 129.6 reduce-scatter.3
